TPU v7x, 256 devices: a whole 4x4x8 slice. The times are simulated.
256 devices in a mesh: dp: 32 (over z, y), tensor: 8 (over x, core).
Axes of the slice: x: 4, y: 4, z: 8, core: 2. Of those that a mesh axis runs over, the one named last changes fastest.
Arguments:
- hidden: bfloat16 [256, 5376], P('dp', 'tensor'), may hold values from -24 to 24
- tangent: bfloat16 [256, 5376], P('dp', 'tensor'), may hold values from -6 to 6
- out_weight: bfloat16 [262144, 5376], P(('dp', 'tensor')), may hold values from -2 to 2
Outputs:
- gn_product: float32 [256, 5376], P('dp', 'tensor')
All inputs are finite; a program needn't handle non-finite values.
Results may differ from a plain program's by a relative error of at most 0.0045.
Values may be sent and summed in bfloat16 or wider, within the bound.
No kernel may reach another device: no remote copies, remote signals or barrier semaphores. Data moves between devices by JAX's collectives and lax.ppermute only.
A program may use at most 64 MiB of HBM per device.

v0:
```python
import functools

import jax
import jax.numpy as jnp
from jax import lax
from jax.experimental import pallas as pl
from jax.experimental.pallas import tpu as pltpu
from jax.sharding import Mesh, PartitionSpec as P

AXES = ("z", "y", "x", "c")
BF = jnp.bfloat16
F32 = jnp.float32
VMEM = pl.BlockSpec(memory_space=pltpu.VMEM)
ANY = pl.BlockSpec(memory_space=pl.ANY)
MIB = 1024 * 1024
NZ, NQ = 8, 4


def perm(move):
    pairs = []
    for z in range(NZ):
        for y in range(NQ):
            for x in range(NQ):
                for c in range(2):
                    tz, ty, tx, tc = move(z, y, x, c)
                    src = ((z * NQ + y) * NQ + x) * 2 + c
                    dst = ((tz % NZ * NQ + ty % NQ) * NQ + tx % NQ) * 2 + tc
                    pairs.append((src, dst))
    return pairs


def send(value, move):
    return lax.ppermute(value, AXES, perm(move))


def along_yx(k):
    return lambda z, y, x, c: (z, y + k, x, c) if c == 0 else (z, y, x + k, c)


def along_xy(k):
    return lambda z, y, x, c: (z, y, x + k, c) if c == 0 else (z, y + k, x, c)


def other_core(z, y, x, c):
    return (z, y, x, 1 - c)


HOPS = (1, 3, 2)


def all_of(value, axes):
    return lax.all_to_all(value, axes, 0, 0)


def scores_kernel(*refs):
    pieces = refs[: 2 * NQ]
    w, scores, slopes, stats, held, whole, sems = refs[2 * NQ :]
    step = pl.program_id(0)
    rows = w.shape[0]
    tokens = scores.shape[1]
    width = held.shape[-1]

    @pl.when(step == 0)
    def _():
        y, x, c = lax.axis_index("y"), lax.axis_index("x"), lax.axis_index("c")
        copies = []
        for own in range(2):
            parity = c if own == 0 else 1 - c
            for k in range(NQ):
                for r in range(NQ):
                    x_back = jnp.where(parity == 0, k, r)
                    y_back = jnp.where(parity == 0, r, k)
                    x_at = lax.rem(x + NQ - x_back, NQ)
                    y_at = lax.rem(y + NQ - y_back, NQ)
                    copy = pltpu.make_async_copy(
                        pieces[own * NQ + k].at[r],
                        held.at[2 * x_at + parity, :, y_at],
                        sems.at[own, k, r],
                    )
                    copy.start()
                    copies.append(copy)
        for copy in copies:
            copy.wait()
        for t in range(2 * NQ):
            whole[:, t * width : (t + 1) * width] = held[t].reshape(2 * tokens, width)

    at = pl.ds(pl.multiple_of(step * rows, rows), rows)
    both = lax.dot_general(
        w[...], whole[...], (((1,), (1,)), ((), ())), preferred_element_type=F32
    )
    scores[at, :] = both[:, :tokens]
    slopes[at, :] = both[:, tokens:]

    @pl.when(step == pl.num_programs(0) - 1)
    def _():
        top = jnp.max(scores[...], axis=0, keepdims=True)
        raised = jnp.exp(scores[...] - top)
        scores[...] = raised
        own = jnp.concatenate(
            (
                top,
                jnp.sum(raised, axis=0, keepdims=True),
                jnp.sum(raised * slopes[...], axis=0, keepdims=True),
                jnp.zeros((5, tokens), F32),
            ),
            0,
        )
        stats[...] = jnp.broadcast_to(own[None], stats.shape)


def merged(parts):
    tops = parts[:, 0]
    top = jnp.max(tops, axis=0, keepdims=True)
    scale = jnp.exp(tops - top)
    total = jnp.sum(scale * parts[:, 1], axis=0, keepdims=True)
    dotted = jnp.sum(scale * parts[:, 2], axis=0, keepdims=True)
    return top, total, dotted


def merge_kernel(parts, out):
    rest = jnp.zeros((5, out.shape[-1]), F32)
    own = jnp.concatenate((*merged(parts[...]), rest), 0)
    out[...] = jnp.broadcast_to(own[None], out.shape)


def product_kernel(parts, mine, raised, slopes, w, keep, give, mixture):
    step = pl.program_id(0)
    tokens = mixture.shape[0]
    width = keep.shape[-1]
    part = tokens // NQ

    @pl.when(step == 0)
    def _():
        top, total, dotted = merged(parts[...])
        scale = jnp.exp(mine[0, 0:1, :] - top) / total
        mean = dotted / total
        mix = (raised[...] * scale) * (slopes[...] - mean)
        mixture[...] = mix.T.astype(BF)

    y, x, c = lax.axis_index("y"), lax.axis_index("x"), lax.axis_index("c")
    product = jnp.dot(mixture[...], w[...], preferred_element_type=F32)
    for half in range(2):
        x_of = 2 * step + half
        x_ahead = lax.rem(x_of + NQ - x, NQ)
        for parity in range(2):
            at = (2 * half + parity) * width
            piece = product[:, at : at + width]
            for y_of in range(NQ):
                rows = piece[y_of * part : (y_of + 1) * part]
                y_ahead = lax.rem(y_of + NQ - y, NQ)
                k, r = (x_ahead, y_ahead) if parity == 0 else (y_ahead, x_ahead)

                @pl.when(c == parity)
                def _():
                    keep[k, r] = rows

                @pl.when(c != parity)
                def _():
                    give[k, r] = rows.astype(BF)


def per_device(hidden, tangent, out_weight):
    rows, width = hidden.shape
    vocab, features = out_weight.shape
    tokens = rows * NZ * NQ
    shape = jax.ShapeDtypeStruct

    with jax.named_scope("gather_z"):
        own = jnp.stack((hidden, tangent))
        block = all_of(jnp.broadcast_to(own[None], (NZ, *own.shape)), "z")
        block = block.transpose(1, 0, 2, 3).reshape(2, rows * NZ, width)
    with jax.named_scope("gather_yx"):
        pieces = {0: block}
        for k in HOPS:
            pieces[k] = send(block, along_yx(k))
        block = jnp.stack([pieces[k] for k in range(NQ)])
    with jax.named_scope("gather_xy"):
        pieces = {0: block}
        for k in HOPS:
            pieces[k] = send(block, along_xy(k))
        theirs = {k: send(pieces[k], other_core) for k in (0,) + HOPS}

    steps = 4
    with jax.named_scope("scores"):
        raised, slopes, mine = pl.pallas_call(
            scores_kernel,
            grid=(steps,),
            out_shape=(
                shape((vocab, tokens), F32),
                shape((vocab, tokens), F32),
                shape((2 * NQ, 8, tokens), F32),
            ),
            in_specs=[ANY] * (2 * NQ)
            + [pl.BlockSpec((vocab // steps, features), lambda i: (i, 0))],
            out_specs=(
                pl.BlockSpec((vocab, tokens), lambda i: (0, 0)),
                pl.BlockSpec((vocab, tokens), lambda i: (0, 0)),
                pl.BlockSpec((2 * NQ, 8, tokens), lambda i: (0, 0, 0)),
            ),
            scratch_shapes=[
                pltpu.VMEM((2 * NQ, 2, NQ, rows * NZ, width), BF),
                pltpu.VMEM((2 * tokens, features), BF),
                pltpu.SemaphoreType.DMA((2, NQ, NQ)),
            ],
            compiler_params=pltpu.CompilerParams(vmem_limit_bytes=32 * MIB),
        )(*(pieces[k] for k in range(NQ)), *(theirs[k] for k in range(NQ)), out_weight)

    with jax.named_scope("statistics"):
        stats = pl.pallas_call(
            merge_kernel,
            out_shape=shape((NZ * NQ, 8, tokens), F32),
            in_specs=[VMEM],
            out_specs=VMEM,
        )(all_of(mine, ("x", "c")))
        parts = all_of(stats, ("z", "y"))

    with jax.named_scope("product"):
        whole = lambda n: pl.BlockSpec(n, lambda i: (0,) * len(n))
        keep, give = pl.pallas_call(
            product_kernel,
            grid=(2,),
            out_shape=(
                shape((NQ, NQ, rows * NZ, width), F32),
                shape((NQ, NQ, rows * NZ, width), BF),
            ),
            in_specs=[whole((NZ * NQ, 8, tokens)), whole((1, 8, tokens))]
            + [whole((vocab, tokens))] * 2
            + [pl.BlockSpec((vocab, features // 2), lambda i: (0, i))],
            out_specs=(
                whole((NQ, NQ, rows * NZ, width)),
                whole((NQ, NQ, rows * NZ, width)),
            ),
            scratch_shapes=[pltpu.VMEM((tokens, vocab), BF)],
            compiler_params=pltpu.CompilerParams(vmem_limit_bytes=40 * MIB),
        )(parts, mine, raised, slopes, out_weight)

    with jax.named_scope("scatter_core"):
        got = send(give, other_core)
    with jax.named_scope("scatter_xy"):
        sums = [keep[k] + got[k].astype(F32) for k in range(NQ)]
        total = sums[0]
        for k in HOPS:
            total = total + send(sums[k].astype(BF), along_xy(k)).astype(F32)
    with jax.named_scope("scatter_yx"):
        total, rest = total[0], total
        for k in HOPS:
            total = total + send(rest[k].astype(BF), along_yx(k)).astype(F32)
    with jax.named_scope("scatter_z"):
        return jnp.sum(all_of(total.reshape(NZ, rows, width), "z"), axis=0)


def solution(mesh):
    fine = Mesh(mesh.devices.reshape(NZ, NQ, NQ, 2), AXES)
    tokens = P(("z", "y"), ("x", "c"))
    return jax.shard_map(
        per_device,
        mesh=fine,
        in_specs=(tokens, tokens, P(AXES, None)),
        out_specs=tokens,
        check_vma=False,
    )
```

profile of v0, /device:TPU:6, one launch (start us, length us, event | category | flops | bytes accessed | tf_op | source)
XLA Modules:
  0.0 152.0 jit_solution(6957971015001337248)
XLA Ops:
  0.0 0.7 pad_maximum_fusion.1
  0.8 18.7 %all_to_all.20 = bf16[8,2,8,672]{3,2,1,0:T(8,128)(2,1)S(1)} all-to-all(bf16[8,2,8,672]{3,2,1,0:T(8,128)(2,1)S(1)} %broadcast_in_dim.2), channel_id=1, replica_groups=mesh['z'=8,'y'=4,'x'=4,'c'=2] {'z'}, dimensions={0} | all-to-all | bytes 344064 | tf_op jit(solution)/shard_map/gather_z/all_to_all | solution.py:52
  19.5 3.1 %collective-permute-start.2 = (bf16[2,64,672]{2,1,0:T(8,128)(2,1)S(1)}, bf16[2,64,672]{2,1,0:T(8,128)(2,1)S(1)}, u32[]{:S(2)}, u32[]{:S(2)}) collective-permute-start(bf16[2,64,672]{2,1,0:T(8,128)(2,1)S(1)} %get-tuple-element.24), channel_id=1, source_target_pairs={{0,24},{1,7},{2,26},{3,1},{4,28},{5,3},{6,30},{7,5},{8,0},{9,15},{... | collective-permute-start | bytes 516104 | tf_op jit(solution)/shard_map/gather_yx/ppermute | solution.py:33
  22.6 0.6 collective-permute-start.1
  23.2 1.0 collective-permute-start
  24.2 3.7 %collective-permute-done.2 = bf16[2,64,672]{2,1,0:T(8,128)(2,1)S(1)} collective-permute-done((bf16[2,64,672]{2,1,0:T(8,128)(2,1)S(1)}, bf16[2,64,672]{2,1,0:T(8,128)(2,1)S(1)}, u32[]{:S(2)}, u32[]{:S(2)}) %collective-permute-start.2) | collective-permute-done | bytes 172064 | tf_op jit(solution)/shard_map/gather_yx/ppermute | solution.py:33
  27.9 1.9 %collective-permute-done.1 = bf16[2,64,672]{2,1,0:T(8,128)(2,1)S(1)} collective-permute-done((bf16[2,64,672]{2,1,0:T(8,128)(2,1)S(1)}, bf16[2,64,672]{2,1,0:T(8,128)(2,1)S(1)}, u32[]{:S(2)}, u32[]{:S(2)}) %collective-permute-start.1) | collective-permute-done | bytes 172064 | tf_op jit(solution)/shard_map/gather_yx/ppermute | solution.py:33
  29.9 2.0 %collective-permute-done = bf16[2,64,672]{2,1,0:T(8,128)(2,1)S(1)} collective-permute-done((bf16[2,64,672]{2,1,0:T(8,128)(2,1)S(1)}, bf16[2,64,672]{2,1,0:T(8,128)(2,1)S(1)}, u32[]{:S(2)}, u32[]{:S(2)}) %collective-permute-start) | collective-permute-done | bytes 172064 | tf_op jit(solution)/shard_map/gather_yx/ppermute | solution.py:33
  31.9 0.1 pad_maximum_fusion.refs_0_
  32.0 0.9 collective-permute-start.5
  32.9 1.1 collective-permute-start.4
  34.0 2.1 %collective-permute-start.3 = (bf16[4,2,64,672]{3,2,1,0:T(8,128)(2,1)S(1)}, bf16[4,2,64,672]{3,2,1,0:T(8,128)(2,1)S(1)}, u32[]{:S(2)}, u32[]{:S(2)}) collective-permute-start(bf16[4,2,64,672]{3,2,1,0:T(8,128)(2,1)S(1)} %pad_maximum_fusion.refs_0_), channel_id=1, source_target_pairs={{0,2},{1,9},{2,4},{3,11},{4,6},{5,13},{6,0},{7,15},{8,10},{9,17},{... | collective-permute-start | bytes 2064392 | tf_op jit(solution)/shard_map/gather_xy/ppermute | solution.py:33
  36.1 0.0 collective-permute-start.6
  36.1 17.6 %collective-permute-done.5.refs_3_ = bf16[4,2,64,672]{3,2,1,0:T(8,128)(2,1)S(1)} collective-permute-done((bf16[4,2,64,672]{3,2,1,0:T(8,128)(2,1)S(1)}, bf16[4,2,64,672]{3,2,1,0:T(8,128)(2,1)S(1)}, u32[]{:S(2)}, u32[]{:S(2)}) %collective-permute-start.5) | collective-permute-done | bytes 688160 | tf_op jit(solution)/shard_map/gather_xy/ppermute | solution.py:33
  53.7 0.0 collective-permute-start.9
  53.7 0.0 collective-permute-done.4.refs_2_
  53.7 0.5 collective-permute-start.8
  54.2 0.4 collective-permute-done.3.refs_1_
  54.6 0.0 collective-permute-start.7
  54.6 0.0 collective-permute-done.6.refs_4_
  54.6 1.4 collective-permute-done.9.refs_7_
  56.0 1.1 collective-permute-done.8.refs_6_
  57.1 1.1 collective-permute-done.7.refs_5_
  58.2 0.0 copy-start
  58.2 4.1 %copy-done = bf16[1024,5376]{1,0:T(8,128)(2,1)S(1)} copy-done((bf16[1024,5376]{1,0:T(8,128)(2,1)S(1)}, bf16[1024,5376]{1,0:T(8,128)(2,1)}, u32[]{:S(2)}) %copy-start) | copy-done | bytes 11010072
  62.4 13.6 %scores.1 = (f32[1024,256]{1,0:T(8,128)S(1)}, f32[1024,256]{1,0:T(8,128)S(1)}, f32[8,8,256]{2,1,0:T(8,128)S(1)}) custom-call(bf16[4,2,64,672]{3,2,1,0:T(8,128)(2,1)S(1)} %pad_maximum_fusion.refs_0_, bf16[4,2,64,672]{3,2,1,0:T(8,128)(2,1)S(1)} %collective-permute-done.3.refs_1_, bf16[4,2,64,672]{3,2,1,0:T(8,128)(2,1)S(1)} %collective-permute-done.4.refs_2_, ...), custom_call_target="tpu_custom_call" | custom-call | tf_op jit(solution)/shard_map/scores/pallas_call | solution.py:185
  76.0 8.0 %all_to_all.21.parts = f32[8,8,256]{2,1,0:T(8,128)} all-to-all(f32[8,8,256]{2,1,0:T(8,128)S(1)} %get-tuple-element.10.mine), channel_id=1, replica_groups=mesh['z'=8,'y'=4,'x'=4,'c'=2] {'x','c'}, dimensions={0} | all-to-all | bytes 131072 | tf_op jit(solution)/shard_map/statistics/all_to_all | solution.py:52
  83.9 1.6 %statistics.1 = f32[32,8,256]{2,1,0:T(8,128)} custom-call(f32[8,8,256]{2,1,0:T(8,128)} %all_to_all.21.parts), custom_call_target="tpu_custom_call" | custom-call | tf_op jit(solution)/shard_map/statistics/pallas_call | solution.py:209
  85.5 17.2 %all_to_all.22.parts = f32[32,8,256]{2,1,0:T(8,128)S(1)} all-to-all(f32[32,8,256]{2,1,0:T(8,128)} %statistics.1), channel_id=1, replica_groups=mesh['z'=8,'y'=4,'x'=4,'c'=2] {'z','y'}, dimensions={0} | all-to-all | bytes 524288 | tf_op jit(solution)/shard_map/statistics/all_to_all | solution.py:52
  102.7 8.8 %product.1 = (f32[4,4,64,672]{3,2,1,0:T(8,128)S(1)}, bf16[4,4,64,672]{3,2,1,0:T(8,128)(2,1)S(1)}) custom-call(f32[32,8,256]{2,1,0:T(8,128)S(1)} %all_to_all.22.parts, f32[8,8,256]{2,1,0:T(8,128)S(1)} %get-tuple-element.10.mine, f32[1024,256]{1,0:T(8,128)S(1)} %get-tuple-element.11.raised, f32[1024,256]{1,0:T(8,128)S(1)} %get-tuple-element.12.slopes, ...), custom_call_target="tpu_custom_call" | custom-call | tf_op jit(solution)/shard_map/product/pallas_call | solution.py:219
  111.5 0.1 collective-permute-start.10
  111.6 3.4 %collective-permute-done.10 = bf16[4,4,64,672]{3,2,1,0:T(8,128)(2,1)S(1)} collective-permute-done((bf16[4,4,64,672]{3,2,1,0:T(8,128)(2,1)S(1)}, bf16[4,4,64,672]{3,2,1,0:T(8,128)(2,1)S(1)}, u32[]{:S(2)}, u32[]{:S(2)}) %collective-permute-start.10) | collective-permute-done | bytes 1376288 | tf_op jit(solution)/shard_map/scatter_core/ppermute | solution.py:33
  115.0 0.4 fusion.2
  115.4 2.1 %collective-permute-start.11 = (bf16[4,64,672]{2,1,0:T(8,128)(2,1)S(1)}, bf16[4,64,672]{2,1,0:T(8,128)(2,1)S(1)}, u32[]{:S(2)}, u32[]{:S(2)}) collective-permute-start(bf16[4,64,672]{2,1,0:T(8,128)(2,1)S(1)} %get-tuple-element.17), channel_id=1, source_target_pairs={{0,2},{1,9},{2,4},{3,11},{4,6},{5,13},{6,0},{7,15},{8,10},{9,17},{... | collective-permute-start | bytes 1032200 | tf_op jit(solution)/shard_map/scatter_xy/ppermute | solution.py:33
  117.5 0.4 collective-permute-start.13
  117.9 1.0 collective-permute-start.12
  119.0 8.1 %collective-permute-done.11 = bf16[4,64,672]{2,1,0:T(8,128)(2,1)S(1)} collective-permute-done((bf16[4,64,672]{2,1,0:T(8,128)(2,1)S(1)}, bf16[4,64,672]{2,1,0:T(8,128)(2,1)S(1)}, u32[]{:S(2)}, u32[]{:S(2)}) %collective-permute-start.11) | collective-permute-done | bytes 344096 | tf_op jit(solution)/shard_map/scatter_xy/ppermute | solution.py:33
  127.1 0.0 collective-permute-done.13
  127.1 3.9 %collective-permute-done.12 = bf16[4,64,672]{2,1,0:T(8,128)(2,1)S(1)} collective-permute-done((bf16[4,64,672]{2,1,0:T(8,128)(2,1)S(1)}, bf16[4,64,672]{2,1,0:T(8,128)(2,1)S(1)}, u32[]{:S(2)}, u32[]{:S(2)}) %collective-permute-start.12) | collective-permute-done | bytes 344096 | tf_op jit(solution)/shard_map/scatter_xy/ppermute | solution.py:33
  131.0 0.3 fusion.9
  131.3 0.1 collective-permute-start.14
  131.4 2.5 %collective-permute-start.16 = (bf16[64,672]{1,0:T(8,128)(2,1)S(1)}, bf16[64,672]{1,0:T(8,128)(2,1)S(1)}, u32[]{:S(2)}, u32[]{:S(2)}) collective-permute-start(bf16[64,672]{1,0:T(8,128)(2,1)S(1)} %get-tuple-element.21), channel_id=1, source_target_pairs={{0,16},{1,5},{2,18},{3,7},{4,20},{5,1},{6,22},{7,3},{8,24},{9,13},... | collective-permute-start | bytes 258056 | tf_op jit(solution)/shard_map/scatter_yx/ppermute | solution.py:33
  134.0 1.5 collective-permute-start.15
  135.4 2.9 %collective-permute-done.14 = bf16[64,672]{1,0:T(8,128)(2,1)S(1)} collective-permute-done((bf16[64,672]{1,0:T(8,128)(2,1)S(1)}, bf16[64,672]{1,0:T(8,128)(2,1)S(1)}, u32[]{:S(2)}, u32[]{:S(2)}) %collective-permute-start.14) | collective-permute-done | bytes 86048 | tf_op jit(solution)/shard_map/scatter_yx/ppermute | solution.py:33
  138.3 0.0 collective-permute-done.16
  138.3 0.9 collective-permute-done.15
  139.2 12.2 %all_to_all.23 = f32[8,8,672]{2,1,0:T(8,128)S(1)} all-to-all(f32[8,8,672]{2,1,0:T(8,128)S(1)} %fusion.8), channel_id=1, replica_groups=mesh['z'=8,'y'=4,'x'=4,'c'=2] {'z'}, dimensions={0} | all-to-all | bytes 344064 | tf_op jit(solution)/shard_map/scatter_z/all_to_all | solution.py:52
  151.4 0.6 reduce_sum.9
  (4 shorter events, 0.1 us)
Async XLA Ops:
  19.5 8.4 %collective-permute-start.2 = (bf16[2,64,672]{2,1,0:T(8,128)(2,1)S(1)}, bf16[2,64,672]{2,1,0:T(8,128)(2,1)S(1)}, u32[]{:S(2)}, u32[]{:S(2)}) collective-permute-start(bf16[2,64,672]{2,1,0:T(8,128)(2,1)S(1)} %get-tuple-element.24), channel_id=1, source_target_pairs={{0,24},{1,7},{2,26},{3,1},{4,28},{5,3},{6,30},{7,5},{8,0},{9,15},{... | collective-permute-start | bytes 516104 | tf_op jit(solution)/shard_map/gather_yx/ppermute | solution.py:33
  22.6 7.3 %collective-permute-start.1 = (bf16[2,64,672]{2,1,0:T(8,128)(2,1)S(1)}, bf16[2,64,672]{2,1,0:T(8,128)(2,1)S(1)}, u32[]{:S(2)}, u32[]{:S(2)}) collective-permute-start(bf16[2,64,672]{2,1,0:T(8,128)(2,1)S(1)} %get-tuple-element.24), channel_id=1, source_target_pairs={{0,16},{1,5},{2,18},{3,7},{4,20},{5,1},{6,22},{7,3},{8,24},{9,13},... | collective-permute-start | bytes 516104 | tf_op jit(solution)/shard_map/gather_yx/ppermute | solution.py:33
  23.2 8.7 %collective-permute-start = (bf16[2,64,672]{2,1,0:T(8,128)(2,1)S(1)}, bf16[2,64,672]{2,1,0:T(8,128)(2,1)S(1)}, u32[]{:S(2)}, u32[]{:S(2)}) collective-permute-start(bf16[2,64,672]{2,1,0:T(8,128)(2,1)S(1)} %get-tuple-element.24), channel_id=1, source_target_pairs={{0,8},{1,3},{2,10},{3,5},{4,12},{5,7},{6,14},{7,1},{8,16},{9,11},{... | collective-permute-start | bytes 516104 | tf_op jit(solution)/shard_map/gather_yx/ppermute | solution.py:33
  32.0 21.7 %collective-permute-start.5 = (bf16[4,2,64,672]{3,2,1,0:T(8,128)(2,1)S(1)}, bf16[4,2,64,672]{3,2,1,0:T(8,128)(2,1)S(1)}, u32[]{:S(2)}, u32[]{:S(2)}) collective-permute-start(bf16[4,2,64,672]{3,2,1,0:T(8,128)(2,1)S(1)} %pad_maximum_fusion.refs_0_), channel_id=1, source_target_pairs={{0,6},{1,25},{2,0},{3,27},{4,2},{5,29},{6,4},{7,31},{8,14},{9,1},{... | collective-permute-start | bytes 2064392 | tf_op jit(solution)/shard_map/gather_xy/ppermute | solution.py:33
  32.9 20.8 %collective-permute-start.4 = (bf16[4,2,64,672]{3,2,1,0:T(8,128)(2,1)S(1)}, bf16[4,2,64,672]{3,2,1,0:T(8,128)(2,1)S(1)}, u32[]{:S(2)}, u32[]{:S(2)}) collective-permute-start(bf16[4,2,64,672]{3,2,1,0:T(8,128)(2,1)S(1)} %pad_maximum_fusion.refs_0_), channel_id=1, source_target_pairs={{0,4},{1,17},{2,6},{3,19},{4,0},{5,21},{6,2},{7,23},{8,12},{9,25},... | collective-permute-start | bytes 2064392 | tf_op jit(solution)/shard_map/gather_xy/ppermute | solution.py:33
  34.0 20.6 %collective-permute-start.3 = (bf16[4,2,64,672]{3,2,1,0:T(8,128)(2,1)S(1)}, bf16[4,2,64,672]{3,2,1,0:T(8,128)(2,1)S(1)}, u32[]{:S(2)}, u32[]{:S(2)}) collective-permute-start(bf16[4,2,64,672]{3,2,1,0:T(8,128)(2,1)S(1)} %pad_maximum_fusion.refs_0_), channel_id=1, source_target_pairs={{0,2},{1,9},{2,4},{3,11},{4,6},{5,13},{6,0},{7,15},{8,10},{9,17},{... | collective-permute-start | bytes 2064392 | tf_op jit(solution)/shard_map/gather_xy/ppermute | solution.py:33
  36.1 18.5 %collective-permute-start.6 = (bf16[4,2,64,672]{3,2,1,0:T(8,128)(2,1)S(1)}, bf16[4,2,64,672]{3,2,1,0:T(8,128)(2,1)S(1)}, u32[]{:S(2)}, u32[]{:S(2)}) collective-permute-start(bf16[4,2,64,672]{3,2,1,0:T(8,128)(2,1)S(1)} %pad_maximum_fusion.refs_0_), channel_id=1, source_target_pairs={{0,1},{1,0},{2,3},{3,2},{4,5},{5,4},{6,7},{7,6},{8,9},{9,8},{10,11... | collective-permute-start | bytes 2064392 | tf_op jit(solution)/shard_map/gather_xy/ppermute | solution.py:33
  53.7 2.3 %collective-permute-start.9 = (bf16[4,2,64,672]{3,2,1,0:T(8,128)(2,1)S(1)}, bf16[4,2,64,672]{3,2,1,0:T(8,128)(2,1)S(1)}, u32[]{:S(2)}, u32[]{:S(2)}) collective-permute-start(bf16[4,2,64,672]{3,2,1,0:T(8,128)(2,1)S(1)} %collective-permute-done.5.refs_3_), channel_id=1, source_target_pairs={{0,1},{1,0},{2,3},{3,2},{4,5},{5,4},{6,7},{7,6},{8,9},{9,8},{10,11... | collective-permute-start | bytes 2064392 | tf_op jit(solution)/shard_map/gather_xy/ppermute | solution.py:33
  53.7 3.4 %collective-permute-start.8 = (bf16[4,2,64,672]{3,2,1,0:T(8,128)(2,1)S(1)}, bf16[4,2,64,672]{3,2,1,0:T(8,128)(2,1)S(1)}, u32[]{:S(2)}, u32[]{:S(2)}) collective-permute-start(bf16[4,2,64,672]{3,2,1,0:T(8,128)(2,1)S(1)} %collective-permute-done.4.refs_2_), channel_id=1, source_target_pairs={{0,1},{1,0},{2,3},{3,2},{4,5},{5,4},{6,7},{7,6},{8,9},{9,8},{10,11... | collective-permute-start | bytes 2064392 | tf_op jit(solution)/shard_map/gather_xy/ppermute | solution.py:33
  54.6 3.6 %collective-permute-start.7 = (bf16[4,2,64,672]{3,2,1,0:T(8,128)(2,1)S(1)}, bf16[4,2,64,672]{3,2,1,0:T(8,128)(2,1)S(1)}, u32[]{:S(2)}, u32[]{:S(2)}) collective-permute-start(bf16[4,2,64,672]{3,2,1,0:T(8,128)(2,1)S(1)} %collective-permute-done.3.refs_1_), channel_id=1, source_target_pairs={{0,1},{1,0},{2,3},{3,2},{4,5},{5,4},{6,7},{7,6},{8,9},{9,8},{10,11... | collective-permute-start | bytes 2064392 | tf_op jit(solution)/shard_map/gather_xy/ppermute | solution.py:33
  58.2 4.1 %copy-start = (bf16[1024,5376]{1,0:T(8,128)(2,1)S(1)}, bf16[1024,5376]{1,0:T(8,128)(2,1)}, u32[]{:S(2)}) copy-start(bf16[1024,5376]{1,0:T(8,128)(2,1)} %w.1) | copy-start | bytes 33030148
  111.5 3.5 %collective-permute-start.10 = (bf16[4,4,64,672]{3,2,1,0:T(8,128)(2,1)S(1)}, bf16[4,4,64,672]{3,2,1,0:T(8,128)(2,1)S(1)}, u32[]{:S(2)}, u32[]{:S(2)}) collective-permute-start(bf16[4,4,64,672]{3,2,1,0:T(8,128)(2,1)S(1)} %get-tuple-element.14), channel_id=1, source_target_pairs={{0,1},{1,0},{2,3},{3,2},{4,5},{5,4},{6,7},{7,6},{8,9},{9,8},{10,11... | collective-permute-start | bytes 4128776 | tf_op jit(solution)/shard_map/scatter_core/ppermute | solution.py:33
  115.4 11.7 %collective-permute-start.11 = (bf16[4,64,672]{2,1,0:T(8,128)(2,1)S(1)}, bf16[4,64,672]{2,1,0:T(8,128)(2,1)S(1)}, u32[]{:S(2)}, u32[]{:S(2)}) collective-permute-start(bf16[4,64,672]{2,1,0:T(8,128)(2,1)S(1)} %get-tuple-element.17), channel_id=1, source_target_pairs={{0,2},{1,9},{2,4},{3,11},{4,6},{5,13},{6,0},{7,15},{8,10},{9,17},{... | collective-permute-start | bytes 1032200 | tf_op jit(solution)/shard_map/scatter_xy/ppermute | solution.py:33
  117.5 9.5 %collective-permute-start.13 = (bf16[4,64,672]{2,1,0:T(8,128)(2,1)S(1)}, bf16[4,64,672]{2,1,0:T(8,128)(2,1)S(1)}, u32[]{:S(2)}, u32[]{:S(2)}) collective-permute-start(bf16[4,64,672]{2,1,0:T(8,128)(2,1)S(1)} %get-tuple-element.18), channel_id=1, source_target_pairs={{0,4},{1,17},{2,6},{3,19},{4,0},{5,21},{6,2},{7,23},{8,12},{9,25},... | collective-permute-start | bytes 1032200 | tf_op jit(solution)/shard_map/scatter_xy/ppermute | solution.py:33
  117.9 13.1 %collective-permute-start.12 = (bf16[4,64,672]{2,1,0:T(8,128)(2,1)S(1)}, bf16[4,64,672]{2,1,0:T(8,128)(2,1)S(1)}, u32[]{:S(2)}, u32[]{:S(2)}) collective-permute-start(bf16[4,64,672]{2,1,0:T(8,128)(2,1)S(1)} %get-tuple-element.19), channel_id=1, source_target_pairs={{0,6},{1,25},{2,0},{3,27},{4,2},{5,29},{6,4},{7,31},{8,14},{9,1},{... | collective-permute-start | bytes 1032200 | tf_op jit(solution)/shard_map/scatter_xy/ppermute | solution.py:33
  131.3 7.0 %collective-permute-start.14 = (bf16[64,672]{1,0:T(8,128)(2,1)S(1)}, bf16[64,672]{1,0:T(8,128)(2,1)S(1)}, u32[]{:S(2)}, u32[]{:S(2)}) collective-permute-start(bf16[64,672]{1,0:T(8,128)(2,1)S(1)} %get-tuple-element.20), channel_id=1, source_target_pairs={{0,8},{1,3},{2,10},{3,5},{4,12},{5,7},{6,14},{7,1},{8,16},{9,11},{... | collective-permute-start | bytes 258056 | tf_op jit(solution)/shard_map/scatter_yx/ppermute | solution.py:33
  131.4 6.9 %collective-permute-start.16 = (bf16[64,672]{1,0:T(8,128)(2,1)S(1)}, bf16[64,672]{1,0:T(8,128)(2,1)S(1)}, u32[]{:S(2)}, u32[]{:S(2)}) collective-permute-start(bf16[64,672]{1,0:T(8,128)(2,1)S(1)} %get-tuple-element.21), channel_id=1, source_target_pairs={{0,16},{1,5},{2,18},{3,7},{4,20},{5,1},{6,22},{7,3},{8,24},{9,13},... | collective-permute-start | bytes 258056 | tf_op jit(solution)/shard_map/scatter_yx/ppermute | solution.py:33
  134.0 5.2 %collective-permute-start.15 = (bf16[64,672]{1,0:T(8,128)(2,1)S(1)}, bf16[64,672]{1,0:T(8,128)(2,1)S(1)}, u32[]{:S(2)}, u32[]{:S(2)}) collective-permute-start(bf16[64,672]{1,0:T(8,128)(2,1)S(1)} %get-tuple-element.22), channel_id=1, source_target_pairs={{0,24},{1,7},{2,26},{3,1},{4,28},{5,3},{6,30},{7,5},{8,0},{9,15},{... | collective-permute-start | bytes 258056 | tf_op jit(solution)/shard_map/scatter_yx/ppermute | solution.py:33
where the time goes:
time: 152 us
  blocking collectives  56 us (37%)
  waiting for transfers between devices  48.5 us (32%)
  Pallas kernels  24 us (16%)
  starting transfers between devices  17.1 us (11%)
  local copies, waits for them, and re-layouts  4.19 us (3%)
  other arithmetic  2.17 us (1%)
    all_to_all x4, blocking collectives, all_of(): return lax.all_to_all(value, axes, 0, 0)  56 us
    ppermute x17, waiting for transfers between devices, send(): return lax.ppermute(value, AXES, perm(move))  48.5 us
    ppermute x17, starting transfers between devices, send(): return lax.ppermute(value, AXES, perm(move))  17.1 us
    pallas_call x1, Pallas kernels, per_device(): pl.pallas_call(scores_kernel, grid=(steps,), out_shape=(shape((vocab, tok...  13.6 us
    pallas_call x1, Pallas kernels, per_device(): pl.pallas_call(product_kernel, grid=(2,), out_shape=(shape((NQ, NQ, rows...  8.84 us
    unnamed x2, local copies, waits for them, and re-layouts  4.13 us
  transfers between devices with their start and end apart: 17, of which 13 were waited for; matrix products, arithmetic and copies ran while one was open for 0% of the time, Pallas kernels for 0%

commit v1 on v0

--- a/solution.py
+++ b/solution.py
@@ -52,18 +52,23 @@
     return lax.all_to_all(value, axes, 0, 0)
 
 
+def load_kernel(w, _, out, sem):
+    copy = pltpu.make_async_copy(w, out, sem)
+    copy.start()
+    copy.wait()
+
+
 def scores_kernel(*refs):
     pieces = refs[: 2 * NQ]
-    w, scores, slopes, stats, held, whole, sems = refs[2 * NQ :]
+    w, scores, slopes, stats, held, whole = refs[2 * NQ :]
     step = pl.program_id(0)
-    rows = w.shape[0]
+    rows = w.shape[0] // pl.num_programs(0)
     tokens = scores.shape[1]
     width = held.shape[-1]
 
     @pl.when(step == 0)
     def _():
         y, x, c = lax.axis_index("y"), lax.axis_index("x"), lax.axis_index("c")
-        copies = []
         for own in range(2):
             parity = c if own == 0 else 1 - c
             for k in range(NQ):
@@ -72,21 +77,14 @@
                     y_back = jnp.where(parity == 0, r, k)
                     x_at = lax.rem(x + NQ - x_back, NQ)
                     y_at = lax.rem(y + NQ - y_back, NQ)
-                    copy = pltpu.make_async_copy(
-                        pieces[own * NQ + k].at[r],
-                        held.at[2 * x_at + parity, :, y_at],
-                        sems.at[own, k, r],
-                    )
-                    copy.start()
-                    copies.append(copy)
-        for copy in copies:
-            copy.wait()
+                    for half in range(2):
+                        held[2 * x_at + parity, half, y_at] = pieces[own * NQ + k][r, half]
         for t in range(2 * NQ):
             whole[:, t * width : (t + 1) * width] = held[t].reshape(2 * tokens, width)
 
     at = pl.ds(pl.multiple_of(step * rows, rows), rows)
     both = lax.dot_general(
-        w[...], whole[...], (((1,), (1,)), ((), ())), preferred_element_type=F32
+        w[at, :], whole[...], (((1,), (1,)), ((), ())), preferred_element_type=F32
     )
     scores[at, :] = both[:, :tokens]
     slopes[at, :] = both[:, tokens:]
@@ -124,39 +122,38 @@
 
 
 def product_kernel(parts, mine, raised, slopes, w, keep, give, mixture):
-    step = pl.program_id(0)
     tokens = mixture.shape[0]
     width = keep.shape[-1]
     part = tokens // NQ
 
-    @pl.when(step == 0)
-    def _():
-        top, total, dotted = merged(parts[...])
-        scale = jnp.exp(mine[0, 0:1, :] - top) / total
-        mean = dotted / total
-        mix = (raised[...] * scale) * (slopes[...] - mean)
-        mixture[...] = mix.T.astype(BF)
+    top, total, dotted = merged(parts[...])
+    scale = jnp.exp(mine[0, 0:1, :] - top) / total
+    mean = dotted / total
+    mix = (raised[...] * scale) * (slopes[...] - mean)
+    mixture[...] = mix.T.astype(BF)
 
     y, x, c = lax.axis_index("y"), lax.axis_index("x"), lax.axis_index("c")
-    product = jnp.dot(mixture[...], w[...], preferred_element_type=F32)
-    for half in range(2):
-        x_of = 2 * step + half
-        x_ahead = lax.rem(x_of + NQ - x, NQ)
-        for parity in range(2):
-            at = (2 * half + parity) * width
-            piece = product[:, at : at + width]
-            for y_of in range(NQ):
-                rows = piece[y_of * part : (y_of + 1) * part]
-                y_ahead = lax.rem(y_of + NQ - y, NQ)
-                k, r = (x_ahead, y_ahead) if parity == 0 else (y_ahead, x_ahead)
-
-                @pl.when(c == parity)
-                def _():
-                    keep[k, r] = rows
-
-                @pl.when(c != parity)
-                def _():
-                    give[k, r] = rows.astype(BF)
+    for pair in range(2):
+        columns = slice(pair * 4 * width, (pair + 1) * 4 * width)
+        product = jnp.dot(mixture[...], w[:, columns], preferred_element_type=F32)
+        for half in range(2):
+            x_of = 2 * pair + half
+            x_ahead = lax.rem(x_of + NQ - x, NQ)
+            for parity in range(2):
+                at = (2 * half + parity) * width
+                piece = product[:, at : at + width]
+                for y_of in range(NQ):
+                    rows = piece[y_of * part : (y_of + 1) * part]
+                    y_ahead = lax.rem(y_of + NQ - y, NQ)
+                    k, r = (x_ahead, y_ahead) if parity == 0 else (y_ahead, x_ahead)
+
+                    @pl.when(c == parity)
+                    def _():
+                        keep[k, r] = rows
+
+                    @pl.when(c != parity)
+                    def _():
+                        give[k, r] = rows.astype(BF)
 
 
 def per_device(hidden, tangent, out_weight):
@@ -174,10 +171,22 @@
         for k in HOPS:
             pieces[k] = send(block, along_yx(k))
         block = jnp.stack([pieces[k] for k in range(NQ)])
+        weight = pl.pallas_call(
+            load_kernel,
+            out_shape=pltpu.VMEM((vocab, features), BF),
+            in_specs=[ANY, ANY],
+            out_specs=VMEM,
+            scratch_shapes=[pltpu.SemaphoreType.DMA],
+            cost_estimate=pl.CostEstimate(
+                flops=0, transcendentals=0, bytes_accessed=4 * vocab * features
+            ),
+            compiler_params=pltpu.CompilerParams(vmem_limit_bytes=MIB),
+        )(pltpu.with_memory_space_constraint(out_weight, pltpu.HBM), block)
     with jax.named_scope("gather_xy"):
         pieces = {0: block}
         for k in HOPS:
             pieces[k] = send(block, along_xy(k))
+        pieces[HOPS[0]], weight = lax.optimization_barrier((pieces[HOPS[0]], weight))
         theirs = {k: send(pieces[k], other_core) for k in (0,) + HOPS}
 
     steps = 4
@@ -190,8 +199,7 @@
                 shape((vocab, tokens), F32),
                 shape((2 * NQ, 8, tokens), F32),
             ),
-            in_specs=[ANY] * (2 * NQ)
-            + [pl.BlockSpec((vocab // steps, features), lambda i: (i, 0))],
+            in_specs=[VMEM] * (2 * NQ + 1),
             out_specs=(
                 pl.BlockSpec((vocab, tokens), lambda i: (0, 0)),
                 pl.BlockSpec((vocab, tokens), lambda i: (0, 0)),
@@ -200,10 +208,9 @@
             scratch_shapes=[
                 pltpu.VMEM((2 * NQ, 2, NQ, rows * NZ, width), BF),
                 pltpu.VMEM((2 * tokens, features), BF),
-                pltpu.SemaphoreType.DMA((2, NQ, NQ)),
             ],
             compiler_params=pltpu.CompilerParams(vmem_limit_bytes=32 * MIB),
-        )(*(pieces[k] for k in range(NQ)), *(theirs[k] for k in range(NQ)), out_weight)
+        )(*(pieces[k] for k in range(NQ)), *(theirs[k] for k in range(NQ)), weight)
 
     with jax.named_scope("statistics"):
         stats = pl.pallas_call(
@@ -211,28 +218,22 @@
             out_shape=shape((NZ * NQ, 8, tokens), F32),
             in_specs=[VMEM],
             out_specs=VMEM,
+            compiler_params=pltpu.CompilerParams(vmem_limit_bytes=4 * MIB),
         )(all_of(mine, ("x", "c")))
         parts = all_of(stats, ("z", "y"))
 
     with jax.named_scope("product"):
-        whole = lambda n: pl.BlockSpec(n, lambda i: (0,) * len(n))
         keep, give = pl.pallas_call(
             product_kernel,
-            grid=(2,),
             out_shape=(
                 shape((NQ, NQ, rows * NZ, width), F32),
                 shape((NQ, NQ, rows * NZ, width), BF),
             ),
-            in_specs=[whole((NZ * NQ, 8, tokens)), whole((1, 8, tokens))]
-            + [whole((vocab, tokens))] * 2
-            + [pl.BlockSpec((vocab, features // 2), lambda i: (0, i))],
-            out_specs=(
-                whole((NQ, NQ, rows * NZ, width)),
-                whole((NQ, NQ, rows * NZ, width)),
-            ),
+            in_specs=[VMEM] * 5,
+            out_specs=(VMEM, VMEM),
             scratch_shapes=[pltpu.VMEM((tokens, vocab), BF)],
-            compiler_params=pltpu.CompilerParams(vmem_limit_bytes=40 * MIB),
-        )(parts, mine, raised, slopes, out_weight)
+            compiler_params=pltpu.CompilerParams(vmem_limit_bytes=24 * MIB),
+        )(parts, mine, raised, slopes, weight)
 
     with jax.named_scope("scatter_core"):
         got = send(give, other_core)
@@ -246,7 +247,8 @@
         for k in HOPS:
             total = total + send(rest[k].astype(BF), along_yx(k)).astype(F32)
     with jax.named_scope("scatter_z"):
-        return jnp.sum(all_of(total.reshape(NZ, rows, width), "z"), axis=0)
+        total = total.astype(BF).reshape(NZ, rows, width)
+        return jnp.sum(all_of(total, "z").astype(F32), axis=0)
 
 
 def solution(mesh):

time: 152 us -> 138 us (0.908)
  Pallas kernels: 24 us -> 19 us
  local copies, waits for them, and re-layouts: 4.19 us -> 0.06 us
  waiting for transfers between devices: 48.5 us -> 45.5 us
  blocking collectives: 56 us -> 54 us
    pallas_call x1, Pallas kernels: 13.6 us -> 8.58 us  [per_device(): pl.pallas_call(scores_kernel, grid=(steps,), out_shape=(shape((vocab, tok...]
    unnamed x2 -> x0, local copies, waits for them, and re-layouts: 4.13 us -> none
    ppermute x17, waiting for transfers between devices: 48.5 us -> 45.5 us  [send(): return lax.ppermute(value, AXES, perm(move))]
    all_to_all x4, blocking collectives: 56 us -> 54 us  [all_of(): return lax.all_to_all(value, axes, 0, 0)]
    pallas_call x1 -> x2, Pallas kernels: 8.84 us -> 10.4 us  [the longest x1 6.25 us: per_device(): pl.pallas_call(product_kernel, out_shape=(shape((NQ, NQ, rows * NZ, width...]
    pallas_call x1, Pallas kernels: 1.58 us -> 0.04 us  [per_device(): pl.pallas_call(merge_kernel, out_shape=shape((NZ * NQ, 8, tokens), F32),...]
  transfers between devices with their start and end apart: 17 -> 17, of which waited for: 13 -> 13; matrix products, arithmetic and copies ran while one was open for 0% -> 0% of each run, Pallas kernels for 0% -> 3%
where the time goes in v1:
time: 138 us; the launch traced here: 137 us
  blocking collectives  54 us (39%)
  waiting for transfers between devices  45.5 us (33%)
  Pallas kernels  19 us (14%)
  starting transfers between devices  16.5 us (12%)
  other arithmetic  2.17 us (2%)
    all_to_all x4, blocking collectives, all_of(): return lax.all_to_all(value, axes, 0, 0)  54 us
    ppermute x17, waiting for transfers between devices, send(): return lax.ppermute(value, AXES, perm(move))  45.5 us
    ppermute x17, starting transfers between devices, send(): return lax.ppermute(value, AXES, perm(move))  16.5 us
    pallas_call x1, Pallas kernels, per_device(): pl.pallas_call(scores_kernel, grid=(steps,), out_shape=(shape((vocab, tok...  8.58 us
    pallas_call x1, Pallas kernels, per_device(): pl.pallas_call(product_kernel, out_shape=(shape((NQ, NQ, rows * NZ, width...  6.25 us
    pallas_call x1, Pallas kernels, per_device(): pl.pallas_call(load_kernel, out_shape=pltpu.VMEM((vocab, features), BF),...  4.14 us
  transfers between devices with their start and end apart: 17, of which 13 were waited for; matrix products, arithmetic and copies ran while one was open for 0% of the time, Pallas kernels for 3%

profile of v1, /device:TPU:6, one launch (start us, length us, event | category | flops | bytes accessed | tf_op | source)
XLA Modules:
  0.0 137.3 jit_solution(15721856355847324683)
XLA Ops:
  0.0 0.7 pad_maximum_fusion.1
  0.8 18.7 %all_to_all.20 = bf16[8,2,8,672]{3,2,1,0:T(8,128)(2,1)S(1)} all-to-all(bf16[8,2,8,672]{3,2,1,0:T(8,128)(2,1)S(1)} %broadcast_in_dim.2), channel_id=1, replica_groups=mesh['z'=8,'y'=4,'x'=4,'c'=2] {'z'}, dimensions={0} | all-to-all | bytes 344064 | tf_op jit(solution)/shard_map/gather_z/all_to_all | solution.py:52
  19.5 3.1 %collective-permute-start.2 = (bf16[2,64,672]{2,1,0:T(8,128)(2,1)S(1)}, bf16[2,64,672]{2,1,0:T(8,128)(2,1)S(1)}, u32[]{:S(2)}, u32[]{:S(2)}) collective-permute-start(bf16[2,64,672]{2,1,0:T(8,128)(2,1)S(1)} %get-tuple-element.28), channel_id=1, source_target_pairs={{0,24},{1,7},{2,26},{3,1},{4,28},{5,3},{6,30},{7,5},{8,0},{9,15},{... | collective-permute-start | bytes 516104 | tf_op jit(solution)/shard_map/gather_yx/ppermute | solution.py:33
  22.6 0.6 collective-permute-start.1
  23.2 1.0 collective-permute-start
  24.2 3.7 %collective-permute-done.2 = bf16[2,64,672]{2,1,0:T(8,128)(2,1)S(1)} collective-permute-done((bf16[2,64,672]{2,1,0:T(8,128)(2,1)S(1)}, bf16[2,64,672]{2,1,0:T(8,128)(2,1)S(1)}, u32[]{:S(2)}, u32[]{:S(2)}) %collective-permute-start.2) | collective-permute-done | bytes 172064 | tf_op jit(solution)/shard_map/gather_yx/ppermute | solution.py:33
  27.9 1.9 %collective-permute-done.1 = bf16[2,64,672]{2,1,0:T(8,128)(2,1)S(1)} collective-permute-done((bf16[2,64,672]{2,1,0:T(8,128)(2,1)S(1)}, bf16[2,64,672]{2,1,0:T(8,128)(2,1)S(1)}, u32[]{:S(2)}, u32[]{:S(2)}) %collective-permute-start.1) | collective-permute-done | bytes 172064 | tf_op jit(solution)/shard_map/gather_yx/ppermute | solution.py:33
  29.9 3.5 %collective-permute-done = bf16[2,64,672]{2,1,0:T(8,128)(2,1)S(1)} collective-permute-done((bf16[2,64,672]{2,1,0:T(8,128)(2,1)S(1)}, bf16[2,64,672]{2,1,0:T(8,128)(2,1)S(1)}, u32[]{:S(2)}, u32[]{:S(2)}) %collective-permute-start) | collective-permute-done | bytes 172064 | tf_op jit(solution)/shard_map/gather_yx/ppermute | solution.py:33
  33.4 0.1 pad_maximum_fusion._.refs_0_
  33.5 0.1 collective-permute-start.3
  33.6 2.0 %collective-permute-start.5 = (bf16[4,2,64,672]{3,2,1,0:T(8,128)(2,1)S(1)}, bf16[4,2,64,672]{3,2,1,0:T(8,128)(2,1)S(1)}, u32[]{:S(2)}, u32[]{:S(2)}) collective-permute-start(bf16[4,2,64,672]{3,2,1,0:T(8,128)(2,1)S(1)} %pad_maximum_fusion._.refs_0_), channel_id=1, source_target_pairs={{0,6},{1,25},{2,0},{3,27},{4,2},{5,29},{6,4},{7,31},{8,14},{9,1},{... | collective-permute-start | bytes 2064392 | tf_op jit(solution)/shard_map/gather_xy/ppermute | solution.py:33
  35.6 1.4 %collective-permute-start.4 = (bf16[4,2,64,672]{3,2,1,0:T(8,128)(2,1)S(1)}, bf16[4,2,64,672]{3,2,1,0:T(8,128)(2,1)S(1)}, u32[]{:S(2)}, u32[]{:S(2)}) collective-permute-start(bf16[4,2,64,672]{3,2,1,0:T(8,128)(2,1)S(1)} %pad_maximum_fusion._.refs_0_), channel_id=1, source_target_pairs={{0,4},{1,17},{2,6},{3,19},{4,0},{5,21},{6,2},{7,23},{8,12},{9,25},... | collective-permute-start | bytes 2064392 | tf_op jit(solution)/shard_map/gather_xy/ppermute | solution.py:33
  37.1 0.0 collective-permute-start.6
  37.1 4.1 %gather_yx.1.refs_8_.w = bf16[1024,5376]{1,0:T(8,128)(2,1)S(1)} custom-call(bf16[1024,5376]{1,0:T(8,128)(2,1)} %w.1, bf16[4,2,64,672]{3,2,1,0:T(8,128)(2,1)S(1)} %pad_maximum_fusion._.refs_0_), custom_call_target="tpu_custom_call" | custom-call | bytes 22020096 | tf_op jit(solution)/shard_map/gather_yx/pallas_call | solution.py:174
  41.2 4.4 %collective-permute-done.3.refs_1_ = bf16[4,2,64,672]{3,2,1,0:T(8,128)(2,1)S(1)} collective-permute-done((bf16[4,2,64,672]{3,2,1,0:T(8,128)(2,1)S(1)}, bf16[4,2,64,672]{3,2,1,0:T(8,128)(2,1)S(1)}, u32[]{:S(2)}, u32[]{:S(2)}) %collective-permute-start.3) | collective-permute-done | bytes 688160 | tf_op jit(solution)/shard_map/gather_xy/ppermute | solution.py:33
  45.6 1.3 collective-permute-done.5.refs_3_
  46.9 0.0 collective-permute-start.9
  46.9 8.6 %collective-permute-done.4.refs_2_ = bf16[4,2,64,672]{3,2,1,0:T(8,128)(2,1)S(1)} collective-permute-done((bf16[4,2,64,672]{3,2,1,0:T(8,128)(2,1)S(1)}, bf16[4,2,64,672]{3,2,1,0:T(8,128)(2,1)S(1)}, u32[]{:S(2)}, u32[]{:S(2)}) %collective-permute-start.4) | collective-permute-done | bytes 688160 | tf_op jit(solution)/shard_map/gather_xy/ppermute | solution.py:33
  55.5 0.0 collective-permute-start.8
  55.5 0.5 collective-permute-start.7
  56.0 0.0 collective-permute-done.6.refs_4_
  56.0 0.0 collective-permute-done.9.refs_7_
  56.0 1.8 %collective-permute-done.8.refs_6_ = bf16[4,2,64,672]{3,2,1,0:T(8,128)(2,1)S(1)} collective-permute-done((bf16[4,2,64,672]{3,2,1,0:T(8,128)(2,1)S(1)}, bf16[4,2,64,672]{3,2,1,0:T(8,128)(2,1)S(1)}, u32[]{:S(2)}, u32[]{:S(2)}) %collective-permute-start.8) | collective-permute-done | bytes 688160 | tf_op jit(solution)/shard_map/gather_xy/ppermute | solution.py:33
  57.8 1.1 collective-permute-done.7.refs_5_
  58.9 8.6 %scores.1 = (f32[1024,256]{1,0:T(8,128)S(1)}, f32[1024,256]{1,0:T(8,128)S(1)}, f32[8,8,256]{2,1,0:T(8,128)S(1)}) custom-call(bf16[4,2,64,672]{3,2,1,0:T(8,128)(2,1)S(1)} %pad_maximum_fusion._.refs_0_, bf16[4,2,64,672]{3,2,1,0:T(8,128)(2,1)S(1)} %collective-permute-done.3.refs_1_, bf16[4,2,64,672]{3,2,1,0:T(8,128)(2,1)S(1)} %collective-permute-done.4.refs_2_, ...), custom_call_target="tpu_custom_call" | custom-call | tf_op jit(solution)/shard_map/scores/pallas_call | solution.py:194
  67.5 7.9 %all_to_all.21.parts = f32[8,8,256]{2,1,0:T(8,128)S(1)} all-to-all(f32[8,8,256]{2,1,0:T(8,128)S(1)} %get-tuple-element.14.mine), channel_id=1, replica_groups=mesh['z'=8,'y'=4,'x'=4,'c'=2] {'x','c'}, dimensions={0} | all-to-all | bytes 131072 | tf_op jit(solution)/shard_map/statistics/all_to_all | solution.py:52
  75.4 16.3 %all_to_all.22.parts = f32[32,8,256]{2,1,0:T(8,128)S(1)} all-to-all(f32[32,8,256]{2,1,0:T(8,128)S(1)} %statistics.1), channel_id=1, replica_groups=mesh['z'=8,'y'=4,'x'=4,'c'=2] {'z','y'}, dimensions={0} | all-to-all | bytes 524288 | tf_op jit(solution)/shard_map/statistics/all_to_all | solution.py:52
  91.7 6.2 %product.1 = (f32[4,4,64,672]{3,2,1,0:T(8,128)S(1)}, bf16[4,4,64,672]{3,2,1,0:T(8,128)(2,1)S(1)}) custom-call(f32[32,8,256]{2,1,0:T(8,128)S(1)} %all_to_all.22.parts, f32[8,8,256]{2,1,0:T(8,128)S(1)} %get-tuple-element.14.mine, f32[1024,256]{1,0:T(8,128)S(1)} %get-tuple-element.15.raised, f32[1024,256]{1,0:T(8,128)S(1)} %get-tuple-element.16.slopes, ...), custom_call_target="tpu_custom_call" | custom-call | tf_op jit(solution)/shard_map/product/pallas_call | solution.py:226
  97.9 0.1 collective-permute-start.10
  98.0 3.4 %collective-permute-done.10 = bf16[4,4,64,672]{3,2,1,0:T(8,128)(2,1)S(1)} collective-permute-done((bf16[4,4,64,672]{3,2,1,0:T(8,128)(2,1)S(1)}, bf16[4,4,64,672]{3,2,1,0:T(8,128)(2,1)S(1)}, u32[]{:S(2)}, u32[]{:S(2)}) %collective-permute-start.10) | collective-permute-done | bytes 1376288 | tf_op jit(solution)/shard_map/scatter_core/ppermute | solution.py:33
  101.4 0.4 fusion.2
  101.8 2.1 %collective-permute-start.11 = (bf16[4,64,672]{2,1,0:T(8,128)(2,1)S(1)}, bf16[4,64,672]{2,1,0:T(8,128)(2,1)S(1)}, u32[]{:S(2)}, u32[]{:S(2)}) collective-permute-start(bf16[4,64,672]{2,1,0:T(8,128)(2,1)S(1)} %get-tuple-element.21), channel_id=1, source_target_pairs={{0,2},{1,9},{2,4},{3,11},{4,6},{5,13},{6,0},{7,15},{8,10},{9,17},{... | collective-permute-start | bytes 1032200 | tf_op jit(solution)/shard_map/scatter_xy/ppermute | solution.py:33
  103.9 0.4 collective-permute-start.13
  104.3 1.0 collective-permute-start.12
  105.4 8.1 %collective-permute-done.11 = bf16[4,64,672]{2,1,0:T(8,128)(2,1)S(1)} collective-permute-done((bf16[4,64,672]{2,1,0:T(8,128)(2,1)S(1)}, bf16[4,64,672]{2,1,0:T(8,128)(2,1)S(1)}, u32[]{:S(2)}, u32[]{:S(2)}) %collective-permute-start.11) | collective-permute-done | bytes 344096 | tf_op jit(solution)/shard_map/scatter_xy/ppermute | solution.py:33
  113.5 0.0 collective-permute-done.13
  113.5 3.9 %collective-permute-done.12 = bf16[4,64,672]{2,1,0:T(8,128)(2,1)S(1)} collective-permute-done((bf16[4,64,672]{2,1,0:T(8,128)(2,1)S(1)}, bf16[4,64,672]{2,1,0:T(8,128)(2,1)S(1)}, u32[]{:S(2)}, u32[]{:S(2)}) %collective-permute-start.12) | collective-permute-done | bytes 344096 | tf_op jit(solution)/shard_map/scatter_xy/ppermute | solution.py:33
  117.4 0.3 fusion.10
  117.7 0.1 collective-permute-start.14
  117.8 2.5 %collective-permute-start.16 = (bf16[64,672]{1,0:T(8,128)(2,1)S(1)}, bf16[64,672]{1,0:T(8,128)(2,1)S(1)}, u32[]{:S(2)}, u32[]{:S(2)}) collective-permute-start(bf16[64,672]{1,0:T(8,128)(2,1)S(1)} %get-tuple-element.25), channel_id=1, source_target_pairs={{0,16},{1,5},{2,18},{3,7},{4,20},{5,1},{6,22},{7,3},{8,24},{9,13},... | collective-permute-start | bytes 258056 | tf_op jit(solution)/shard_map/scatter_yx/ppermute | solution.py:33
  120.4 1.5 %collective-permute-start.15 = (bf16[64,672]{1,0:T(8,128)(2,1)S(1)}, bf16[64,672]{1,0:T(8,128)(2,1)S(1)}, u32[]{:S(2)}, u32[]{:S(2)}) collective-permute-start(bf16[64,672]{1,0:T(8,128)(2,1)S(1)} %get-tuple-element.26), channel_id=1, source_target_pairs={{0,24},{1,7},{2,26},{3,1},{4,28},{5,3},{6,30},{7,5},{8,0},{9,15},{... | collective-permute-start | bytes 258056 | tf_op jit(solution)/shard_map/scatter_yx/ppermute | solution.py:33
  121.8 2.9 %collective-permute-done.14 = bf16[64,672]{1,0:T(8,128)(2,1)S(1)} collective-permute-done((bf16[64,672]{1,0:T(8,128)(2,1)S(1)}, bf16[64,672]{1,0:T(8,128)(2,1)S(1)}, u32[]{:S(2)}, u32[]{:S(2)}) %collective-permute-start.14) | collective-permute-done | bytes 86048 | tf_op jit(solution)/shard_map/scatter_yx/ppermute | solution.py:33
  124.7 0.0 collective-permute-done.16
  124.7 0.9 collective-permute-done.15
  125.6 0.1 fusion.9
  125.6 11.1 %all_to_all.23 = bf16[8,8,672]{2,1,0:T(8,128)(2,1)S(1)} all-to-all(bf16[8,8,672]{2,1,0:T(8,128)(2,1)S(1)} %fusion.9), channel_id=1, replica_groups=mesh['z'=8,'y'=4,'x'=4,'c'=2] {'z'}, dimensions={0} | all-to-all | bytes 172032 | tf_op jit(solution)/shard_map/scatter_z/all_to_all | solution.py:52
  136.7 0.6 convert_reduce_fusion
  (4 shorter events, 0.1 us)
Async XLA Ops:
  19.5 8.4 %collective-permute-start.2 = (bf16[2,64,672]{2,1,0:T(8,128)(2,1)S(1)}, bf16[2,64,672]{2,1,0:T(8,128)(2,1)S(1)}, u32[]{:S(2)}, u32[]{:S(2)}) collective-permute-start(bf16[2,64,672]{2,1,0:T(8,128)(2,1)S(1)} %get-tuple-element.28), channel_id=1, source_target_pairs={{0,24},{1,7},{2,26},{3,1},{4,28},{5,3},{6,30},{7,5},{8,0},{9,15},{... | collective-permute-start | bytes 516104 | tf_op jit(solution)/shard_map/gather_yx/ppermute | solution.py:33
  22.6 7.3 %collective-permute-start.1 = (bf16[2,64,672]{2,1,0:T(8,128)(2,1)S(1)}, bf16[2,64,672]{2,1,0:T(8,128)(2,1)S(1)}, u32[]{:S(2)}, u32[]{:S(2)}) collective-permute-start(bf16[2,64,672]{2,1,0:T(8,128)(2,1)S(1)} %get-tuple-element.28), channel_id=1, source_target_pairs={{0,16},{1,5},{2,18},{3,7},{4,20},{5,1},{6,22},{7,3},{8,24},{9,13},... | collective-permute-start | bytes 516104 | tf_op jit(solution)/shard_map/gather_yx/ppermute | solution.py:33
  23.2 10.2 %collective-permute-start = (bf16[2,64,672]{2,1,0:T(8,128)(2,1)S(1)}, bf16[2,64,672]{2,1,0:T(8,128)(2,1)S(1)}, u32[]{:S(2)}, u32[]{:S(2)}) collective-permute-start(bf16[2,64,672]{2,1,0:T(8,128)(2,1)S(1)} %get-tuple-element.28), channel_id=1, source_target_pairs={{0,8},{1,3},{2,10},{3,5},{4,12},{5,7},{6,14},{7,1},{8,16},{9,11},{... | collective-permute-start | bytes 516104 | tf_op jit(solution)/shard_map/gather_yx/ppermute | solution.py:33
  33.5 12.1 %collective-permute-start.3 = (bf16[4,2,64,672]{3,2,1,0:T(8,128)(2,1)S(1)}, bf16[4,2,64,672]{3,2,1,0:T(8,128)(2,1)S(1)}, u32[]{:S(2)}, u32[]{:S(2)}) collective-permute-start(bf16[4,2,64,672]{3,2,1,0:T(8,128)(2,1)S(1)} %pad_maximum_fusion._.refs_0_), channel_id=1, source_target_pairs={{0,2},{1,9},{2,4},{3,11},{4,6},{5,13},{6,0},{7,15},{8,10},{9,17},{... | collective-permute-start | bytes 2064392 | tf_op jit(solution)/shard_map/gather_xy/ppermute | solution.py:33
  33.6 13.3 %collective-permute-start.5 = (bf16[4,2,64,672]{3,2,1,0:T(8,128)(2,1)S(1)}, bf16[4,2,64,672]{3,2,1,0:T(8,128)(2,1)S(1)}, u32[]{:S(2)}, u32[]{:S(2)}) collective-permute-start(bf16[4,2,64,672]{3,2,1,0:T(8,128)(2,1)S(1)} %pad_maximum_fusion._.refs_0_), channel_id=1, source_target_pairs={{0,6},{1,25},{2,0},{3,27},{4,2},{5,29},{6,4},{7,31},{8,14},{9,1},{... | collective-permute-start | bytes 2064392 | tf_op jit(solution)/shard_map/gather_xy/ppermute | solution.py:33
  35.6 19.8 %collective-permute-start.4 = (bf16[4,2,64,672]{3,2,1,0:T(8,128)(2,1)S(1)}, bf16[4,2,64,672]{3,2,1,0:T(8,128)(2,1)S(1)}, u32[]{:S(2)}, u32[]{:S(2)}) collective-permute-start(bf16[4,2,64,672]{3,2,1,0:T(8,128)(2,1)S(1)} %pad_maximum_fusion._.refs_0_), channel_id=1, source_target_pairs={{0,4},{1,17},{2,6},{3,19},{4,0},{5,21},{6,2},{7,23},{8,12},{9,25},... | collective-permute-start | bytes 2064392 | tf_op jit(solution)/shard_map/gather_xy/ppermute | solution.py:33
  37.1 18.9 %collective-permute-start.6 = (bf16[4,2,64,672]{3,2,1,0:T(8,128)(2,1)S(1)}, bf16[4,2,64,672]{3,2,1,0:T(8,128)(2,1)S(1)}, u32[]{:S(2)}, u32[]{:S(2)}) collective-permute-start(bf16[4,2,64,672]{3,2,1,0:T(8,128)(2,1)S(1)} %pad_maximum_fusion._.refs_0_), channel_id=1, source_target_pairs={{0,1},{1,0},{2,3},{3,2},{4,5},{5,4},{6,7},{7,6},{8,9},{9,8},{10,11... | collective-permute-start | bytes 2064392 | tf_op jit(solution)/shard_map/gather_xy/ppermute | solution.py:33
  46.9 9.1 %collective-permute-start.9 = (bf16[4,2,64,672]{3,2,1,0:T(8,128)(2,1)S(1)}, bf16[4,2,64,672]{3,2,1,0:T(8,128)(2,1)S(1)}, u32[]{:S(2)}, u32[]{:S(2)}) collective-permute-start(bf16[4,2,64,672]{3,2,1,0:T(8,128)(2,1)S(1)} %collective-permute-done.5.refs_3_), channel_id=1, source_target_pairs={{0,1},{1,0},{2,3},{3,2},{4,5},{5,4},{6,7},{7,6},{8,9},{9,8},{10,11... | collective-permute-start | bytes 2064392 | tf_op jit(solution)/shard_map/gather_xy/ppermute | solution.py:33
  55.5 2.3 %collective-permute-start.8 = (bf16[4,2,64,672]{3,2,1,0:T(8,128)(2,1)S(1)}, bf16[4,2,64,672]{3,2,1,0:T(8,128)(2,1)S(1)}, u32[]{:S(2)}, u32[]{:S(2)}) collective-permute-start(bf16[4,2,64,672]{3,2,1,0:T(8,128)(2,1)S(1)} %collective-permute-done.4.refs_2_), channel_id=1, source_target_pairs={{0,1},{1,0},{2,3},{3,2},{4,5},{5,4},{6,7},{7,6},{8,9},{9,8},{10,11... | collective-permute-start | bytes 2064392 | tf_op jit(solution)/shard_map/gather_xy/ppermute | solution.py:33
  55.5 3.4 %collective-permute-start.7 = (bf16[4,2,64,672]{3,2,1,0:T(8,128)(2,1)S(1)}, bf16[4,2,64,672]{3,2,1,0:T(8,128)(2,1)S(1)}, u32[]{:S(2)}, u32[]{:S(2)}) collective-permute-start(bf16[4,2,64,672]{3,2,1,0:T(8,128)(2,1)S(1)} %collective-permute-done.3.refs_1_), channel_id=1, source_target_pairs={{0,1},{1,0},{2,3},{3,2},{4,5},{5,4},{6,7},{7,6},{8,9},{9,8},{10,11... | collective-permute-start | bytes 2064392 | tf_op jit(solution)/shard_map/gather_xy/ppermute | solution.py:33
  97.9 3.5 %collective-permute-start.10 = (bf16[4,4,64,672]{3,2,1,0:T(8,128)(2,1)S(1)}, bf16[4,4,64,672]{3,2,1,0:T(8,128)(2,1)S(1)}, u32[]{:S(2)}, u32[]{:S(2)}) collective-permute-start(bf16[4,4,64,672]{3,2,1,0:T(8,128)(2,1)S(1)} %get-tuple-element.18), channel_id=1, source_target_pairs={{0,1},{1,0},{2,3},{3,2},{4,5},{5,4},{6,7},{7,6},{8,9},{9,8},{10,11... | collective-permute-start | bytes 4128776 | tf_op jit(solution)/shard_map/scatter_core/ppermute | solution.py:33
  101.8 11.7 %collective-permute-start.11 = (bf16[4,64,672]{2,1,0:T(8,128)(2,1)S(1)}, bf16[4,64,672]{2,1,0:T(8,128)(2,1)S(1)}, u32[]{:S(2)}, u32[]{:S(2)}) collective-permute-start(bf16[4,64,672]{2,1,0:T(8,128)(2,1)S(1)} %get-tuple-element.21), channel_id=1, source_target_pairs={{0,2},{1,9},{2,4},{3,11},{4,6},{5,13},{6,0},{7,15},{8,10},{9,17},{... | collective-permute-start | bytes 1032200 | tf_op jit(solution)/shard_map/scatter_xy/ppermute | solution.py:33
  103.9 9.5 %collective-permute-start.13 = (bf16[4,64,672]{2,1,0:T(8,128)(2,1)S(1)}, bf16[4,64,672]{2,1,0:T(8,128)(2,1)S(1)}, u32[]{:S(2)}, u32[]{:S(2)}) collective-permute-start(bf16[4,64,672]{2,1,0:T(8,128)(2,1)S(1)} %get-tuple-element.22), channel_id=1, source_target_pairs={{0,4},{1,17},{2,6},{3,19},{4,0},{5,21},{6,2},{7,23},{8,12},{9,25},... | collective-permute-start | bytes 1032200 | tf_op jit(solution)/shard_map/scatter_xy/ppermute | solution.py:33
  104.3 13.1 %collective-permute-start.12 = (bf16[4,64,672]{2,1,0:T(8,128)(2,1)S(1)}, bf16[4,64,672]{2,1,0:T(8,128)(2,1)S(1)}, u32[]{:S(2)}, u32[]{:S(2)}) collective-permute-start(bf16[4,64,672]{2,1,0:T(8,128)(2,1)S(1)} %get-tuple-element.23), channel_id=1, source_target_pairs={{0,6},{1,25},{2,0},{3,27},{4,2},{5,29},{6,4},{7,31},{8,14},{9,1},{... | collective-permute-start | bytes 1032200 | tf_op jit(solution)/shard_map/scatter_xy/ppermute | solution.py:33
  117.7 7.0 %collective-permute-start.14 = (bf16[64,672]{1,0:T(8,128)(2,1)S(1)}, bf16[64,672]{1,0:T(8,128)(2,1)S(1)}, u32[]{:S(2)}, u32[]{:S(2)}) collective-permute-start(bf16[64,672]{1,0:T(8,128)(2,1)S(1)} %get-tuple-element.24), channel_id=1, source_target_pairs={{0,8},{1,3},{2,10},{3,5},{4,12},{5,7},{6,14},{7,1},{8,16},{9,11},{... | collective-permute-start | bytes 258056 | tf_op jit(solution)/shard_map/scatter_yx/ppermute | solution.py:33
  117.8 6.9 %collective-permute-start.16 = (bf16[64,672]{1,0:T(8,128)(2,1)S(1)}, bf16[64,672]{1,0:T(8,128)(2,1)S(1)}, u32[]{:S(2)}, u32[]{:S(2)}) collective-permute-start(bf16[64,672]{1,0:T(8,128)(2,1)S(1)} %get-tuple-element.25), channel_id=1, source_target_pairs={{0,16},{1,5},{2,18},{3,7},{4,20},{5,1},{6,22},{7,3},{8,24},{9,13},... | collective-permute-start | bytes 258056 | tf_op jit(solution)/shard_map/scatter_yx/ppermute | solution.py:33
  120.4 5.2 %collective-permute-start.15 = (bf16[64,672]{1,0:T(8,128)(2,1)S(1)}, bf16[64,672]{1,0:T(8,128)(2,1)S(1)}, u32[]{:S(2)}, u32[]{:S(2)}) collective-permute-start(bf16[64,672]{1,0:T(8,128)(2,1)S(1)} %get-tuple-element.26), channel_id=1, source_target_pairs={{0,24},{1,7},{2,26},{3,1},{4,28},{5,3},{6,30},{7,5},{8,0},{9,15},{... | collective-permute-start | bytes 258056 | tf_op jit(solution)/shard_map/scatter_yx/ppermute | solution.py:33

commit v2 on v1

v2 whole, which is shorter than its diff:
```python
import functools

import jax
import jax.numpy as jnp
from jax import lax
from jax.experimental import pallas as pl
from jax.experimental.pallas import tpu as pltpu
from jax.sharding import Mesh, PartitionSpec as P

AXES = ("z", "y", "x", "c")
BF = jnp.bfloat16
F32 = jnp.float32
VMEM = pl.BlockSpec(memory_space=pltpu.VMEM)
ANY = pl.BlockSpec(memory_space=pl.ANY)
MIB = 1024 * 1024
NZ, NQ = 8, 4


def perm(move):
    pairs = []
    for z in range(NZ):
        for y in range(NQ):
            for x in range(NQ):
                for c in range(2):
                    tz, ty, tx, tc = move(z, y, x, c)
                    src = ((z * NQ + y) * NQ + x) * 2 + c
                    dst = ((tz % NZ * NQ + ty % NQ) * NQ + tx % NQ) * 2 + tc
                    pairs.append((src, dst))
    return pairs


def send(value, move):
    return lax.ppermute(value, AXES, perm(move))


def along_yx(k):
    return lambda z, y, x, c: (z, y + k, x, c) if c == 0 else (z, y, x + k, c)


def along_xy(k):
    return lambda z, y, x, c: (z, y, x + k, c) if c == 0 else (z, y + k, x, c)


def other_core(z, y, x, c):
    return (z, y, x, 1 - c)


HOPS = (1, 3, 2)


def all_of(value, axes):
    return lax.all_to_all(value, axes, 0, 0)


def load_kernel(w, _, out, sem):
    copy = pltpu.make_async_copy(w, out, sem)
    copy.start()
    copy.wait()


def times_weight(refs, out):
    pieces = refs[: 2 * NQ]
    w, held, whole = refs[2 * NQ :]
    step = pl.program_id(0)
    rows = w.shape[0] // pl.num_programs(0)
    tokens, width = out.shape[1], held.shape[-1]

    @pl.when(step == 0)
    def _():
        y, x, c = lax.axis_index("y"), lax.axis_index("x"), lax.axis_index("c")
        for own in range(2):
            parity = c if own == 0 else 1 - c
            for k in range(NQ):
                for r in range(NQ):
                    x_back = jnp.where(parity == 0, k, r)
                    y_back = jnp.where(parity == 0, r, k)
                    x_at = lax.rem(x + NQ - x_back, NQ)
                    y_at = lax.rem(y + NQ - y_back, NQ)
                    held[2 * x_at + parity, y_at] = pieces[own * NQ + k][r]
        for t in range(2 * NQ):
            whole[:, t * width : (t + 1) * width] = held[t].reshape(tokens, width)

    at = pl.ds(pl.multiple_of(step * rows, rows), rows)
    out[at, :] = lax.dot_general(
        w[at, :], whole[...], (((1,), (1,)), ((), ())), preferred_element_type=F32
    )


def scores_kernel(*refs):
    raised, stats = refs[-4:-2]
    times_weight((*refs[:-4], *refs[-2:]), raised)

    @pl.when(pl.program_id(0) == pl.num_programs(0) - 1)
    def _():
        top = jnp.max(raised[...], axis=0, keepdims=True)
        value = jnp.exp(raised[...] - top)
        raised[...] = value
        total = jnp.sum(value, axis=0, keepdims=True)
        stats[...] = jnp.concatenate((top, total, total, total), 0)


def slopes_kernel(raised, top, *refs):
    slopes, stats = refs[-4:-2]
    times_weight((*refs[:-4], *refs[-2:]), slopes)

    @pl.when(pl.program_id(0) == pl.num_programs(0) - 1)
    def _():
        dotted = jnp.sum(raised[...] * slopes[...], axis=0, keepdims=True)
        own = jnp.concatenate((top[0:2, :], dotted, dotted), 0)
        stats[...] = jnp.broadcast_to(own[None], stats.shape)


def merged(parts):
    tops = parts[:, 0]
    top = jnp.max(tops, axis=0, keepdims=True)
    scale = jnp.exp(tops - top)
    total = jnp.sum(scale * parts[:, 1], axis=0, keepdims=True)
    dotted = jnp.sum(scale * parts[:, 2], axis=0, keepdims=True)
    return top, total, dotted


def merge_kernel(parts, out):
    top, total, dotted = merged(parts[...])
    own = jnp.concatenate((top, total, dotted, dotted), 0)
    out[...] = jnp.broadcast_to(own[None], out.shape)


def part_product(mixture, w, parity, out):
    y, x = lax.axis_index("y"), lax.axis_index("x")
    width, part = out.shape[-1], out.shape[-2]
    for x_of in range(NQ):
        first = (2 * x_of + parity) * width
        start = first // 128 * 128
        stop = -(-(first + width) // 128) * 128
        product = jnp.dot(mixture[...], w[:, start:stop], preferred_element_type=F32)
        piece = product[:, first - start : first - start + width].astype(out.dtype)
        x_ahead = lax.rem(x_of + NQ - x, NQ)
        for y_of in range(NQ):
            y_ahead = lax.rem(y_of + NQ - y, NQ)
            k, r = (x_ahead, y_ahead) if parity == 0 else (y_ahead, x_ahead)
            out[k, r] = piece[y_of * part : (y_of + 1) * part]


def give_kernel(parts, own_top, raised, slopes, w, give, mixture):
    top, total, dotted = merged(parts[...])
    scale = jnp.exp(own_top[0:1, :] - top) / total
    mean = dotted / total
    mix = (raised[...] * scale) * (slopes[...] - mean)
    mixture[...] = mix.T.astype(BF)
    for parity in range(2):
        pl.when(lax.axis_index("c") != parity)(
            functools.partial(part_product, mixture, w, parity, give)
        )


def keep_kernel(mixture, w, keep):
    for parity in range(2):
        pl.when(lax.axis_index("c") == parity)(
            functools.partial(part_product, mixture, w, parity, keep)
        )


def per_device(hidden, tangent, out_weight):
    rows, width = hidden.shape
    vocab, features = out_weight.shape
    tokens = rows * NZ * NQ
    shape = jax.ShapeDtypeStruct

    with jax.named_scope("gather_z"):
        own = jnp.stack((hidden, tangent))
        block = all_of(jnp.broadcast_to(own[None], (NZ, *own.shape)), "z")
        block = block.transpose(1, 0, 2, 3).reshape(2, rows * NZ, width)
    with jax.named_scope("gather_yx"):
        pieces = {0: block}
        for k in HOPS:
            pieces[k] = send(block, along_yx(k))
        blocks = [jnp.stack([pieces[k][i] for k in range(NQ)]) for i in range(2)]
        weight = pl.pallas_call(
            load_kernel,
            out_shape=pltpu.VMEM((vocab, features), BF),
            in_specs=[ANY, ANY],
            out_specs=VMEM,
            scratch_shapes=[pltpu.SemaphoreType.DMA],
            cost_estimate=pl.CostEstimate(
                flops=0, transcendentals=0, bytes_accessed=4 * vocab * features
            ),
            compiler_params=pltpu.CompilerParams(vmem_limit_bytes=MIB),
        )(pltpu.with_memory_space_constraint(out_weight, pltpu.HBM), blocks[0])
    with jax.named_scope("gather_xy"):
        mine, theirs = [], []
        for block in blocks:
            mine.append({0: block})
            for k in HOPS:
                mine[-1][k] = send(block, along_xy(k))
        mine[0][0], weight = lax.optimization_barrier((mine[0][0], weight))
        theirs.append({k: send(mine[0][k], other_core) for k in (0,) + HOPS})
        inputs = [[*(mine[0][k] for k in range(NQ)), *(theirs[0][k] for k in range(NQ))]]

    steps = 4
    at_once = lambda *n: pl.BlockSpec(n, lambda i: (0,) * len(n))
    scratch = [
        pltpu.VMEM((2 * NQ, NQ, rows * NZ, width), BF),
        pltpu.VMEM((tokens, features), BF),
    ]
    with jax.named_scope("scores"):
        raised, top = pl.pallas_call(
            scores_kernel,
            grid=(steps,),
            out_shape=(shape((vocab, tokens), F32), shape((4, tokens), F32)),
            in_specs=[VMEM] * (2 * NQ + 1),
            out_specs=(at_once(vocab, tokens), at_once(4, tokens)),
            scratch_shapes=scratch,
            cost_estimate=pl.CostEstimate(flops=0, transcendentals=0, bytes_accessed=0),
            compiler_params=pltpu.CompilerParams(vmem_limit_bytes=24 * MIB),
        )(*inputs[0], weight)
    with jax.named_scope("gather_xy"):
        theirs.append({0: send(mine[1][0], other_core)})
        held = lax.optimization_barrier((raised, *(mine[1][k] for k in HOPS)))
        raised = held[0]
        for k, piece in zip(HOPS, held[1:]):
            mine[1][k] = piece
            theirs[1][k] = send(piece, other_core)
        inputs.append([*(mine[1][k] for k in range(NQ)), *(theirs[1][k] for k in range(NQ))])
    with jax.named_scope("slopes"):
        slopes, stats = pl.pallas_call(
            slopes_kernel,
            grid=(steps,),
            out_shape=(shape((vocab, tokens), F32), shape((2 * NQ, 4, tokens), F32)),
            in_specs=[VMEM] * (2 * NQ + 3),
            out_specs=(at_once(vocab, tokens), at_once(2 * NQ, 4, tokens)),
            scratch_shapes=scratch,
            compiler_params=pltpu.CompilerParams(vmem_limit_bytes=24 * MIB),
        )(raised, top, *inputs[1], weight)

    with jax.named_scope("statistics"):
        stats = pl.pallas_call(
            merge_kernel,
            out_shape=shape((NZ * NQ, 4, tokens), F32),
            in_specs=[VMEM],
            out_specs=VMEM,
            compiler_params=pltpu.CompilerParams(vmem_limit_bytes=4 * MIB),
        )(all_of(stats, ("x", "c")))
        parts = all_of(stats, ("z", "y"))

    with jax.named_scope("product"):
        give, mixture = pl.pallas_call(
            give_kernel,
            out_shape=(
                shape((NQ, NQ, rows * NZ, width), BF),
                shape((tokens, vocab), BF),
            ),
            in_specs=[VMEM] * 5,
            out_specs=(VMEM, VMEM),
            compiler_params=pltpu.CompilerParams(vmem_limit_bytes=16 * MIB),
        )(parts, top, raised, slopes, weight)
        got = send(give, other_core)
        keep = pl.pallas_call(
            keep_kernel,
            out_shape=shape((NQ, NQ, rows * NZ, width), F32),
            in_specs=[VMEM] * 2,
            out_specs=VMEM,
            cost_estimate=pl.CostEstimate(
                flops=vocab * tokens * features,
                transcendentals=0,
                bytes_accessed=2 * vocab * features,
            ),
            compiler_params=pltpu.CompilerParams(vmem_limit_bytes=16 * MIB),
        )(mixture, weight)

    with jax.named_scope("scatter_xy"):
        sums = [keep[k] + got[k].astype(F32) for k in range(NQ)]
        total = sums[0]
        for k in HOPS:
            total = total + send(sums[k].astype(BF), along_xy(k)).astype(F32)
    with jax.named_scope("scatter_yx"):
        total, rest = total[0], total
        for k in HOPS:
            total = total + send(rest[k].astype(BF), along_yx(k)).astype(F32)
    with jax.named_scope("scatter_z"):
        return jnp.sum(all_of(total.reshape(NZ, rows, width), "z"), axis=0)


def solution(mesh):
    fine = Mesh(mesh.devices.reshape(NZ, NQ, NQ, 2), AXES)
    tokens = P(("z", "y"), ("x", "c"))
    return jax.shard_map(
        per_device,
        mesh=fine,
        in_specs=(tokens, tokens, P(AXES, None)),
        out_specs=tokens,
        check_vma=False,
    )
```

time: 138 us -> 133 us (0.964)
  waiting for transfers between devices: 45.5 us -> 37.1 us
  starting transfers between devices: 16.5 us -> 21.6 us
    ppermute x17 -> x24, waiting for transfers between devices: 45.5 us -> 37.1 us  [send(): return lax.ppermute(value, AXES, perm(move))]
    ppermute x17 -> x24, starting transfers between devices: 16.5 us -> 21.6 us  [send(): return lax.ppermute(value, AXES, perm(move))]
    pallas_call x1, Pallas kernels: 8.58 us -> 4.91 us  [per_device(): pl.pallas_call(scores_kernel, grid=(steps,), out_shape=(shape((vocab, tok...]
    pallas_call x2 -> x4, Pallas kernels: 6.29 us -> 9.14 us  [the longest x1 4.87 us: per_device(): pl.pallas_call(slopes_kernel, grid=(steps,), out_shape=(shape((vocab, tok...]
  transfers between devices with their start and end apart: 17 -> 24, of which waited for: 13 -> 15; matrix products, arithmetic and copies ran while one was open for 0% -> 0% of each run, Pallas kernels for 3% -> 8%
where the time goes in v2:
time: 133 us
  blocking collectives  53.4 us (40%)
  waiting for transfers between devices  37.1 us (28%)
  starting transfers between devices  21.6 us (16%)
  Pallas kernels  18.2 us (14%)
  other arithmetic  2.08 us (2%)
    all_to_all x4, blocking collectives, all_of(): return lax.all_to_all(value, axes, 0, 0)  53.4 us
    ppermute x24, waiting for transfers between devices, send(): return lax.ppermute(value, AXES, perm(move))  37.1 us
    ppermute x24, starting transfers between devices, send(): return lax.ppermute(value, AXES, perm(move))  21.6 us
    pallas_call x1, Pallas kernels, per_device(): pl.pallas_call(scores_kernel, grid=(steps,), out_shape=(shape((vocab, tok...  4.91 us
    pallas_call x1, Pallas kernels, per_device(): pl.pallas_call(slopes_kernel, grid=(steps,), out_shape=(shape((vocab, tok...  4.87 us
    pallas_call x1, Pallas kernels, per_device(): pl.pallas_call(load_kernel, out_shape=pltpu.VMEM((vocab, features), BF),...  4.14 us
  transfers between devices with their start and end apart: 24, of which 15 were waited for; matrix products, arithmetic and copies ran while one was open for 0% of the time, Pallas kernels for 8%

profile of v2, /device:TPU:6, one launch (start us, length us, event | category | flops | bytes accessed | tf_op | source)
XLA Modules:
  0.0 132.6 jit_solution(3088387708609195390)
XLA Ops:
  0.0 0.7 pad_maximum_fusion.2
  0.8 18.7 %all_to_all.20 = bf16[8,2,8,672]{3,2,1,0:T(8,128)(2,1)S(1)} all-to-all(bf16[8,2,8,672]{3,2,1,0:T(8,128)(2,1)S(1)} %broadcast_in_dim.2), channel_id=1, replica_groups=mesh['z'=8,'y'=4,'x'=4,'c'=2] {'z'}, dimensions={0} | all-to-all | bytes 344064 | tf_op jit(solution)/shard_map/gather_z/all_to_all | solution.py:52
  19.5 1.7 %collective-permute-start = (bf16[2,64,672]{2,1,0:T(8,128)(2,1)S(1)}, bf16[2,64,672]{2,1,0:T(8,128)(2,1)S(1)}, u32[]{:S(2)}, u32[]{:S(2)}) collective-permute-start(bf16[2,64,672]{2,1,0:T(8,128)(2,1)S(1)} %copy_bitcast_fusion), channel_id=1, source_target_pairs={{0,8},{1,3},{2,10},{3,5},{4,12},{5,7},{6,14},{7,1},{8,16},{9,11},{... | collective-permute-start | bytes 516104 | tf_op jit(solution)/shard_map/gather_yx/ppermute | solution.py:33
  21.2 2.9 %collective-permute-start.1 = (bf16[2,64,672]{2,1,0:T(8,128)(2,1)S(1)}, bf16[2,64,672]{2,1,0:T(8,128)(2,1)S(1)}, u32[]{:S(2)}, u32[]{:S(2)}) collective-permute-start(bf16[2,64,672]{2,1,0:T(8,128)(2,1)S(1)} %copy_bitcast_fusion), channel_id=1, source_target_pairs={{0,16},{1,5},{2,18},{3,7},{4,20},{5,1},{6,22},{7,3},{8,24},{9,13},... | collective-permute-start | bytes 516104 | tf_op jit(solution)/shard_map/gather_yx/ppermute | solution.py:33
  24.1 1.3 %collective-permute-start.2 = (bf16[2,64,672]{2,1,0:T(8,128)(2,1)S(1)}, bf16[2,64,672]{2,1,0:T(8,128)(2,1)S(1)}, u32[]{:S(2)}, u32[]{:S(2)}) collective-permute-start(bf16[2,64,672]{2,1,0:T(8,128)(2,1)S(1)} %copy_bitcast_fusion), channel_id=1, source_target_pairs={{0,24},{1,7},{2,26},{3,1},{4,28},{5,3},{6,30},{7,5},{8,0},{9,15},{... | collective-permute-start | bytes 516104 | tf_op jit(solution)/shard_map/gather_yx/ppermute | solution.py:33
  25.4 1.0 collective-permute-done
  26.5 3.3 %collective-permute-done.1 = bf16[2,64,672]{2,1,0:T(8,128)(2,1)S(1)} collective-permute-done((bf16[2,64,672]{2,1,0:T(8,128)(2,1)S(1)}, bf16[2,64,672]{2,1,0:T(8,128)(2,1)S(1)}, u32[]{:S(2)}, u32[]{:S(2)}) %collective-permute-start.1) | collective-permute-done | bytes 172064 | tf_op jit(solution)/shard_map/gather_yx/ppermute | solution.py:33
  29.8 0.0 collective-permute-done.2
  29.9 0.1 pad_maximum_fusion._.refs_0_
  29.9 0.6 collective-permute-start.3
  30.5 2.4 %collective-permute-start.4 = (bf16[4,64,672]{2,1,0:T(8,128)(2,1)S(1)}, bf16[4,64,672]{2,1,0:T(8,128)(2,1)S(1)}, u32[]{:S(2)}, u32[]{:S(2)}) collective-permute-start(bf16[4,64,672]{2,1,0:T(8,128)(2,1)S(1)} %pad_maximum_fusion._.refs_0_), channel_id=1, source_target_pairs={{0,4},{1,17},{2,6},{3,19},{4,0},{5,21},{6,2},{7,23},{8,12},{9,25},... | collective-permute-start | bytes 1032200 | tf_op jit(solution)/shard_map/gather_xy/ppermute | solution.py:33
  32.9 0.0 collective-permute-start.5
  32.9 4.1 %gather_yx.1.refs_8_.w = bf16[1024,5376]{1,0:T(8,128)(2,1)S(1)} custom-call(bf16[1024,5376]{1,0:T(8,128)(2,1)} %w.1, bf16[4,64,672]{2,1,0:T(8,128)(2,1)S(1)} %pad_maximum_fusion._.refs_0_), custom_call_target="tpu_custom_call" | custom-call | bytes 22020096 | tf_op jit(solution)/shard_map/gather_yx/pallas_call | solution.py:178
  37.0 0.1 collective-permute-start.6
  37.1 0.6 collective-permute-done.3.refs_1_
  37.8 0.0 collective-permute-start.7
  37.8 0.1 pad_maximum_fusion.1.refs_0_
  37.8 2.0 %collective-permute-done.4.refs_2_ = bf16[4,64,672]{2,1,0:T(8,128)(2,1)S(1)} collective-permute-done((bf16[4,64,672]{2,1,0:T(8,128)(2,1)S(1)}, bf16[4,64,672]{2,1,0:T(8,128)(2,1)S(1)}, u32[]{:S(2)}, u32[]{:S(2)}) %collective-permute-start.4) | collective-permute-done | bytes 344096 | tf_op jit(solution)/shard_map/gather_xy/ppermute | solution.py:33
  39.9 0.0 collective-permute-start.8
  39.9 4.1 %collective-permute-done.5.refs_3_ = bf16[4,64,672]{2,1,0:T(8,128)(2,1)S(1)} collective-permute-done((bf16[4,64,672]{2,1,0:T(8,128)(2,1)S(1)}, bf16[4,64,672]{2,1,0:T(8,128)(2,1)S(1)}, u32[]{:S(2)}, u32[]{:S(2)}) %collective-permute-start.5) | collective-permute-done | bytes 344096 | tf_op jit(solution)/shard_map/gather_xy/ppermute | solution.py:33
  44.0 0.0 collective-permute-start.9
  44.0 1.2 collective-permute-start.10
  45.2 0.0 collective-permute-done.6.refs_4_
  45.2 0.8 collective-permute-start.11
  46.0 0.0 collective-permute-done.7.refs_5_
  46.0 2.0 %collective-permute-start.12 = (bf16[4,64,672]{2,1,0:T(8,128)(2,1)S(1)}, bf16[4,64,672]{2,1,0:T(8,128)(2,1)S(1)}, u32[]{:S(2)}, u32[]{:S(2)}) collective-permute-start(bf16[4,64,672]{2,1,0:T(8,128)(2,1)S(1)} %pad_maximum_fusion.1.refs_0_), channel_id=1, source_target_pairs={{0,4},{1,17},{2,6},{3,19},{4,0},{5,21},{6,2},{7,23},{8,12},{9,25},... | collective-permute-start | bytes 1032200 | tf_op jit(solution)/shard_map/gather_xy/ppermute | solution.py:33
  48.0 0.0 collective-permute-done.8.refs_6_
  48.0 0.5 collective-permute-start.13
  48.5 0.0 collective-permute-done.9.refs_7_
  48.5 4.9 %scores.1 = (f32[1024,256]{1,0:T(8,128)S(1)}, f32[4,256]{1,0:T(4,128)S(1)}) custom-call(bf16[4,64,672]{2,1,0:T(8,128)(2,1)S(1)} %pad_maximum_fusion._.refs_0_, bf16[4,64,672]{2,1,0:T(8,128)(2,1)S(1)} %collective-permute-done.3.refs_1_, bf16[4,64,672]{2,1,0:T(8,128)(2,1)S(1)} %collective-permute-done.4.refs_2_, ...), custom_call_target="tpu_custom_call" | custom-call | tf_op jit(solution)/shard_map/scores/pallas_call | solution.py:206
  53.4 0.0 collective-permute-done.10.refs_1_
  53.4 5.0 %collective-permute-done.11.refs_3_ = bf16[4,64,672]{2,1,0:T(8,128)(2,1)S(1)} collective-permute-done((bf16[4,64,672]{2,1,0:T(8,128)(2,1)S(1)}, bf16[4,64,672]{2,1,0:T(8,128)(2,1)S(1)}, u32[]{:S(2)}, u32[]{:S(2)}) %collective-permute-start.11) | collective-permute-done | bytes 344096 | tf_op jit(solution)/shard_map/gather_xy/ppermute | solution.py:33
  58.4 0.0 collective-permute-done.12.refs_2_
  58.4 0.0 collective-permute-start.14
  58.4 0.5 collective-permute-start.15
  58.9 0.0 collective-permute-start.16
  58.9 0.0 collective-permute-done.13.refs_4_
  58.9 1.2 collective-permute-done.14.refs_5_
  60.1 0.6 collective-permute-done.15.refs_6_
  60.7 0.6 collective-permute-done.16.refs_7_
  61.2 4.9 %slopes.1 = (f32[1024,256]{1,0:T(8,128)S(1)}, f32[8,4,256]{2,1,0:T(4,128)S(1)}) custom-call(f32[1024,256]{1,0:T(8,128)S(1)} %get-tuple-element.20.raised, f32[4,256]{1,0:T(4,128)S(1)} %get-tuple-element.21.top.own_top, bf16[4,64,672]{2,1,0:T(8,128)(2,1)S(1)} %pad_maximum_fusion.1.refs_0_, bf16[4,64,672]{2,1,0:T(8,128)(2,1)S(1)} %collective-permute-done.10.refs_1_, ...), custom_call_target="tpu_custom_call" | custom-call | tf_op jit(solution)/shard_map/slopes/pallas_call | solution.py:225
  66.1 7.7 %all_to_all.21.parts = f32[8,4,256]{2,1,0:T(4,128)S(1)} all-to-all(f32[8,4,256]{2,1,0:T(4,128)S(1)} %get-tuple-element.25), channel_id=1, replica_groups=mesh['z'=8,'y'=4,'x'=4,'c'=2] {'x','c'}, dimensions={0} | all-to-all | bytes 65536 | tf_op jit(solution)/shard_map/statistics/all_to_all | solution.py:52
  73.8 14.8 %all_to_all.22.parts = f32[32,4,256]{2,1,0:T(4,128)S(1)} all-to-all(f32[32,4,256]{2,1,0:T(4,128)S(1)} %statistics.1), channel_id=1, replica_groups=mesh['z'=8,'y'=4,'x'=4,'c'=2] {'z','y'}, dimensions={0} | all-to-all | bytes 262144 | tf_op jit(solution)/shard_map/statistics/all_to_all | solution.py:52
  88.6 2.2 %product.2 = (bf16[4,4,64,672]{3,2,1,0:T(8,128)(2,1)S(1)}, bf16[256,1024]{1,0:T(8,128)(2,1)S(1)}) custom-call(f32[32,4,256]{2,1,0:T(4,128)S(1)} %all_to_all.22.parts, f32[4,256]{1,0:T(4,128)S(1)} %get-tuple-element.21.top.own_top, f32[1024,256]{1,0:T(8,128)S(1)} %get-tuple-element.20.raised, f32[1024,256]{1,0:T(8,128)S(1)} %get-tuple-element.26.slopes, ...), custom_call_target="tpu_custom_call" | custom-call | tf_op jit(solution)/shard_map/product/pallas_call | solution.py:246
  90.9 0.1 collective-permute-start.17
  91.0 2.0 %product.3 = f32[4,4,64,672]{3,2,1,0:T(8,128)S(1)} custom-call(bf16[256,1024]{1,0:T(8,128)(2,1)S(1)} %get-tuple-element.27.mixture, bf16[1024,5376]{1,0:T(8,128)(2,1)S(1)} %gather_yx.1.refs_8_.w), custom_call_target="tpu_custom_call" | custom-call | flops 1409286144 | bytes 11010048 | tf_op jit(solution)/shard_map/product/pallas_call | solution.py:257
  93.0 1.4 %collective-permute-done.17 = bf16[4,4,64,672]{3,2,1,0:T(8,128)(2,1)S(1)} collective-permute-done((bf16[4,4,64,672]{3,2,1,0:T(8,128)(2,1)S(1)}, bf16[4,4,64,672]{3,2,1,0:T(8,128)(2,1)S(1)}, u32[]{:S(2)}, u32[]{:S(2)}) %collective-permute-start.17) | collective-permute-done | bytes 1376288 | tf_op jit(solution)/shard_map/product/ppermute | solution.py:33
  94.4 0.3 fusion.7
  94.7 2.1 %collective-permute-start.18 = (bf16[4,64,672]{2,1,0:T(8,128)(2,1)S(1)}, bf16[4,64,672]{2,1,0:T(8,128)(2,1)S(1)}, u32[]{:S(2)}, u32[]{:S(2)}) collective-permute-start(bf16[4,64,672]{2,1,0:T(8,128)(2,1)S(1)} %get-tuple-element.31), channel_id=1, source_target_pairs={{0,2},{1,9},{2,4},{3,11},{4,6},{5,13},{6,0},{7,15},{8,10},{9,17},{... | collective-permute-start | bytes 1032200 | tf_op jit(solution)/shard_map/scatter_xy/ppermute | solution.py:33
  96.8 0.0 collective-permute-start.19
  96.8 2.0 %collective-permute-start.20 = (bf16[4,64,672]{2,1,0:T(8,128)(2,1)S(1)}, bf16[4,64,672]{2,1,0:T(8,128)(2,1)S(1)}, u32[]{:S(2)}, u32[]{:S(2)}) collective-permute-start(bf16[4,64,672]{2,1,0:T(8,128)(2,1)S(1)} %get-tuple-element.32), channel_id=1, source_target_pairs={{0,4},{1,17},{2,6},{3,19},{4,0},{5,21},{6,2},{7,23},{8,12},{9,25},... | collective-permute-start | bytes 1032200 | tf_op jit(solution)/shard_map/scatter_xy/ppermute | solution.py:33
  98.9 7.5 %collective-permute-done.18 = bf16[4,64,672]{2,1,0:T(8,128)(2,1)S(1)} collective-permute-done((bf16[4,64,672]{2,1,0:T(8,128)(2,1)S(1)}, bf16[4,64,672]{2,1,0:T(8,128)(2,1)S(1)}, u32[]{:S(2)}, u32[]{:S(2)}) %collective-permute-start.18) | collective-permute-done | bytes 344096 | tf_op jit(solution)/shard_map/scatter_xy/ppermute | solution.py:33
  106.4 3.7 %collective-permute-done.19 = bf16[4,64,672]{2,1,0:T(8,128)(2,1)S(1)} collective-permute-done((bf16[4,64,672]{2,1,0:T(8,128)(2,1)S(1)}, bf16[4,64,672]{2,1,0:T(8,128)(2,1)S(1)}, u32[]{:S(2)}, u32[]{:S(2)}) %collective-permute-start.19) | collective-permute-done | bytes 344096 | tf_op jit(solution)/shard_map/scatter_xy/ppermute | solution.py:33
  110.0 0.0 collective-permute-done.20
  110.0 0.2 fusion.14
  110.3 0.2 collective-permute-start.21
  110.5 3.1 %collective-permute-start.22 = (bf16[64,672]{1,0:T(8,128)(2,1)S(1)}, bf16[64,672]{1,0:T(8,128)(2,1)S(1)}, u32[]{:S(2)}, u32[]{:S(2)}) collective-permute-start(bf16[64,672]{1,0:T(8,128)(2,1)S(1)} %get-tuple-element.36), channel_id=1, source_target_pairs={{0,24},{1,7},{2,26},{3,1},{4,28},{5,3},{6,30},{7,5},{8,0},{9,15},{... | collective-permute-start | bytes 258056 | tf_op jit(solution)/shard_map/scatter_yx/ppermute | solution.py:33
  113.6 0.0 collective-permute-start.23
  113.7 2.6 %collective-permute-done.21 = bf16[64,672]{1,0:T(8,128)(2,1)S(1)} collective-permute-done((bf16[64,672]{1,0:T(8,128)(2,1)S(1)}, bf16[64,672]{1,0:T(8,128)(2,1)S(1)}, u32[]{:S(2)}, u32[]{:S(2)}) %collective-permute-start.21) | collective-permute-done | bytes 86048 | tf_op jit(solution)/shard_map/scatter_yx/ppermute | solution.py:33
  116.2 0.6 collective-permute-done.22
  116.8 2.9 %collective-permute-done.23 = bf16[64,672]{1,0:T(8,128)(2,1)S(1)} collective-permute-done((bf16[64,672]{1,0:T(8,128)(2,1)S(1)}, bf16[64,672]{1,0:T(8,128)(2,1)S(1)}, u32[]{:S(2)}, u32[]{:S(2)}) %collective-permute-start.23) | collective-permute-done | bytes 86048 | tf_op jit(solution)/shard_map/scatter_yx/ppermute | solution.py:33
  119.8 12.2 %all_to_all.23 = f32[8,8,672]{2,1,0:T(8,128)S(1)} all-to-all(f32[8,8,672]{2,1,0:T(8,128)S(1)} %fusion.13), channel_id=1, replica_groups=mesh['z'=8,'y'=4,'x'=4,'c'=2] {'z'}, dimensions={0} | all-to-all | bytes 344064 | tf_op jit(solution)/shard_map/scatter_z/all_to_all | solution.py:52
  132.0 0.6 reduce_sum.9
  (9 shorter events, 0.2 us)
Async XLA Ops:
  19.5 7.0 %collective-permute-start = (bf16[2,64,672]{2,1,0:T(8,128)(2,1)S(1)}, bf16[2,64,672]{2,1,0:T(8,128)(2,1)S(1)}, u32[]{:S(2)}, u32[]{:S(2)}) collective-permute-start(bf16[2,64,672]{2,1,0:T(8,128)(2,1)S(1)} %copy_bitcast_fusion), channel_id=1, source_target_pairs={{0,8},{1,3},{2,10},{3,5},{4,12},{5,7},{6,14},{7,1},{8,16},{9,11},{... | collective-permute-start | bytes 516104 | tf_op jit(solution)/shard_map/gather_yx/ppermute | solution.py:33
  21.2 8.7 %collective-permute-start.1 = (bf16[2,64,672]{2,1,0:T(8,128)(2,1)S(1)}, bf16[2,64,672]{2,1,0:T(8,128)(2,1)S(1)}, u32[]{:S(2)}, u32[]{:S(2)}) collective-permute-start(bf16[2,64,672]{2,1,0:T(8,128)(2,1)S(1)} %copy_bitcast_fusion), channel_id=1, source_target_pairs={{0,16},{1,5},{2,18},{3,7},{4,20},{5,1},{6,22},{7,3},{8,24},{9,13},... | collective-permute-start | bytes 516104 | tf_op jit(solution)/shard_map/gather_yx/ppermute | solution.py:33
  24.1 5.8 %collective-permute-start.2 = (bf16[2,64,672]{2,1,0:T(8,128)(2,1)S(1)}, bf16[2,64,672]{2,1,0:T(8,128)(2,1)S(1)}, u32[]{:S(2)}, u32[]{:S(2)}) collective-permute-start(bf16[2,64,672]{2,1,0:T(8,128)(2,1)S(1)} %copy_bitcast_fusion), channel_id=1, source_target_pairs={{0,24},{1,7},{2,26},{3,1},{4,28},{5,3},{6,30},{7,5},{8,0},{9,15},{... | collective-permute-start | bytes 516104 | tf_op jit(solution)/shard_map/gather_yx/ppermute | solution.py:33
  29.9 7.9 %collective-permute-start.3 = (bf16[4,64,672]{2,1,0:T(8,128)(2,1)S(1)}, bf16[4,64,672]{2,1,0:T(8,128)(2,1)S(1)}, u32[]{:S(2)}, u32[]{:S(2)}) collective-permute-start(bf16[4,64,672]{2,1,0:T(8,128)(2,1)S(1)} %pad_maximum_fusion._.refs_0_), channel_id=1, source_target_pairs={{0,2},{1,9},{2,4},{3,11},{4,6},{5,13},{6,0},{7,15},{8,10},{9,17},{... | collective-permute-start | bytes 1032200 | tf_op jit(solution)/shard_map/gather_xy/ppermute | solution.py:33
  30.5 9.4 %collective-permute-start.4 = (bf16[4,64,672]{2,1,0:T(8,128)(2,1)S(1)}, bf16[4,64,672]{2,1,0:T(8,128)(2,1)S(1)}, u32[]{:S(2)}, u32[]{:S(2)}) collective-permute-start(bf16[4,64,672]{2,1,0:T(8,128)(2,1)S(1)} %pad_maximum_fusion._.refs_0_), channel_id=1, source_target_pairs={{0,4},{1,17},{2,6},{3,19},{4,0},{5,21},{6,2},{7,23},{8,12},{9,25},... | collective-permute-start | bytes 1032200 | tf_op jit(solution)/shard_map/gather_xy/ppermute | solution.py:33
  32.9 11.1 %collective-permute-start.5 = (bf16[4,64,672]{2,1,0:T(8,128)(2,1)S(1)}, bf16[4,64,672]{2,1,0:T(8,128)(2,1)S(1)}, u32[]{:S(2)}, u32[]{:S(2)}) collective-permute-start(bf16[4,64,672]{2,1,0:T(8,128)(2,1)S(1)} %pad_maximum_fusion._.refs_0_), channel_id=1, source_target_pairs={{0,6},{1,25},{2,0},{3,27},{4,2},{5,29},{6,4},{7,31},{8,14},{9,1},{... | collective-permute-start | bytes 1032200 | tf_op jit(solution)/shard_map/gather_xy/ppermute | solution.py:33
  37.0 8.1 %collective-permute-start.6 = (bf16[4,64,672]{2,1,0:T(8,128)(2,1)S(1)}, bf16[4,64,672]{2,1,0:T(8,128)(2,1)S(1)}, u32[]{:S(2)}, u32[]{:S(2)}) collective-permute-start(bf16[4,64,672]{2,1,0:T(8,128)(2,1)S(1)} %pad_maximum_fusion._.refs_0_), channel_id=1, source_target_pairs={{0,1},{1,0},{2,3},{3,2},{4,5},{5,4},{6,7},{7,6},{8,9},{9,8},{10,11... | collective-permute-start | bytes 1032200 | tf_op jit(solution)/shard_map/gather_xy/ppermute | solution.py:33
  37.8 8.2 %collective-permute-start.7 = (bf16[4,64,672]{2,1,0:T(8,128)(2,1)S(1)}, bf16[4,64,672]{2,1,0:T(8,128)(2,1)S(1)}, u32[]{:S(2)}, u32[]{:S(2)}) collective-permute-start(bf16[4,64,672]{2,1,0:T(8,128)(2,1)S(1)} %collective-permute-done.3.refs_1_), channel_id=1, source_target_pairs={{0,1},{1,0},{2,3},{3,2},{4,5},{5,4},{6,7},{7,6},{8,9},{9,8},{10,11... | collective-permute-start | bytes 1032200 | tf_op jit(solution)/shard_map/gather_xy/ppermute | solution.py:33
  39.9 8.2 %collective-permute-start.8 = (bf16[4,64,672]{2,1,0:T(8,128)(2,1)S(1)}, bf16[4,64,672]{2,1,0:T(8,128)(2,1)S(1)}, u32[]{:S(2)}, u32[]{:S(2)}) collective-permute-start(bf16[4,64,672]{2,1,0:T(8,128)(2,1)S(1)} %collective-permute-done.4.refs_2_), channel_id=1, source_target_pairs={{0,1},{1,0},{2,3},{3,2},{4,5},{5,4},{6,7},{7,6},{8,9},{9,8},{10,11... | collective-permute-start | bytes 1032200 | tf_op jit(solution)/shard_map/gather_xy/ppermute | solution.py:33
  44.0 4.5 %collective-permute-start.9 = (bf16[4,64,672]{2,1,0:T(8,128)(2,1)S(1)}, bf16[4,64,672]{2,1,0:T(8,128)(2,1)S(1)}, u32[]{:S(2)}, u32[]{:S(2)}) collective-permute-start(bf16[4,64,672]{2,1,0:T(8,128)(2,1)S(1)} %collective-permute-done.5.refs_3_), channel_id=1, source_target_pairs={{0,1},{1,0},{2,3},{3,2},{4,5},{5,4},{6,7},{7,6},{8,9},{9,8},{10,11... | collective-permute-start | bytes 1032200 | tf_op jit(solution)/shard_map/gather_xy/ppermute | solution.py:33
  44.0 9.4 %collective-permute-start.10 = (bf16[4,64,672]{2,1,0:T(8,128)(2,1)S(1)}, bf16[4,64,672]{2,1,0:T(8,128)(2,1)S(1)}, u32[]{:S(2)}, u32[]{:S(2)}) collective-permute-start(bf16[4,64,672]{2,1,0:T(8,128)(2,1)S(1)} %pad_maximum_fusion.1.refs_0_), channel_id=1, source_target_pairs={{0,2},{1,9},{2,4},{3,11},{4,6},{5,13},{6,0},{7,15},{8,10},{9,17},{... | collective-permute-start | bytes 1032200 | tf_op jit(solution)/shard_map/gather_xy/ppermute | solution.py:33
  45.2 13.2 %collective-permute-start.11 = (bf16[4,64,672]{2,1,0:T(8,128)(2,1)S(1)}, bf16[4,64,672]{2,1,0:T(8,128)(2,1)S(1)}, u32[]{:S(2)}, u32[]{:S(2)}) collective-permute-start(bf16[4,64,672]{2,1,0:T(8,128)(2,1)S(1)} %pad_maximum_fusion.1.refs_0_), channel_id=1, source_target_pairs={{0,6},{1,25},{2,0},{3,27},{4,2},{5,29},{6,4},{7,31},{8,14},{9,1},{... | collective-permute-start | bytes 1032200 | tf_op jit(solution)/shard_map/gather_xy/ppermute | solution.py:33
  46.0 12.4 %collective-permute-start.12 = (bf16[4,64,672]{2,1,0:T(8,128)(2,1)S(1)}, bf16[4,64,672]{2,1,0:T(8,128)(2,1)S(1)}, u32[]{:S(2)}, u32[]{:S(2)}) collective-permute-start(bf16[4,64,672]{2,1,0:T(8,128)(2,1)S(1)} %pad_maximum_fusion.1.refs_0_), channel_id=1, source_target_pairs={{0,4},{1,17},{2,6},{3,19},{4,0},{5,21},{6,2},{7,23},{8,12},{9,25},... | collective-permute-start | bytes 1032200 | tf_op jit(solution)/shard_map/gather_xy/ppermute | solution.py:33
  48.0 10.9 %collective-permute-start.13 = (bf16[4,64,672]{2,1,0:T(8,128)(2,1)S(1)}, bf16[4,64,672]{2,1,0:T(8,128)(2,1)S(1)}, u32[]{:S(2)}, u32[]{:S(2)}) collective-permute-start(bf16[4,64,672]{2,1,0:T(8,128)(2,1)S(1)} %pad_maximum_fusion.1.refs_0_), channel_id=1, source_target_pairs={{0,1},{1,0},{2,3},{3,2},{4,5},{5,4},{6,7},{7,6},{8,9},{9,8},{10,11... | collective-permute-start | bytes 1032200 | tf_op jit(solution)/shard_map/gather_xy/ppermute | solution.py:33
  58.4 1.7 %collective-permute-start.14 = (bf16[4,64,672]{2,1,0:T(8,128)(2,1)S(1)}, bf16[4,64,672]{2,1,0:T(8,128)(2,1)S(1)}, u32[]{:S(2)}, u32[]{:S(2)}) collective-permute-start(bf16[4,64,672]{2,1,0:T(8,128)(2,1)S(1)} %collective-permute-done.10.refs_1_), channel_id=1, source_target_pairs={{0,1},{1,0},{2,3},{3,2},{4,5},{5,4},{6,7},{7,6},{8,9},{9,8},{10,11... | collective-permute-start | bytes 1032200 | tf_op jit(solution)/shard_map/gather_xy/ppermute | solution.py:33
  58.4 2.3 %collective-permute-start.15 = (bf16[4,64,672]{2,1,0:T(8,128)(2,1)S(1)}, bf16[4,64,672]{2,1,0:T(8,128)(2,1)S(1)}, u32[]{:S(2)}, u32[]{:S(2)}) collective-permute-start(bf16[4,64,672]{2,1,0:T(8,128)(2,1)S(1)} %collective-permute-done.12.refs_2_), channel_id=1, source_target_pairs={{0,1},{1,0},{2,3},{3,2},{4,5},{5,4},{6,7},{7,6},{8,9},{9,8},{10,11... | collective-permute-start | bytes 1032200 | tf_op jit(solution)/shard_map/gather_xy/ppermute | solution.py:33
  58.9 2.3 %collective-permute-start.16 = (bf16[4,64,672]{2,1,0:T(8,128)(2,1)S(1)}, bf16[4,64,672]{2,1,0:T(8,128)(2,1)S(1)}, u32[]{:S(2)}, u32[]{:S(2)}) collective-permute-start(bf16[4,64,672]{2,1,0:T(8,128)(2,1)S(1)} %collective-permute-done.11.refs_3_), channel_id=1, source_target_pairs={{0,1},{1,0},{2,3},{3,2},{4,5},{5,4},{6,7},{7,6},{8,9},{9,8},{10,11... | collective-permute-start | bytes 1032200 | tf_op jit(solution)/shard_map/gather_xy/ppermute | solution.py:33
  90.9 3.5 %collective-permute-start.17 = (bf16[4,4,64,672]{3,2,1,0:T(8,128)(2,1)S(1)}, bf16[4,4,64,672]{3,2,1,0:T(8,128)(2,1)S(1)}, u32[]{:S(2)}, u32[]{:S(2)}) collective-permute-start(bf16[4,4,64,672]{3,2,1,0:T(8,128)(2,1)S(1)} %get-tuple-element.28), channel_id=1, source_target_pairs={{0,1},{1,0},{2,3},{3,2},{4,5},{5,4},{6,7},{7,6},{8,9},{9,8},{10,11... | collective-permute-start | bytes 4128776 | tf_op jit(solution)/shard_map/product/ppermute | solution.py:33
  94.7 11.7 %collective-permute-start.18 = (bf16[4,64,672]{2,1,0:T(8,128)(2,1)S(1)}, bf16[4,64,672]{2,1,0:T(8,128)(2,1)S(1)}, u32[]{:S(2)}, u32[]{:S(2)}) collective-permute-start(bf16[4,64,672]{2,1,0:T(8,128)(2,1)S(1)} %get-tuple-element.31), channel_id=1, source_target_pairs={{0,2},{1,9},{2,4},{3,11},{4,6},{5,13},{6,0},{7,15},{8,10},{9,17},{... | collective-permute-start | bytes 1032200 | tf_op jit(solution)/shard_map/scatter_xy/ppermute | solution.py:33
  96.8 13.2 %collective-permute-start.19 = (bf16[4,64,672]{2,1,0:T(8,128)(2,1)S(1)}, bf16[4,64,672]{2,1,0:T(8,128)(2,1)S(1)}, u32[]{:S(2)}, u32[]{:S(2)}) collective-permute-start(bf16[4,64,672]{2,1,0:T(8,128)(2,1)S(1)} %get-tuple-element.33), channel_id=1, source_target_pairs={{0,6},{1,25},{2,0},{3,27},{4,2},{5,29},{6,4},{7,31},{8,14},{9,1},{... | collective-permute-start | bytes 1032200 | tf_op jit(solution)/shard_map/scatter_xy/ppermute | solution.py:33
  96.8 13.2 %collective-permute-start.20 = (bf16[4,64,672]{2,1,0:T(8,128)(2,1)S(1)}, bf16[4,64,672]{2,1,0:T(8,128)(2,1)S(1)}, u32[]{:S(2)}, u32[]{:S(2)}) collective-permute-start(bf16[4,64,672]{2,1,0:T(8,128)(2,1)S(1)} %get-tuple-element.32), channel_id=1, source_target_pairs={{0,4},{1,17},{2,6},{3,19},{4,0},{5,21},{6,2},{7,23},{8,12},{9,25},... | collective-permute-start | bytes 1032200 | tf_op jit(solution)/shard_map/scatter_xy/ppermute | solution.py:33
  110.3 5.9 %collective-permute-start.21 = (bf16[64,672]{1,0:T(8,128)(2,1)S(1)}, bf16[64,672]{1,0:T(8,128)(2,1)S(1)}, u32[]{:S(2)}, u32[]{:S(2)}) collective-permute-start(bf16[64,672]{1,0:T(8,128)(2,1)S(1)} %get-tuple-element.34), channel_id=1, source_target_pairs={{0,8},{1,3},{2,10},{3,5},{4,12},{5,7},{6,14},{7,1},{8,16},{9,11},{... | collective-permute-start | bytes 258056 | tf_op jit(solution)/shard_map/scatter_yx/ppermute | solution.py:33
  110.5 6.3 %collective-permute-start.22 = (bf16[64,672]{1,0:T(8,128)(2,1)S(1)}, bf16[64,672]{1,0:T(8,128)(2,1)S(1)}, u32[]{:S(2)}, u32[]{:S(2)}) collective-permute-start(bf16[64,672]{1,0:T(8,128)(2,1)S(1)} %get-tuple-element.36), channel_id=1, source_target_pairs={{0,24},{1,7},{2,26},{3,1},{4,28},{5,3},{6,30},{7,5},{8,0},{9,15},{... | collective-permute-start | bytes 258056 | tf_op jit(solution)/shard_map/scatter_yx/ppermute | solution.py:33
  113.6 6.1 %collective-permute-start.23 = (bf16[64,672]{1,0:T(8,128)(2,1)S(1)}, bf16[64,672]{1,0:T(8,128)(2,1)S(1)}, u32[]{:S(2)}, u32[]{:S(2)}) collective-permute-start(bf16[64,672]{1,0:T(8,128)(2,1)S(1)} %get-tuple-element.35), channel_id=1, source_target_pairs={{0,16},{1,5},{2,18},{3,7},{4,20},{5,1},{6,22},{7,3},{8,24},{9,13},... | collective-permute-start | bytes 258056 | tf_op jit(solution)/shard_map/scatter_yx/ppermute | solution.py:33

commit v3 on v2

--- a/solution.py
+++ b/solution.py
@@ -58,56 +58,47 @@
     copy.wait()
 
 
-def times_weight(refs, out):
-    pieces = refs[: 2 * NQ]
-    w, held, whole = refs[2 * NQ :]
+def scores_kernel(*refs):
+    own, theirs = refs[:5], refs[5:10]
+    w, scores, slopes, stats, tops, held, whole = refs[10:]
     step = pl.program_id(0)
     rows = w.shape[0] // pl.num_programs(0)
-    tokens, width = out.shape[1], held.shape[-1]
+    tokens = scores.shape[1]
+    width = held.shape[-1]
 
     @pl.when(step == 0)
     def _():
         y, x, c = lax.axis_index("y"), lax.axis_index("x"), lax.axis_index("c")
-        for own in range(2):
-            parity = c if own == 0 else 1 - c
+        for pieces, parity in ((own, c), (theirs, 1 - c)):
             for k in range(NQ):
                 for r in range(NQ):
                     x_back = jnp.where(parity == 0, k, r)
                     y_back = jnp.where(parity == 0, r, k)
                     x_at = lax.rem(x + NQ - x_back, NQ)
                     y_at = lax.rem(y + NQ - y_back, NQ)
-                    held[2 * x_at + parity, y_at] = pieces[own * NQ + k][r]
+                    for half in range(2):
+                        piece = pieces[3 + half][r] if k == 2 else pieces[k % 3 + k // 3 * 2][half, r]
+                        held[2 * x_at + parity, half, y_at] = piece
         for t in range(2 * NQ):
-            whole[:, t * width : (t + 1) * width] = held[t].reshape(tokens, width)
+            whole[:, t * width : (t + 1) * width] = held[t].reshape(2 * tokens, width)
 
     at = pl.ds(pl.multiple_of(step * rows, rows), rows)
-    out[at, :] = lax.dot_general(
+    both = lax.dot_general(
         w[at, :], whole[...], (((1,), (1,)), ((), ())), preferred_element_type=F32
     )
-
-
-def scores_kernel(*refs):
-    raised, stats = refs[-4:-2]
-    times_weight((*refs[:-4], *refs[-2:]), raised)
-
-    @pl.when(pl.program_id(0) == pl.num_programs(0) - 1)
+    scores[at, :] = both[:, :tokens]
+    slopes[at, :] = both[:, tokens:]
+
+    @pl.when(step == pl.num_programs(0) - 1)
     def _():
-        top = jnp.max(raised[...], axis=0, keepdims=True)
-        value = jnp.exp(raised[...] - top)
-        raised[...] = value
-        total = jnp.sum(value, axis=0, keepdims=True)
-        stats[...] = jnp.concatenate((top, total, total, total), 0)
-
-
-def slopes_kernel(raised, top, *refs):
-    slopes, stats = refs[-4:-2]
-    times_weight((*refs[:-4], *refs[-2:]), slopes)
-
-    @pl.when(pl.program_id(0) == pl.num_programs(0) - 1)
-    def _():
-        dotted = jnp.sum(raised[...] * slopes[...], axis=0, keepdims=True)
-        own = jnp.concatenate((top[0:2, :], dotted, dotted), 0)
-        stats[...] = jnp.broadcast_to(own[None], stats.shape)
+        top = jnp.max(scores[...], axis=0, keepdims=True)
+        raised = jnp.exp(scores[...] - top)
+        scores[...] = raised
+        total = jnp.sum(raised, axis=0, keepdims=True)
+        dotted = jnp.sum(raised * slopes[...], axis=0, keepdims=True)
+        own_stats = jnp.concatenate((top, total, dotted, dotted), 0)
+        stats[...] = jnp.broadcast_to(own_stats[None], stats.shape)
+        tops[...] = jnp.broadcast_to(top, tops.shape)
 
 
 def merged(parts):
@@ -174,7 +165,7 @@
         pieces = {0: block}
         for k in HOPS:
             pieces[k] = send(block, along_yx(k))
-        blocks = [jnp.stack([pieces[k][i] for k in range(NQ)]) for i in range(2)]
+        block = jnp.stack([pieces[k] for k in range(NQ)], 1)
         weight = pl.pallas_call(
             load_kernel,
             out_shape=pltpu.VMEM((vocab, features), BF),
@@ -185,52 +176,38 @@
                 flops=0, transcendentals=0, bytes_accessed=4 * vocab * features
             ),
             compiler_params=pltpu.CompilerParams(vmem_limit_bytes=MIB),
-        )(pltpu.with_memory_space_constraint(out_weight, pltpu.HBM), blocks[0])
+        )(pltpu.with_memory_space_constraint(out_weight, pltpu.HBM), block)
     with jax.named_scope("gather_xy"):
-        mine, theirs = [], []
-        for block in blocks:
-            mine.append({0: block})
-            for k in HOPS:
-                mine[-1][k] = send(block, along_xy(k))
-        mine[0][0], weight = lax.optimization_barrier((mine[0][0], weight))
-        theirs.append({k: send(mine[0][k], other_core) for k in (0,) + HOPS})
-        inputs = [[*(mine[0][k] for k in range(NQ)), *(theirs[0][k] for k in range(NQ))]]
+        behind, ahead = send(block, along_xy(1)), send(block, along_xy(3))
+        held, weight = lax.optimization_barrier((block, weight))
+        own = [held, behind, ahead, send(behind[0], along_xy(1)), send(ahead[1], along_xy(3))]
+        theirs = [send(piece, other_core) for piece in own]
 
     steps = 4
     at_once = lambda *n: pl.BlockSpec(n, lambda i: (0,) * len(n))
-    scratch = [
-        pltpu.VMEM((2 * NQ, NQ, rows * NZ, width), BF),
-        pltpu.VMEM((tokens, features), BF),
-    ]
     with jax.named_scope("scores"):
-        raised, top = pl.pallas_call(
+        raised, slopes, stats, top = pl.pallas_call(
             scores_kernel,
             grid=(steps,),
-            out_shape=(shape((vocab, tokens), F32), shape((4, tokens), F32)),
-            in_specs=[VMEM] * (2 * NQ + 1),
-            out_specs=(at_once(vocab, tokens), at_once(4, tokens)),
-            scratch_shapes=scratch,
-            cost_estimate=pl.CostEstimate(flops=0, transcendentals=0, bytes_accessed=0),
-            compiler_params=pltpu.CompilerParams(vmem_limit_bytes=24 * MIB),
-        )(*inputs[0], weight)
-    with jax.named_scope("gather_xy"):
-        theirs.append({0: send(mine[1][0], other_core)})
-        held = lax.optimization_barrier((raised, *(mine[1][k] for k in HOPS)))
-        raised = held[0]
-        for k, piece in zip(HOPS, held[1:]):
-            mine[1][k] = piece
-            theirs[1][k] = send(piece, other_core)
-        inputs.append([*(mine[1][k] for k in range(NQ)), *(theirs[1][k] for k in range(NQ))])
-    with jax.named_scope("slopes"):
-        slopes, stats = pl.pallas_call(
-            slopes_kernel,
-            grid=(steps,),
-            out_shape=(shape((vocab, tokens), F32), shape((2 * NQ, 4, tokens), F32)),
-            in_specs=[VMEM] * (2 * NQ + 3),
-            out_specs=(at_once(vocab, tokens), at_once(2 * NQ, 4, tokens)),
-            scratch_shapes=scratch,
-            compiler_params=pltpu.CompilerParams(vmem_limit_bytes=24 * MIB),
-        )(raised, top, *inputs[1], weight)
+            out_shape=(
+                shape((vocab, tokens), F32),
+                shape((vocab, tokens), F32),
+                shape((2 * NQ, 4, tokens), F32),
+                shape((4, tokens), F32),
+            ),
+            in_specs=[VMEM] * 11,
+            out_specs=(
+                at_once(vocab, tokens),
+                at_once(vocab, tokens),
+                at_once(2 * NQ, 4, tokens),
+                at_once(4, tokens),
+            ),
+            scratch_shapes=[
+                pltpu.VMEM((2 * NQ, 2, NQ, rows * NZ, width), BF),
+                pltpu.VMEM((2 * tokens, features), BF),
+            ],
+            compiler_params=pltpu.CompilerParams(vmem_limit_bytes=20 * MIB),
+        )(*own, *theirs, weight)
 
     with jax.named_scope("statistics"):
         stats = pl.pallas_call(
@@ -251,7 +228,7 @@
             ),
             in_specs=[VMEM] * 5,
             out_specs=(VMEM, VMEM),
-            compiler_params=pltpu.CompilerParams(vmem_limit_bytes=16 * MIB),
+            compiler_params=pltpu.CompilerParams(vmem_limit_bytes=8 * MIB),
         )(parts, top, raised, slopes, weight)
         got = send(give, other_core)
         keep = pl.pallas_call(
@@ -264,7 +241,7 @@
                 transcendentals=0,
                 bytes_accessed=2 * vocab * features,
             ),
-            compiler_params=pltpu.CompilerParams(vmem_limit_bytes=16 * MIB),
+            compiler_params=pltpu.CompilerParams(vmem_limit_bytes=8 * MIB),
         )(mixture, weight)
 
     with jax.named_scope("scatter_xy"):

time: 133 us -> 131 us (0.985)
  starting transfers between devices: 21.6 us -> 20 us
    pallas_call x1 -> x0, Pallas kernels: 4.87 us -> none  [per_device(): pl.pallas_call(slopes_kernel, grid=(steps,), out_shape=(shape((vocab, tok...]
    pallas_call x1, Pallas kernels: 4.91 us -> 8.58 us  [per_device(): pl.pallas_call(scores_kernel, grid=(steps,), out_shape=(shape((vocab, tok...]
    ppermute x24 -> x19, starting transfers between devices: 21.6 us -> 20 us  [send(): return lax.ppermute(value, AXES, perm(move))]
    ppermute x24 -> x19, waiting for transfers between devices: 37.1 us -> 37.7 us  [send(): return lax.ppermute(value, AXES, perm(move))]
  transfers between devices with their start and end apart: 24 -> 19, of which waited for: 15 -> 12; matrix products, arithmetic and copies ran while one was open for 0% -> 0% of each run, Pallas kernels for 8% -> 5%
where the time goes in v3:
time: 131 us; the launch traced here: 130 us
  blocking collectives  53.2 us (41%)
  waiting for transfers between devices  37.7 us (29%)
  starting transfers between devices  20 us (15%)
  Pallas kernels  16.9 us (13%)
  other arithmetic  2.07 us (2%)
    all_to_all x4, blocking collectives, all_of(): return lax.all_to_all(value, axes, 0, 0)  53.2 us
    ppermute x19, waiting for transfers between devices, send(): return lax.ppermute(value, AXES, perm(move))  37.7 us
    ppermute x19, starting transfers between devices, send(): return lax.ppermute(value, AXES, perm(move))  20 us
    pallas_call x1, Pallas kernels, per_device(): pl.pallas_call(scores_kernel, grid=(steps,), out_shape=(shape((vocab, tok...  8.58 us
    pallas_call x1, Pallas kernels, per_device(): pl.pallas_call(load_kernel, out_shape=pltpu.VMEM((vocab, features), BF),...  4.14 us
  transfers between devices with their start and end apart: 19, of which 12 were waited for; matrix products, arithmetic and copies ran while one was open for 0% of the time, Pallas kernels for 5%

profile of v3, /device:TPU:6, one launch (start us, length us, event | category | flops | bytes accessed | tf_op | source)
XLA Modules:
  0.0 130.2 jit_solution(8971456810871167940)
XLA Ops:
  0.0 0.7 pad_maximum_fusion.1
  0.8 18.7 %all_to_all.20 = bf16[8,2,8,672]{3,2,1,0:T(8,128)(2,1)S(1)} all-to-all(bf16[8,2,8,672]{3,2,1,0:T(8,128)(2,1)S(1)} %broadcast_in_dim.2), channel_id=1, replica_groups=mesh['z'=8,'y'=4,'x'=4,'c'=2] {'z'}, dimensions={0} | all-to-all | bytes 344064 | tf_op jit(solution)/shard_map/gather_z/all_to_all | solution.py:52
  19.5 3.1 %collective-permute-start.2 = (bf16[2,64,672]{2,1,0:T(8,128)(2,1)S(1)}, bf16[2,64,672]{2,1,0:T(8,128)(2,1)S(1)}, u32[]{:S(2)}, u32[]{:S(2)}) collective-permute-start(bf16[2,64,672]{2,1,0:T(8,128)(2,1)S(1)} %get-tuple-element.30), channel_id=1, source_target_pairs={{0,24},{1,7},{2,26},{3,1},{4,28},{5,3},{6,30},{7,5},{8,0},{9,15},{... | collective-permute-start | bytes 516104 | tf_op jit(solution)/shard_map/gather_yx/ppermute | solution.py:33
  22.6 0.6 collective-permute-start.1
  23.2 1.0 collective-permute-start
  24.2 3.7 %collective-permute-done.2 = bf16[2,64,672]{2,1,0:T(8,128)(2,1)S(1)} collective-permute-done((bf16[2,64,672]{2,1,0:T(8,128)(2,1)S(1)}, bf16[2,64,672]{2,1,0:T(8,128)(2,1)S(1)}, u32[]{:S(2)}, u32[]{:S(2)}) %collective-permute-start.2) | collective-permute-done | bytes 172064 | tf_op jit(solution)/shard_map/gather_yx/ppermute | solution.py:33
  27.9 1.9 %collective-permute-done.1 = bf16[2,64,672]{2,1,0:T(8,128)(2,1)S(1)} collective-permute-done((bf16[2,64,672]{2,1,0:T(8,128)(2,1)S(1)}, bf16[2,64,672]{2,1,0:T(8,128)(2,1)S(1)}, u32[]{:S(2)}, u32[]{:S(2)}) %collective-permute-start.1) | collective-permute-done | bytes 172064 | tf_op jit(solution)/shard_map/gather_yx/ppermute | solution.py:33
  29.9 2.0 %collective-permute-done = bf16[2,64,672]{2,1,0:T(8,128)(2,1)S(1)} collective-permute-done((bf16[2,64,672]{2,1,0:T(8,128)(2,1)S(1)}, bf16[2,64,672]{2,1,0:T(8,128)(2,1)S(1)}, u32[]{:S(2)}, u32[]{:S(2)}) %collective-permute-start) | collective-permute-done | bytes 172064 | tf_op jit(solution)/shard_map/gather_yx/ppermute | solution.py:33
  31.9 0.1 pad_maximum_fusion._.refs_0_
  32.0 0.9 collective-permute-start.4
  32.9 2.4 %collective-permute-start.3 = (bf16[2,4,64,672]{3,2,1,0:T(8,128)(2,1)S(1)}, bf16[2,4,64,672]{3,2,1,0:T(8,128)(2,1)S(1)}, u32[]{:S(2)}, u32[]{:S(2)}) collective-permute-start(bf16[2,4,64,672]{3,2,1,0:T(8,128)(2,1)S(1)} %pad_maximum_fusion._.refs_0_), channel_id=1, source_target_pairs={{0,2},{1,9},{2,4},{3,11},{4,6},{5,13},{6,0},{7,15},{8,10},{9,17},{... | collective-permute-start | bytes 2064392 | tf_op jit(solution)/shard_map/gather_xy/ppermute | solution.py:33
  35.3 4.1 %gather_yx.1.refs_10_.w = bf16[1024,5376]{1,0:T(8,128)(2,1)S(1)} custom-call(bf16[1024,5376]{1,0:T(8,128)(2,1)} %w.1, bf16[2,4,64,672]{3,2,1,0:T(8,128)(2,1)S(1)} %pad_maximum_fusion._.refs_0_), custom_call_target="tpu_custom_call" | custom-call | bytes 22020096 | tf_op jit(solution)/shard_map/gather_yx/pallas_call | solution.py:169
  39.5 0.1 collective-permute-start.7
  39.6 5.7 %collective-permute-done.4.refs_2_ = bf16[2,4,64,672]{3,2,1,0:T(8,128)(2,1)S(1)} collective-permute-done((bf16[2,4,64,672]{3,2,1,0:T(8,128)(2,1)S(1)}, bf16[2,4,64,672]{3,2,1,0:T(8,128)(2,1)S(1)}, u32[]{:S(2)}, u32[]{:S(2)}) %collective-permute-start.4) | collective-permute-done | bytes 688160 | tf_op jit(solution)/shard_map/gather_xy/ppermute | solution.py:33
  45.3 0.1 collective-permute-start.6
  45.4 0.0 collective-permute-done.3.refs_1_
  45.4 3.3 %collective-permute-start.5 = (bf16[4,64,672]{2,1,0:T(8,128)(2,1)S(1)}, bf16[4,64,672]{2,1,0:T(8,128)(2,1)S(1)}, u32[]{:S(2)}, u32[]{:S(2)}) collective-permute-start(bf16[4,64,672]{2,1,0:T(8,128)(2,1)S(1)} %slice_bitcast_fusion.1), channel_id=1, source_target_pairs={{0,2},{1,9},{2,4},{3,11},{4,6},{5,13},{6,0},{7,15},{8,10},{9,17},{... | collective-permute-start | bytes 1032200 | tf_op jit(solution)/shard_map/gather_xy/ppermute | solution.py:33
  48.7 0.0 collective-permute-start.9
  48.7 0.5 collective-permute-start.8
  49.2 5.1 %collective-permute-done.6.refs_4_ = bf16[4,64,672]{2,1,0:T(8,128)(2,1)S(1)} collective-permute-done((bf16[4,64,672]{2,1,0:T(8,128)(2,1)S(1)}, bf16[4,64,672]{2,1,0:T(8,128)(2,1)S(1)}, u32[]{:S(2)}, u32[]{:S(2)}) %collective-permute-start.6) | collective-permute-done | bytes 344096 | tf_op jit(solution)/shard_map/gather_xy/ppermute | solution.py:33
  54.4 0.0 collective-permute-start.11
  54.4 0.0 collective-permute-done.5.refs_3_
  54.4 0.5 collective-permute-start.10
  54.9 0.0 collective-permute-done.7.refs_5_
  54.9 1.2 collective-permute-done.11.refs_9_
  56.1 0.0 collective-permute-done.9.refs_7_
  56.1 0.6 collective-permute-done.10.refs_8_
  56.7 0.0 collective-permute-done.8.refs_6_
  56.7 8.6 %scores.1 = (f32[1024,256]{1,0:T(8,128)S(1)}, f32[1024,256]{1,0:T(8,128)S(1)}, f32[8,4,256]{2,1,0:T(4,128)S(1)}, f32[4,256]{1,0:T(4,128)S(1)}) custom-call(bf16[2,4,64,672]{3,2,1,0:T(8,128)(2,1)S(1)} %pad_maximum_fusion._.refs_0_, bf16[2,4,64,672]{3,2,1,0:T(8,128)(2,1)S(1)} %collective-permute-done.3.refs_1_, ...), custom_call_target="tpu_custom_call" | custom-call | tf_op jit(solution)/shard_map/scores/pallas_call | solution.py:189
  65.3 8.5 %all_to_all.21.parts = f32[8,4,256]{2,1,0:T(4,128)S(1)} all-to-all(f32[8,4,256]{2,1,0:T(4,128)S(1)} %get-tuple-element.15), channel_id=1, replica_groups=mesh['z'=8,'y'=4,'x'=4,'c'=2] {'x','c'}, dimensions={0} | all-to-all | bytes 65536 | tf_op jit(solution)/shard_map/statistics/all_to_all | solution.py:52
  73.8 13.7 %all_to_all.22.parts = f32[32,4,256]{2,1,0:T(4,128)S(1)} all-to-all(f32[32,4,256]{2,1,0:T(4,128)S(1)} %statistics.1), channel_id=1, replica_groups=mesh['z'=8,'y'=4,'x'=4,'c'=2] {'z','y'}, dimensions={0} | all-to-all | bytes 262144 | tf_op jit(solution)/shard_map/statistics/all_to_all | solution.py:52
  87.6 2.2 %product.2 = (bf16[4,4,64,672]{3,2,1,0:T(8,128)(2,1)S(1)}, bf16[256,1024]{1,0:T(8,128)(2,1)S(1)}) custom-call(f32[32,4,256]{2,1,0:T(4,128)S(1)} %all_to_all.22.parts, f32[4,256]{1,0:T(4,128)S(1)} %get-tuple-element.16.own_top, f32[1024,256]{1,0:T(8,128)S(1)} %get-tuple-element.17.raised, f32[1024,256]{1,0:T(8,128)S(1)} %get-tuple-element.18.slopes, ...), custom_call_target="tpu_custom_call" | custom-call | tf_op jit(solution)/shard_map/product/pallas_call | solution.py:223
  89.8 0.1 collective-permute-start.12
  89.9 2.0 %product.3 = f32[4,4,64,672]{3,2,1,0:T(8,128)S(1)} custom-call(bf16[256,1024]{1,0:T(8,128)(2,1)S(1)} %get-tuple-element.19.mixture, bf16[1024,5376]{1,0:T(8,128)(2,1)S(1)} %gather_yx.1.refs_10_.w), custom_call_target="tpu_custom_call" | custom-call | flops 1409286144 | bytes 11010048 | tf_op jit(solution)/shard_map/product/pallas_call | solution.py:234
  91.9 1.4 %collective-permute-done.12 = bf16[4,4,64,672]{3,2,1,0:T(8,128)(2,1)S(1)} collective-permute-done((bf16[4,4,64,672]{3,2,1,0:T(8,128)(2,1)S(1)}, bf16[4,4,64,672]{3,2,1,0:T(8,128)(2,1)S(1)}, u32[]{:S(2)}, u32[]{:S(2)}) %collective-permute-start.12) | collective-permute-done | bytes 1376288 | tf_op jit(solution)/shard_map/product/ppermute | solution.py:33
  93.3 0.3 fusion.7
  93.6 2.1 %collective-permute-start.13 = (bf16[4,64,672]{2,1,0:T(8,128)(2,1)S(1)}, bf16[4,64,672]{2,1,0:T(8,128)(2,1)S(1)}, u32[]{:S(2)}, u32[]{:S(2)}) collective-permute-start(bf16[4,64,672]{2,1,0:T(8,128)(2,1)S(1)} %get-tuple-element.23), channel_id=1, source_target_pairs={{0,2},{1,9},{2,4},{3,11},{4,6},{5,13},{6,0},{7,15},{8,10},{9,17},{... | collective-permute-start | bytes 1032200 | tf_op jit(solution)/shard_map/scatter_xy/ppermute | solution.py:33
  95.7 0.5 collective-permute-start.15
  96.2 0.9 collective-permute-start.14
  97.2 8.1 %collective-permute-done.13 = bf16[4,64,672]{2,1,0:T(8,128)(2,1)S(1)} collective-permute-done((bf16[4,64,672]{2,1,0:T(8,128)(2,1)S(1)}, bf16[4,64,672]{2,1,0:T(8,128)(2,1)S(1)}, u32[]{:S(2)}, u32[]{:S(2)}) %collective-permute-start.13) | collective-permute-done | bytes 344096 | tf_op jit(solution)/shard_map/scatter_xy/ppermute | solution.py:33
  105.3 0.0 collective-permute-done.15
  105.3 3.9 %collective-permute-done.14 = bf16[4,64,672]{2,1,0:T(8,128)(2,1)S(1)} collective-permute-done((bf16[4,64,672]{2,1,0:T(8,128)(2,1)S(1)}, bf16[4,64,672]{2,1,0:T(8,128)(2,1)S(1)}, u32[]{:S(2)}, u32[]{:S(2)}) %collective-permute-start.14) | collective-permute-done | bytes 344096 | tf_op jit(solution)/shard_map/scatter_xy/ppermute | solution.py:33
  109.2 0.2 fusion.14
  109.5 0.1 collective-permute-start.16
  109.6 2.7 %collective-permute-start.18 = (bf16[64,672]{1,0:T(8,128)(2,1)S(1)}, bf16[64,672]{1,0:T(8,128)(2,1)S(1)}, u32[]{:S(2)}, u32[]{:S(2)}) collective-permute-start(bf16[64,672]{1,0:T(8,128)(2,1)S(1)} %get-tuple-element.27), channel_id=1, source_target_pairs={{0,16},{1,5},{2,18},{3,7},{4,20},{5,1},{6,22},{7,3},{8,24},{9,13},... | collective-permute-start | bytes 258056 | tf_op jit(solution)/shard_map/scatter_yx/ppermute | solution.py:33
  112.3 1.0 collective-permute-start.17
  113.3 3.1 %collective-permute-done.16 = bf16[64,672]{1,0:T(8,128)(2,1)S(1)} collective-permute-done((bf16[64,672]{1,0:T(8,128)(2,1)S(1)}, bf16[64,672]{1,0:T(8,128)(2,1)S(1)}, u32[]{:S(2)}, u32[]{:S(2)}) %collective-permute-start.16) | collective-permute-done | bytes 86048 | tf_op jit(solution)/shard_map/scatter_yx/ppermute | solution.py:33
  116.5 0.0 collective-permute-done.18
  116.5 0.9 collective-permute-done.17
  117.4 12.2 %all_to_all.23 = f32[8,8,672]{2,1,0:T(8,128)S(1)} all-to-all(f32[8,8,672]{2,1,0:T(8,128)S(1)} %fusion.13), channel_id=1, replica_groups=mesh['z'=8,'y'=4,'x'=4,'c'=2] {'z'}, dimensions={0} | all-to-all | bytes 344064 | tf_op jit(solution)/shard_map/scatter_z/all_to_all | solution.py:52
  129.5 0.6 reduce_sum.9
  (7 shorter events, 0.2 us)
Async XLA Ops:
  19.5 8.4 %collective-permute-start.2 = (bf16[2,64,672]{2,1,0:T(8,128)(2,1)S(1)}, bf16[2,64,672]{2,1,0:T(8,128)(2,1)S(1)}, u32[]{:S(2)}, u32[]{:S(2)}) collective-permute-start(bf16[2,64,672]{2,1,0:T(8,128)(2,1)S(1)} %get-tuple-element.30), channel_id=1, source_target_pairs={{0,24},{1,7},{2,26},{3,1},{4,28},{5,3},{6,30},{7,5},{8,0},{9,15},{... | collective-permute-start | bytes 516104 | tf_op jit(solution)/shard_map/gather_yx/ppermute | solution.py:33
  22.6 7.3 %collective-permute-start.1 = (bf16[2,64,672]{2,1,0:T(8,128)(2,1)S(1)}, bf16[2,64,672]{2,1,0:T(8,128)(2,1)S(1)}, u32[]{:S(2)}, u32[]{:S(2)}) collective-permute-start(bf16[2,64,672]{2,1,0:T(8,128)(2,1)S(1)} %get-tuple-element.30), channel_id=1, source_target_pairs={{0,16},{1,5},{2,18},{3,7},{4,20},{5,1},{6,22},{7,3},{8,24},{9,13},... | collective-permute-start | bytes 516104 | tf_op jit(solution)/shard_map/gather_yx/ppermute | solution.py:33
  23.2 8.7 %collective-permute-start = (bf16[2,64,672]{2,1,0:T(8,128)(2,1)S(1)}, bf16[2,64,672]{2,1,0:T(8,128)(2,1)S(1)}, u32[]{:S(2)}, u32[]{:S(2)}) collective-permute-start(bf16[2,64,672]{2,1,0:T(8,128)(2,1)S(1)} %get-tuple-element.30), channel_id=1, source_target_pairs={{0,8},{1,3},{2,10},{3,5},{4,12},{5,7},{6,14},{7,1},{8,16},{9,11},{... | collective-permute-start | bytes 516104 | tf_op jit(solution)/shard_map/gather_yx/ppermute | solution.py:33
  32.0 13.3 %collective-permute-start.4 = (bf16[2,4,64,672]{3,2,1,0:T(8,128)(2,1)S(1)}, bf16[2,4,64,672]{3,2,1,0:T(8,128)(2,1)S(1)}, u32[]{:S(2)}, u32[]{:S(2)}) collective-permute-start(bf16[2,4,64,672]{3,2,1,0:T(8,128)(2,1)S(1)} %pad_maximum_fusion._.refs_0_), channel_id=1, source_target_pairs={{0,6},{1,25},{2,0},{3,27},{4,2},{5,29},{6,4},{7,31},{8,14},{9,1},{... | collective-permute-start | bytes 2064392 | tf_op jit(solution)/shard_map/gather_xy/ppermute | solution.py:33
  32.9 12.5 %collective-permute-start.3 = (bf16[2,4,64,672]{3,2,1,0:T(8,128)(2,1)S(1)}, bf16[2,4,64,672]{3,2,1,0:T(8,128)(2,1)S(1)}, u32[]{:S(2)}, u32[]{:S(2)}) collective-permute-start(bf16[2,4,64,672]{3,2,1,0:T(8,128)(2,1)S(1)} %pad_maximum_fusion._.refs_0_), channel_id=1, source_target_pairs={{0,2},{1,9},{2,4},{3,11},{4,6},{5,13},{6,0},{7,15},{8,10},{9,17},{... | collective-permute-start | bytes 2064392 | tf_op jit(solution)/shard_map/gather_xy/ppermute | solution.py:33
  39.5 15.4 %collective-permute-start.7 = (bf16[2,4,64,672]{3,2,1,0:T(8,128)(2,1)S(1)}, bf16[2,4,64,672]{3,2,1,0:T(8,128)(2,1)S(1)}, u32[]{:S(2)}, u32[]{:S(2)}) collective-permute-start(bf16[2,4,64,672]{3,2,1,0:T(8,128)(2,1)S(1)} %pad_maximum_fusion._.refs_0_), channel_id=1, source_target_pairs={{0,1},{1,0},{2,3},{3,2},{4,5},{5,4},{6,7},{7,6},{8,9},{9,8},{10,11... | collective-permute-start | bytes 2064392 | tf_op jit(solution)/shard_map/gather_xy/ppermute | solution.py:33
  45.3 9.1 %collective-permute-start.6 = (bf16[4,64,672]{2,1,0:T(8,128)(2,1)S(1)}, bf16[4,64,672]{2,1,0:T(8,128)(2,1)S(1)}, u32[]{:S(2)}, u32[]{:S(2)}) collective-permute-start(bf16[4,64,672]{2,1,0:T(8,128)(2,1)S(1)} %slice_bitcast_fusion), channel_id=1, source_target_pairs={{0,6},{1,25},{2,0},{3,27},{4,2},{5,29},{6,4},{7,31},{8,14},{9,1},{... | collective-permute-start | bytes 1032200 | tf_op jit(solution)/shard_map/gather_xy/ppermute | solution.py:33
  45.4 8.9 %collective-permute-start.5 = (bf16[4,64,672]{2,1,0:T(8,128)(2,1)S(1)}, bf16[4,64,672]{2,1,0:T(8,128)(2,1)S(1)}, u32[]{:S(2)}, u32[]{:S(2)}) collective-permute-start(bf16[4,64,672]{2,1,0:T(8,128)(2,1)S(1)} %slice_bitcast_fusion.1), channel_id=1, source_target_pairs={{0,2},{1,9},{2,4},{3,11},{4,6},{5,13},{6,0},{7,15},{8,10},{9,17},{... | collective-permute-start | bytes 1032200 | tf_op jit(solution)/shard_map/gather_xy/ppermute | solution.py:33
  48.7 7.4 %collective-permute-start.9 = (bf16[2,4,64,672]{3,2,1,0:T(8,128)(2,1)S(1)}, bf16[2,4,64,672]{3,2,1,0:T(8,128)(2,1)S(1)}, u32[]{:S(2)}, u32[]{:S(2)}) collective-permute-start(bf16[2,4,64,672]{3,2,1,0:T(8,128)(2,1)S(1)} %collective-permute-done.4.refs_2_), channel_id=1, source_target_pairs={{0,1},{1,0},{2,3},{3,2},{4,5},{5,4},{6,7},{7,6},{8,9},{9,8},{10,11... | collective-permute-start | bytes 2064392 | tf_op jit(solution)/shard_map/gather_xy/ppermute | solution.py:33
  48.7 7.9 %collective-permute-start.8 = (bf16[2,4,64,672]{3,2,1,0:T(8,128)(2,1)S(1)}, bf16[2,4,64,672]{3,2,1,0:T(8,128)(2,1)S(1)}, u32[]{:S(2)}, u32[]{:S(2)}) collective-permute-start(bf16[2,4,64,672]{3,2,1,0:T(8,128)(2,1)S(1)} %collective-permute-done.3.refs_1_), channel_id=1, source_target_pairs={{0,1},{1,0},{2,3},{3,2},{4,5},{5,4},{6,7},{7,6},{8,9},{9,8},{10,11... | collective-permute-start | bytes 2064392 | tf_op jit(solution)/shard_map/gather_xy/ppermute | solution.py:33
  54.4 1.7 %collective-permute-start.11 = (bf16[4,64,672]{2,1,0:T(8,128)(2,1)S(1)}, bf16[4,64,672]{2,1,0:T(8,128)(2,1)S(1)}, u32[]{:S(2)}, u32[]{:S(2)}) collective-permute-start(bf16[4,64,672]{2,1,0:T(8,128)(2,1)S(1)} %collective-permute-done.6.refs_4_), channel_id=1, source_target_pairs={{0,1},{1,0},{2,3},{3,2},{4,5},{5,4},{6,7},{7,6},{8,9},{9,8},{10,11... | collective-permute-start | bytes 1032200 | tf_op jit(solution)/shard_map/gather_xy/ppermute | solution.py:33
  54.4 2.3 %collective-permute-start.10 = (bf16[4,64,672]{2,1,0:T(8,128)(2,1)S(1)}, bf16[4,64,672]{2,1,0:T(8,128)(2,1)S(1)}, u32[]{:S(2)}, u32[]{:S(2)}) collective-permute-start(bf16[4,64,672]{2,1,0:T(8,128)(2,1)S(1)} %collective-permute-done.5.refs_3_), channel_id=1, source_target_pairs={{0,1},{1,0},{2,3},{3,2},{4,5},{5,4},{6,7},{7,6},{8,9},{9,8},{10,11... | collective-permute-start | bytes 1032200 | tf_op jit(solution)/shard_map/gather_xy/ppermute | solution.py:33
  89.8 3.5 %collective-permute-start.12 = (bf16[4,4,64,672]{3,2,1,0:T(8,128)(2,1)S(1)}, bf16[4,4,64,672]{3,2,1,0:T(8,128)(2,1)S(1)}, u32[]{:S(2)}, u32[]{:S(2)}) collective-permute-start(bf16[4,4,64,672]{3,2,1,0:T(8,128)(2,1)S(1)} %get-tuple-element.20), channel_id=1, source_target_pairs={{0,1},{1,0},{2,3},{3,2},{4,5},{5,4},{6,7},{7,6},{8,9},{9,8},{10,11... | collective-permute-start | bytes 4128776 | tf_op jit(solution)/shard_map/product/ppermute | solution.py:33
  93.6 11.7 %collective-permute-start.13 = (bf16[4,64,672]{2,1,0:T(8,128)(2,1)S(1)}, bf16[4,64,672]{2,1,0:T(8,128)(2,1)S(1)}, u32[]{:S(2)}, u32[]{:S(2)}) collective-permute-start(bf16[4,64,672]{2,1,0:T(8,128)(2,1)S(1)} %get-tuple-element.23), channel_id=1, source_target_pairs={{0,2},{1,9},{2,4},{3,11},{4,6},{5,13},{6,0},{7,15},{8,10},{9,17},{... | collective-permute-start | bytes 1032200 | tf_op jit(solution)/shard_map/scatter_xy/ppermute | solution.py:33
  95.7 9.5 %collective-permute-start.15 = (bf16[4,64,672]{2,1,0:T(8,128)(2,1)S(1)}, bf16[4,64,672]{2,1,0:T(8,128)(2,1)S(1)}, u32[]{:S(2)}, u32[]{:S(2)}) collective-permute-start(bf16[4,64,672]{2,1,0:T(8,128)(2,1)S(1)} %get-tuple-element.24), channel_id=1, source_target_pairs={{0,4},{1,17},{2,6},{3,19},{4,0},{5,21},{6,2},{7,23},{8,12},{9,25},... | collective-permute-start | bytes 1032200 | tf_op jit(solution)/shard_map/scatter_xy/ppermute | solution.py:33
  96.2 13.0 %collective-permute-start.14 = (bf16[4,64,672]{2,1,0:T(8,128)(2,1)S(1)}, bf16[4,64,672]{2,1,0:T(8,128)(2,1)S(1)}, u32[]{:S(2)}, u32[]{:S(2)}) collective-permute-start(bf16[4,64,672]{2,1,0:T(8,128)(2,1)S(1)} %get-tuple-element.25), channel_id=1, source_target_pairs={{0,6},{1,25},{2,0},{3,27},{4,2},{5,29},{6,4},{7,31},{8,14},{9,1},{... | collective-permute-start | bytes 1032200 | tf_op jit(solution)/shard_map/scatter_xy/ppermute | solution.py:33
  109.5 7.0 %collective-permute-start.16 = (bf16[64,672]{1,0:T(8,128)(2,1)S(1)}, bf16[64,672]{1,0:T(8,128)(2,1)S(1)}, u32[]{:S(2)}, u32[]{:S(2)}) collective-permute-start(bf16[64,672]{1,0:T(8,128)(2,1)S(1)} %get-tuple-element.26), channel_id=1, source_target_pairs={{0,8},{1,3},{2,10},{3,5},{4,12},{5,7},{6,14},{7,1},{8,16},{9,11},{... | collective-permute-start | bytes 258056 | tf_op jit(solution)/shard_map/scatter_yx/ppermute | solution.py:33
  109.6 6.9 %collective-permute-start.18 = (bf16[64,672]{1,0:T(8,128)(2,1)S(1)}, bf16[64,672]{1,0:T(8,128)(2,1)S(1)}, u32[]{:S(2)}, u32[]{:S(2)}) collective-permute-start(bf16[64,672]{1,0:T(8,128)(2,1)S(1)} %get-tuple-element.27), channel_id=1, source_target_pairs={{0,16},{1,5},{2,18},{3,7},{4,20},{5,1},{6,22},{7,3},{8,24},{9,13},... | collective-permute-start | bytes 258056 | tf_op jit(solution)/shard_map/scatter_yx/ppermute | solution.py:33
  112.3 5.0 %collective-permute-start.17 = (bf16[64,672]{1,0:T(8,128)(2,1)S(1)}, bf16[64,672]{1,0:T(8,128)(2,1)S(1)}, u32[]{:S(2)}, u32[]{:S(2)}) collective-permute-start(bf16[64,672]{1,0:T(8,128)(2,1)S(1)} %get-tuple-element.28), channel_id=1, source_target_pairs={{0,24},{1,7},{2,26},{3,1},{4,28},{5,3},{6,30},{7,5},{8,0},{9,15},{... | collective-permute-start | bytes 258056 | tf_op jit(solution)/shard_map/scatter_yx/ppermute | solution.py:33

commit v4 on v3

--- a/solution.py
+++ b/solution.py
@@ -52,6 +52,12 @@
     return lax.all_to_all(value, axes, 0, 0)
 
 
+def turn_kernel(block, out):
+    both = block[...].astype(F32)
+    rows = [both[:, i].reshape(-1, both.shape[-1]) for i in range(2)]
+    out[...] = jnp.concatenate(rows, 0).T.astype(BF)
+
+
 def load_kernel(w, _, out, sem):
     copy = pltpu.make_async_copy(w, out, sem)
     copy.start()
@@ -60,11 +66,10 @@
 
 def scores_kernel(*refs):
     own, theirs = refs[:5], refs[5:10]
-    w, scores, slopes, stats, tops, held, whole = refs[10:]
+    w, scores, slopes, stats, tops, whole = refs[10:]
     step = pl.program_id(0)
     rows = w.shape[0] // pl.num_programs(0)
-    tokens = scores.shape[1]
-    width = held.shape[-1]
+    width, lanes = own[0].shape[1:]
 
     @pl.when(step == 0)
     def _():
@@ -76,18 +81,23 @@
                     y_back = jnp.where(parity == 0, r, k)
                     x_at = lax.rem(x + NQ - x_back, NQ)
                     y_at = lax.rem(y + NQ - y_back, NQ)
-                    for half in range(2):
-                        piece = pieces[3 + half][r] if k == 2 else pieces[k % 3 + k // 3 * 2][half, r]
-                        held[2 * x_at + parity, half, y_at] = piece
-        for t in range(2 * NQ):
-            whole[:, t * width : (t + 1) * width] = held[t].reshape(2 * tokens, width)
+                    if k == 2:
+                        piece = pieces[3 + r // 2][r % 2]
+                    else:
+                        piece = pieces[k % 3 + k // 3 * 2][r]
+                    first = pl.multiple_of((2 * x_at + parity) * width, width)
+                    column = pl.multiple_of(y_at * lanes, lanes)
+                    whole[pl.ds(first, width), pl.ds(column, lanes)] = piece
 
     at = pl.ds(pl.multiple_of(step * rows, rows), rows)
-    both = lax.dot_general(
-        w[at, :], whole[...], (((1,), (1,)), ((), ())), preferred_element_type=F32
-    )
-    scores[at, :] = both[:, :tokens]
-    slopes[at, :] = both[:, tokens:]
+    both = jnp.dot(w[at, :], whole[...], preferred_element_type=F32)
+    low = lax.broadcasted_iota(jnp.int32, (rows, lanes), 1) < lanes // 2
+    for pair in range(NQ // 2):
+        first = both[:, 2 * pair * lanes : (2 * pair + 1) * lanes]
+        second = both[:, (2 * pair + 1) * lanes : (2 * pair + 2) * lanes]
+        columns = slice(pair * lanes, (pair + 1) * lanes)
+        scores[at, columns] = jnp.where(low, first, pltpu.roll(second, lanes // 2, 1))
+        slopes[at, columns] = jnp.where(low, pltpu.roll(first, lanes // 2, 1), second)
 
     @pl.when(step == pl.num_programs(0) - 1)
     def _():
@@ -160,12 +170,18 @@
     with jax.named_scope("gather_z"):
         own = jnp.stack((hidden, tangent))
         block = all_of(jnp.broadcast_to(own[None], (NZ, *own.shape)), "z")
-        block = block.transpose(1, 0, 2, 3).reshape(2, rows * NZ, width)
+        block = pl.pallas_call(
+            turn_kernel,
+            out_shape=shape((width, 2 * rows * NZ), BF),
+            in_specs=[VMEM],
+            out_specs=VMEM,
+            compiler_params=pltpu.CompilerParams(vmem_limit_bytes=4 * MIB),
+        )(block)
     with jax.named_scope("gather_yx"):
         pieces = {0: block}
         for k in HOPS:
             pieces[k] = send(block, along_yx(k))
-        block = jnp.stack([pieces[k] for k in range(NQ)], 1)
+        block = jnp.stack([pieces[k] for k in range(NQ)])
         weight = pl.pallas_call(
             load_kernel,
             out_shape=pltpu.VMEM((vocab, features), BF),
@@ -180,7 +196,7 @@
     with jax.named_scope("gather_xy"):
         behind, ahead = send(block, along_xy(1)), send(block, along_xy(3))
         held, weight = lax.optimization_barrier((block, weight))
-        own = [held, behind, ahead, send(behind[0], along_xy(1)), send(ahead[1], along_xy(3))]
+        own = [held, behind, ahead, send(behind[:2], along_xy(1)), send(ahead[2:], along_xy(3))]
         theirs = [send(piece, other_core) for piece in own]
 
     steps = 4
@@ -203,8 +219,7 @@
                 at_once(4, tokens),
             ),
             scratch_shapes=[
-                pltpu.VMEM((2 * NQ, 2, NQ, rows * NZ, width), BF),
-                pltpu.VMEM((2 * tokens, features), BF),
+                pltpu.VMEM((features, 2 * tokens), BF),
             ],
             compiler_params=pltpu.CompilerParams(vmem_limit_bytes=20 * MIB),
         )(*own, *theirs, weight)

time: 131 us -> 128 us (0.977)
  waiting for transfers between devices: 37.7 us -> 35.5 us
    ppermute x19, waiting for transfers between devices: 37.7 us -> 35.5 us  [send(): return lax.ppermute(value, AXES, perm(move))]
where the time goes in v4:
time: 128 us
  blocking collectives  53.2 us (42%)
  waiting for transfers between devices  35.5 us (28%)
  starting transfers between devices  20 us (16%)
  Pallas kernels  17 us (13%)
  other arithmetic  2.05 us (2%)
    all_to_all x4, blocking collectives, all_of(): return lax.all_to_all(value, axes, 0, 0)  53.2 us
    ppermute x19, waiting for transfers between devices, send(): return lax.ppermute(value, AXES, perm(move))  35.5 us
    ppermute x19, starting transfers between devices, send(): return lax.ppermute(value, AXES, perm(move))  20 us
    pallas_call x1, Pallas kernels, per_device(): pl.pallas_call(scores_kernel, grid=(steps,), out_shape=(shape((vocab, tok...  8.35 us
    pallas_call x1, Pallas kernels, per_device(): pl.pallas_call(load_kernel, out_shape=pltpu.VMEM((vocab, features), BF),...  4.14 us
  transfers between devices with their start and end apart: 19, of which 12 were waited for; matrix products, arithmetic and copies ran while one was open for 0% of the time, Pallas kernels for 5%

profile of v4, /device:TPU:6, one launch (start us, length us, event | category | flops | bytes accessed | tf_op | source)
XLA Modules:
  0.0 128.0 jit_solution(16091437119135320737)
XLA Ops:
  0.0 0.7 pad_maximum_fusion.1
  0.8 18.7 %all_to_all.20.block = bf16[8,2,8,672]{3,2,1,0:T(8,128)(2,1)S(1)} all-to-all(bf16[8,2,8,672]{3,2,1,0:T(8,128)(2,1)S(1)} %broadcast_in_dim.2), channel_id=1, replica_groups=mesh['z'=8,'y'=4,'x'=4,'c'=2] {'z'}, dimensions={0} | all-to-all | bytes 344064 | tf_op jit(solution)/shard_map/gather_z/all_to_all | solution.py:52
  19.5 0.1 gather_z.1
  19.6 3.1 %collective-permute-start.2 = (bf16[672,128]{1,0:T(8,128)(2,1)S(1)}, bf16[672,128]{1,0:T(8,128)(2,1)S(1)}, u32[]{:S(2)}, u32[]{:S(2)}) collective-permute-start(bf16[672,128]{1,0:T(8,128)(2,1)S(1)} %gather_z.1), channel_id=1, source_target_pairs={{0,24},{1,7},{2,26},{3,1},{4,28},{5,3},{6,30},{7,5},{8,0},{9,15},{... | collective-permute-start | bytes 516104 | tf_op jit(solution)/shard_map/gather_yx/ppermute | solution.py:33
  22.7 0.6 collective-permute-start.1
  23.3 1.0 collective-permute-start
  24.3 3.2 %collective-permute-done.2 = bf16[672,128]{1,0:T(8,128)(2,1)S(1)} collective-permute-done((bf16[672,128]{1,0:T(8,128)(2,1)S(1)}, bf16[672,128]{1,0:T(8,128)(2,1)S(1)}, u32[]{:S(2)}, u32[]{:S(2)}) %collective-permute-start.2) | collective-permute-done | bytes 172064 | tf_op jit(solution)/shard_map/gather_yx/ppermute | solution.py:33
  27.5 2.2 %collective-permute-done.1 = bf16[672,128]{1,0:T(8,128)(2,1)S(1)} collective-permute-done((bf16[672,128]{1,0:T(8,128)(2,1)S(1)}, bf16[672,128]{1,0:T(8,128)(2,1)S(1)}, u32[]{:S(2)}, u32[]{:S(2)}) %collective-permute-start.1) | collective-permute-done | bytes 172064 | tf_op jit(solution)/shard_map/gather_yx/ppermute | solution.py:33
  29.7 1.7 %collective-permute-done = bf16[672,128]{1,0:T(8,128)(2,1)S(1)} collective-permute-done((bf16[672,128]{1,0:T(8,128)(2,1)S(1)}, bf16[672,128]{1,0:T(8,128)(2,1)S(1)}, u32[]{:S(2)}, u32[]{:S(2)}) %collective-permute-start) | collective-permute-done | bytes 172064 | tf_op jit(solution)/shard_map/gather_yx/ppermute | solution.py:33
  31.5 0.1 pad_maximum_fusion._.refs_0_
  31.6 0.9 collective-permute-start.4
  32.5 2.4 %collective-permute-start.3 = (bf16[4,672,128]{2,1,0:T(8,128)(2,1)S(1)}, bf16[4,672,128]{2,1,0:T(8,128)(2,1)S(1)}, u32[]{:S(2)}, u32[]{:S(2)}) collective-permute-start(bf16[4,672,128]{2,1,0:T(8,128)(2,1)S(1)} %pad_maximum_fusion._.refs_0_), channel_id=1, source_target_pairs={{0,2},{1,9},{2,4},{3,11},{4,6},{5,13},{6,0},{7,15},{8,10},{9,17},{... | collective-permute-start | bytes 2064392 | tf_op jit(solution)/shard_map/gather_xy/ppermute | solution.py:33
  34.9 4.1 %gather_yx.1.refs_10_.w = bf16[1024,5376]{1,0:T(8,128)(2,1)S(1)} custom-call(bf16[1024,5376]{1,0:T(8,128)(2,1)} %w.1, bf16[4,672,128]{2,1,0:T(8,128)(2,1)S(1)} %pad_maximum_fusion._.refs_0_), custom_call_target="tpu_custom_call" | custom-call | bytes 22020096 | tf_op jit(solution)/shard_map/gather_yx/pallas_call | solution.py:185
  39.0 0.1 collective-permute-start.7
  39.1 4.7 %collective-permute-done.4.refs_2_ = bf16[4,672,128]{2,1,0:T(8,128)(2,1)S(1)} collective-permute-done((bf16[4,672,128]{2,1,0:T(8,128)(2,1)S(1)}, bf16[4,672,128]{2,1,0:T(8,128)(2,1)S(1)}, u32[]{:S(2)}, u32[]{:S(2)}) %collective-permute-start.4) | collective-permute-done | bytes 688160 | tf_op jit(solution)/shard_map/gather_xy/ppermute | solution.py:33
  43.8 0.1 collective-permute-start.6
  43.9 0.0 collective-permute-done.3.refs_1_
  43.9 3.3 %collective-permute-start.5 = (bf16[2,672,128]{2,1,0:T(8,128)(2,1)S(1)}, bf16[2,672,128]{2,1,0:T(8,128)(2,1)S(1)}, u32[]{:S(2)}, u32[]{:S(2)}) collective-permute-start(bf16[2,672,128]{2,1,0:T(8,128)(2,1)S(1)} %slice.59), channel_id=1, source_target_pairs={{0,2},{1,9},{2,4},{3,11},{4,6},{5,13},{6,0},{7,15},{8,10},{9,17},{... | collective-permute-start | bytes 1032200 | tf_op jit(solution)/shard_map/gather_xy/ppermute | solution.py:33
  47.2 0.0 collective-permute-start.9
  47.2 0.5 collective-permute-start.8
  47.7 4.6 %collective-permute-done.6.refs_4_ = bf16[2,672,128]{2,1,0:T(8,128)(2,1)S(1)} collective-permute-done((bf16[2,672,128]{2,1,0:T(8,128)(2,1)S(1)}, bf16[2,672,128]{2,1,0:T(8,128)(2,1)S(1)}, u32[]{:S(2)}, u32[]{:S(2)}) %collective-permute-start.6) | collective-permute-done | bytes 344096 | tf_op jit(solution)/shard_map/gather_xy/ppermute | solution.py:33
  52.3 0.0 collective-permute-start.11
  52.4 0.0 collective-permute-done.5.refs_3_
  52.4 0.5 collective-permute-start.10
  52.9 0.0 collective-permute-done.7.refs_5_
  52.9 1.1 collective-permute-done.11.refs_9_
  54.0 0.0 collective-permute-done.9.refs_7_
  54.0 0.5 collective-permute-done.10.refs_8_
  54.5 0.0 collective-permute-done.8.refs_6_
  54.5 8.4 %scores.1 = (f32[1024,256]{1,0:T(8,128)S(1)}, f32[1024,256]{1,0:T(8,128)S(1)}, f32[8,4,256]{2,1,0:T(4,128)S(1)}, f32[4,256]{1,0:T(4,128)S(1)}) custom-call(bf16[4,672,128]{2,1,0:T(8,128)(2,1)S(1)} %pad_maximum_fusion._.refs_0_, bf16[4,672,128]{2,1,0:T(8,128)(2,1)S(1)} %collective-permute-done.3.refs_1_, ...), custom_call_target="tpu_custom_call" | custom-call | tf_op jit(solution)/shard_map/scores/pallas_call | solution.py:205
  62.9 8.6 %all_to_all.21.parts = f32[8,4,256]{2,1,0:T(4,128)S(1)} all-to-all(f32[8,4,256]{2,1,0:T(4,128)S(1)} %get-tuple-element.15), channel_id=1, replica_groups=mesh['z'=8,'y'=4,'x'=4,'c'=2] {'x','c'}, dimensions={0} | all-to-all | bytes 65536 | tf_op jit(solution)/shard_map/statistics/all_to_all | solution.py:52
  71.5 13.7 %all_to_all.22.parts = f32[32,4,256]{2,1,0:T(4,128)S(1)} all-to-all(f32[32,4,256]{2,1,0:T(4,128)S(1)} %statistics.1), channel_id=1, replica_groups=mesh['z'=8,'y'=4,'x'=4,'c'=2] {'z','y'}, dimensions={0} | all-to-all | bytes 262144 | tf_op jit(solution)/shard_map/statistics/all_to_all | solution.py:52
  85.2 2.4 %product.2 = (bf16[4,4,64,672]{3,2,1,0:T(8,128)(2,1)S(1)}, bf16[256,1024]{1,0:T(8,128)(2,1)S(1)}) custom-call(f32[32,4,256]{2,1,0:T(4,128)S(1)} %all_to_all.22.parts, f32[4,256]{1,0:T(4,128)S(1)} %get-tuple-element.16.own_top, f32[1024,256]{1,0:T(8,128)S(1)} %get-tuple-element.17.raised, f32[1024,256]{1,0:T(8,128)S(1)} %get-tuple-element.18.slopes, ...), custom_call_target="tpu_custom_call" | custom-call | tf_op jit(solution)/shard_map/product/pallas_call | solution.py:238
  87.6 0.1 collective-permute-start.12
  87.7 2.0 %product.3 = f32[4,4,64,672]{3,2,1,0:T(8,128)S(1)} custom-call(bf16[256,1024]{1,0:T(8,128)(2,1)S(1)} %get-tuple-element.19.mixture, bf16[1024,5376]{1,0:T(8,128)(2,1)S(1)} %gather_yx.1.refs_10_.w), custom_call_target="tpu_custom_call" | custom-call | flops 1409286144 | bytes 11010048 | tf_op jit(solution)/shard_map/product/pallas_call | solution.py:249
  89.7 1.4 %collective-permute-done.12 = bf16[4,4,64,672]{3,2,1,0:T(8,128)(2,1)S(1)} collective-permute-done((bf16[4,4,64,672]{3,2,1,0:T(8,128)(2,1)S(1)}, bf16[4,4,64,672]{3,2,1,0:T(8,128)(2,1)S(1)}, u32[]{:S(2)}, u32[]{:S(2)}) %collective-permute-start.12) | collective-permute-done | bytes 1376288 | tf_op jit(solution)/shard_map/product/ppermute | solution.py:33
  91.1 0.3 fusion.7
  91.4 2.2 %collective-permute-start.13 = (bf16[4,64,672]{2,1,0:T(8,128)(2,1)S(1)}, bf16[4,64,672]{2,1,0:T(8,128)(2,1)S(1)}, u32[]{:S(2)}, u32[]{:S(2)}) collective-permute-start(bf16[4,64,672]{2,1,0:T(8,128)(2,1)S(1)} %get-tuple-element.23), channel_id=1, source_target_pairs={{0,2},{1,9},{2,4},{3,11},{4,6},{5,13},{6,0},{7,15},{8,10},{9,17},{... | collective-permute-start | bytes 1032200 | tf_op jit(solution)/shard_map/scatter_xy/ppermute | solution.py:33
  93.6 0.5 collective-permute-start.15
  94.1 0.9 collective-permute-start.14
  95.0 8.1 %collective-permute-done.13 = bf16[4,64,672]{2,1,0:T(8,128)(2,1)S(1)} collective-permute-done((bf16[4,64,672]{2,1,0:T(8,128)(2,1)S(1)}, bf16[4,64,672]{2,1,0:T(8,128)(2,1)S(1)}, u32[]{:S(2)}, u32[]{:S(2)}) %collective-permute-start.13) | collective-permute-done | bytes 344096 | tf_op jit(solution)/shard_map/scatter_xy/ppermute | solution.py:33
  103.1 0.0 collective-permute-done.15
  103.1 3.9 %collective-permute-done.14 = bf16[4,64,672]{2,1,0:T(8,128)(2,1)S(1)} collective-permute-done((bf16[4,64,672]{2,1,0:T(8,128)(2,1)S(1)}, bf16[4,64,672]{2,1,0:T(8,128)(2,1)S(1)}, u32[]{:S(2)}, u32[]{:S(2)}) %collective-permute-start.14) | collective-permute-done | bytes 344096 | tf_op jit(solution)/shard_map/scatter_xy/ppermute | solution.py:33
  107.1 0.2 fusion.14
  107.3 0.1 collective-permute-start.16
  107.4 2.7 %collective-permute-start.18 = (bf16[64,672]{1,0:T(8,128)(2,1)S(1)}, bf16[64,672]{1,0:T(8,128)(2,1)S(1)}, u32[]{:S(2)}, u32[]{:S(2)}) collective-permute-start(bf16[64,672]{1,0:T(8,128)(2,1)S(1)} %get-tuple-element.27), channel_id=1, source_target_pairs={{0,16},{1,5},{2,18},{3,7},{4,20},{5,1},{6,22},{7,3},{8,24},{9,13},... | collective-permute-start | bytes 258056 | tf_op jit(solution)/shard_map/scatter_yx/ppermute | solution.py:33
  110.2 1.0 collective-permute-start.17
  111.2 3.1 %collective-permute-done.16 = bf16[64,672]{1,0:T(8,128)(2,1)S(1)} collective-permute-done((bf16[64,672]{1,0:T(8,128)(2,1)S(1)}, bf16[64,672]{1,0:T(8,128)(2,1)S(1)}, u32[]{:S(2)}, u32[]{:S(2)}) %collective-permute-start.16) | collective-permute-done | bytes 86048 | tf_op jit(solution)/shard_map/scatter_yx/ppermute | solution.py:33
  114.3 0.0 collective-permute-done.18
  114.3 0.9 collective-permute-done.17
  115.2 12.2 %all_to_all.23 = f32[8,8,672]{2,1,0:T(8,128)S(1)} all-to-all(f32[8,8,672]{2,1,0:T(8,128)S(1)} %fusion.13), channel_id=1, replica_groups=mesh['z'=8,'y'=4,'x'=4,'c'=2] {'z'}, dimensions={0} | all-to-all | bytes 344064 | tf_op jit(solution)/shard_map/scatter_z/all_to_all | solution.py:52
  127.4 0.6 reduce_sum.9
  (6 shorter events, 0.2 us)
Async XLA Ops:
  19.6 7.9 %collective-permute-start.2 = (bf16[672,128]{1,0:T(8,128)(2,1)S(1)}, bf16[672,128]{1,0:T(8,128)(2,1)S(1)}, u32[]{:S(2)}, u32[]{:S(2)}) collective-permute-start(bf16[672,128]{1,0:T(8,128)(2,1)S(1)} %gather_z.1), channel_id=1, source_target_pairs={{0,24},{1,7},{2,26},{3,1},{4,28},{5,3},{6,30},{7,5},{8,0},{9,15},{... | collective-permute-start | bytes 516104 | tf_op jit(solution)/shard_map/gather_yx/ppermute | solution.py:33
  22.7 7.0 %collective-permute-start.1 = (bf16[672,128]{1,0:T(8,128)(2,1)S(1)}, bf16[672,128]{1,0:T(8,128)(2,1)S(1)}, u32[]{:S(2)}, u32[]{:S(2)}) collective-permute-start(bf16[672,128]{1,0:T(8,128)(2,1)S(1)} %gather_z.1), channel_id=1, source_target_pairs={{0,16},{1,5},{2,18},{3,7},{4,20},{5,1},{6,22},{7,3},{8,24},{9,13},... | collective-permute-start | bytes 516104 | tf_op jit(solution)/shard_map/gather_yx/ppermute | solution.py:33
  23.3 8.1 %collective-permute-start = (bf16[672,128]{1,0:T(8,128)(2,1)S(1)}, bf16[672,128]{1,0:T(8,128)(2,1)S(1)}, u32[]{:S(2)}, u32[]{:S(2)}) collective-permute-start(bf16[672,128]{1,0:T(8,128)(2,1)S(1)} %gather_z.1), channel_id=1, source_target_pairs={{0,8},{1,3},{2,10},{3,5},{4,12},{5,7},{6,14},{7,1},{8,16},{9,11},{... | collective-permute-start | bytes 516104 | tf_op jit(solution)/shard_map/gather_yx/ppermute | solution.py:33
  31.6 12.2 %collective-permute-start.4 = (bf16[4,672,128]{2,1,0:T(8,128)(2,1)S(1)}, bf16[4,672,128]{2,1,0:T(8,128)(2,1)S(1)}, u32[]{:S(2)}, u32[]{:S(2)}) collective-permute-start(bf16[4,672,128]{2,1,0:T(8,128)(2,1)S(1)} %pad_maximum_fusion._.refs_0_), channel_id=1, source_target_pairs={{0,6},{1,25},{2,0},{3,27},{4,2},{5,29},{6,4},{7,31},{8,14},{9,1},{... | collective-permute-start | bytes 2064392 | tf_op jit(solution)/shard_map/gather_xy/ppermute | solution.py:33
  32.5 11.4 %collective-permute-start.3 = (bf16[4,672,128]{2,1,0:T(8,128)(2,1)S(1)}, bf16[4,672,128]{2,1,0:T(8,128)(2,1)S(1)}, u32[]{:S(2)}, u32[]{:S(2)}) collective-permute-start(bf16[4,672,128]{2,1,0:T(8,128)(2,1)S(1)} %pad_maximum_fusion._.refs_0_), channel_id=1, source_target_pairs={{0,2},{1,9},{2,4},{3,11},{4,6},{5,13},{6,0},{7,15},{8,10},{9,17},{... | collective-permute-start | bytes 2064392 | tf_op jit(solution)/shard_map/gather_xy/ppermute | solution.py:33
  39.0 13.8 %collective-permute-start.7 = (bf16[4,672,128]{2,1,0:T(8,128)(2,1)S(1)}, bf16[4,672,128]{2,1,0:T(8,128)(2,1)S(1)}, u32[]{:S(2)}, u32[]{:S(2)}) collective-permute-start(bf16[4,672,128]{2,1,0:T(8,128)(2,1)S(1)} %pad_maximum_fusion._.refs_0_), channel_id=1, source_target_pairs={{0,1},{1,0},{2,3},{3,2},{4,5},{5,4},{6,7},{7,6},{8,9},{9,8},{10,11... | collective-permute-start | bytes 2064392 | tf_op jit(solution)/shard_map/gather_xy/ppermute | solution.py:33
  43.8 8.5 %collective-permute-start.6 = (bf16[2,672,128]{2,1,0:T(8,128)(2,1)S(1)}, bf16[2,672,128]{2,1,0:T(8,128)(2,1)S(1)}, u32[]{:S(2)}, u32[]{:S(2)}) collective-permute-start(bf16[2,672,128]{2,1,0:T(8,128)(2,1)S(1)} %slice.60), channel_id=1, source_target_pairs={{0,6},{1,25},{2,0},{3,27},{4,2},{5,29},{6,4},{7,31},{8,14},{9,1},{... | collective-permute-start | bytes 1032200 | tf_op jit(solution)/shard_map/gather_xy/ppermute | solution.py:33
  43.9 8.4 %collective-permute-start.5 = (bf16[2,672,128]{2,1,0:T(8,128)(2,1)S(1)}, bf16[2,672,128]{2,1,0:T(8,128)(2,1)S(1)}, u32[]{:S(2)}, u32[]{:S(2)}) collective-permute-start(bf16[2,672,128]{2,1,0:T(8,128)(2,1)S(1)} %slice.59), channel_id=1, source_target_pairs={{0,2},{1,9},{2,4},{3,11},{4,6},{5,13},{6,0},{7,15},{8,10},{9,17},{... | collective-permute-start | bytes 1032200 | tf_op jit(solution)/shard_map/gather_xy/ppermute | solution.py:33
  47.2 6.8 %collective-permute-start.9 = (bf16[4,672,128]{2,1,0:T(8,128)(2,1)S(1)}, bf16[4,672,128]{2,1,0:T(8,128)(2,1)S(1)}, u32[]{:S(2)}, u32[]{:S(2)}) collective-permute-start(bf16[4,672,128]{2,1,0:T(8,128)(2,1)S(1)} %collective-permute-done.4.refs_2_), channel_id=1, source_target_pairs={{0,1},{1,0},{2,3},{3,2},{4,5},{5,4},{6,7},{7,6},{8,9},{9,8},{10,11... | collective-permute-start | bytes 2064392 | tf_op jit(solution)/shard_map/gather_xy/ppermute | solution.py:33
  47.2 7.3 %collective-permute-start.8 = (bf16[4,672,128]{2,1,0:T(8,128)(2,1)S(1)}, bf16[4,672,128]{2,1,0:T(8,128)(2,1)S(1)}, u32[]{:S(2)}, u32[]{:S(2)}) collective-permute-start(bf16[4,672,128]{2,1,0:T(8,128)(2,1)S(1)} %collective-permute-done.3.refs_1_), channel_id=1, source_target_pairs={{0,1},{1,0},{2,3},{3,2},{4,5},{5,4},{6,7},{7,6},{8,9},{9,8},{10,11... | collective-permute-start | bytes 2064392 | tf_op jit(solution)/shard_map/gather_xy/ppermute | solution.py:33
  52.3 1.7 %collective-permute-start.11 = (bf16[2,672,128]{2,1,0:T(8,128)(2,1)S(1)}, bf16[2,672,128]{2,1,0:T(8,128)(2,1)S(1)}, u32[]{:S(2)}, u32[]{:S(2)}) collective-permute-start(bf16[2,672,128]{2,1,0:T(8,128)(2,1)S(1)} %collective-permute-done.6.refs_4_), channel_id=1, source_target_pairs={{0,1},{1,0},{2,3},{3,2},{4,5},{5,4},{6,7},{7,6},{8,9},{9,8},{10,11... | collective-permute-start | bytes 1032200 | tf_op jit(solution)/shard_map/gather_xy/ppermute | solution.py:33
  52.4 2.1 %collective-permute-start.10 = (bf16[2,672,128]{2,1,0:T(8,128)(2,1)S(1)}, bf16[2,672,128]{2,1,0:T(8,128)(2,1)S(1)}, u32[]{:S(2)}, u32[]{:S(2)}) collective-permute-start(bf16[2,672,128]{2,1,0:T(8,128)(2,1)S(1)} %collective-permute-done.5.refs_3_), channel_id=1, source_target_pairs={{0,1},{1,0},{2,3},{3,2},{4,5},{5,4},{6,7},{7,6},{8,9},{9,8},{10,11... | collective-permute-start | bytes 1032200 | tf_op jit(solution)/shard_map/gather_xy/ppermute | solution.py:33
  87.6 3.5 %collective-permute-start.12 = (bf16[4,4,64,672]{3,2,1,0:T(8,128)(2,1)S(1)}, bf16[4,4,64,672]{3,2,1,0:T(8,128)(2,1)S(1)}, u32[]{:S(2)}, u32[]{:S(2)}) collective-permute-start(bf16[4,4,64,672]{3,2,1,0:T(8,128)(2,1)S(1)} %get-tuple-element.20), channel_id=1, source_target_pairs={{0,1},{1,0},{2,3},{3,2},{4,5},{5,4},{6,7},{7,6},{8,9},{9,8},{10,11... | collective-permute-start | bytes 4128776 | tf_op jit(solution)/shard_map/product/ppermute | solution.py:33
  91.4 11.7 %collective-permute-start.13 = (bf16[4,64,672]{2,1,0:T(8,128)(2,1)S(1)}, bf16[4,64,672]{2,1,0:T(8,128)(2,1)S(1)}, u32[]{:S(2)}, u32[]{:S(2)}) collective-permute-start(bf16[4,64,672]{2,1,0:T(8,128)(2,1)S(1)} %get-tuple-element.23), channel_id=1, source_target_pairs={{0,2},{1,9},{2,4},{3,11},{4,6},{5,13},{6,0},{7,15},{8,10},{9,17},{... | collective-permute-start | bytes 1032200 | tf_op jit(solution)/shard_map/scatter_xy/ppermute | solution.py:33
  93.6 9.5 %collective-permute-start.15 = (bf16[4,64,672]{2,1,0:T(8,128)(2,1)S(1)}, bf16[4,64,672]{2,1,0:T(8,128)(2,1)S(1)}, u32[]{:S(2)}, u32[]{:S(2)}) collective-permute-start(bf16[4,64,672]{2,1,0:T(8,128)(2,1)S(1)} %get-tuple-element.24), channel_id=1, source_target_pairs={{0,4},{1,17},{2,6},{3,19},{4,0},{5,21},{6,2},{7,23},{8,12},{9,25},... | collective-permute-start | bytes 1032200 | tf_op jit(solution)/shard_map/scatter_xy/ppermute | solution.py:33
  94.1 13.0 %collective-permute-start.14 = (bf16[4,64,672]{2,1,0:T(8,128)(2,1)S(1)}, bf16[4,64,672]{2,1,0:T(8,128)(2,1)S(1)}, u32[]{:S(2)}, u32[]{:S(2)}) collective-permute-start(bf16[4,64,672]{2,1,0:T(8,128)(2,1)S(1)} %get-tuple-element.25), channel_id=1, source_target_pairs={{0,6},{1,25},{2,0},{3,27},{4,2},{5,29},{6,4},{7,31},{8,14},{9,1},{... | collective-permute-start | bytes 1032200 | tf_op jit(solution)/shard_map/scatter_xy/ppermute | solution.py:33
  107.3 7.0 %collective-permute-start.16 = (bf16[64,672]{1,0:T(8,128)(2,1)S(1)}, bf16[64,672]{1,0:T(8,128)(2,1)S(1)}, u32[]{:S(2)}, u32[]{:S(2)}) collective-permute-start(bf16[64,672]{1,0:T(8,128)(2,1)S(1)} %get-tuple-element.26), channel_id=1, source_target_pairs={{0,8},{1,3},{2,10},{3,5},{4,12},{5,7},{6,14},{7,1},{8,16},{9,11},{... | collective-permute-start | bytes 258056 | tf_op jit(solution)/shard_map/scatter_yx/ppermute | solution.py:33
  107.4 6.9 %collective-permute-start.18 = (bf16[64,672]{1,0:T(8,128)(2,1)S(1)}, bf16[64,672]{1,0:T(8,128)(2,1)S(1)}, u32[]{:S(2)}, u32[]{:S(2)}) collective-permute-start(bf16[64,672]{1,0:T(8,128)(2,1)S(1)} %get-tuple-element.27), channel_id=1, source_target_pairs={{0,16},{1,5},{2,18},{3,7},{4,20},{5,1},{6,22},{7,3},{8,24},{9,13},... | collective-permute-start | bytes 258056 | tf_op jit(solution)/shard_map/scatter_yx/ppermute | solution.py:33
  110.2 5.0 %collective-permute-start.17 = (bf16[64,672]{1,0:T(8,128)(2,1)S(1)}, bf16[64,672]{1,0:T(8,128)(2,1)S(1)}, u32[]{:S(2)}, u32[]{:S(2)}) collective-permute-start(bf16[64,672]{1,0:T(8,128)(2,1)S(1)} %get-tuple-element.28), channel_id=1, source_target_pairs={{0,24},{1,7},{2,26},{3,1},{4,28},{5,3},{6,30},{7,5},{8,0},{9,15},{... | collective-permute-start | bytes 258056 | tf_op jit(solution)/shard_map/scatter_yx/ppermute | solution.py:33

commit v5 on v4

--- a/solution.py
+++ b/solution.py
@@ -46,6 +46,7 @@
 
 
 HOPS = (1, 3, 2)
+PLACE = (0, 2, 1, 3)
 
 
 def all_of(value, axes):
@@ -65,50 +66,38 @@
 
 
 def scores_kernel(*refs):
-    own, theirs = refs[:5], refs[5:10]
-    w, scores, slopes, stats, tops, whole = refs[10:]
-    step = pl.program_id(0)
-    rows = w.shape[0] // pl.num_programs(0)
+    own, theirs = refs[:NQ], refs[NQ : 2 * NQ]
+    w, raised, slopes, stats, tops, whole = refs[2 * NQ :]
     width, lanes = own[0].shape[1:]
-
-    @pl.when(step == 0)
-    def _():
-        y, x, c = lax.axis_index("y"), lax.axis_index("x"), lax.axis_index("c")
-        for pieces, parity in ((own, c), (theirs, 1 - c)):
-            for k in range(NQ):
-                for r in range(NQ):
-                    x_back = jnp.where(parity == 0, k, r)
-                    y_back = jnp.where(parity == 0, r, k)
-                    x_at = lax.rem(x + NQ - x_back, NQ)
-                    y_at = lax.rem(y + NQ - y_back, NQ)
-                    if k == 2:
-                        piece = pieces[3 + r // 2][r % 2]
-                    else:
-                        piece = pieces[k % 3 + k // 3 * 2][r]
-                    first = pl.multiple_of((2 * x_at + parity) * width, width)
-                    column = pl.multiple_of(y_at * lanes, lanes)
-                    whole[pl.ds(first, width), pl.ds(column, lanes)] = piece
-
-    at = pl.ds(pl.multiple_of(step * rows, rows), rows)
-    both = jnp.dot(w[at, :], whole[...], preferred_element_type=F32)
-    low = lax.broadcasted_iota(jnp.int32, (rows, lanes), 1) < lanes // 2
+    y, x, c = lax.axis_index("y"), lax.axis_index("x"), lax.axis_index("c")
+    for pieces, parity in ((own, c), (theirs, 1 - c)):
+        for k in range(NQ):
+            for r in range(NQ):
+                x_back = jnp.where(parity == 0, k, r)
+                y_back = jnp.where(parity == 0, r, k)
+                x_at = lax.rem(x + NQ - x_back, NQ)
+                y_at = lax.rem(y + NQ - y_back, NQ)
+                first = pl.multiple_of((2 * x_at + parity) * width, width)
+                column = pl.multiple_of(y_at * lanes, lanes)
+                whole[pl.ds(first, width), pl.ds(column, lanes)] = pieces[PLACE[k]][r]
+
+    both = jnp.dot(w[...], whole[...], preferred_element_type=F32)
+    low = lax.broadcasted_iota(jnp.int32, (both.shape[0], lanes), 1) < lanes // 2
     for pair in range(NQ // 2):
         first = both[:, 2 * pair * lanes : (2 * pair + 1) * lanes]
         second = both[:, (2 * pair + 1) * lanes : (2 * pair + 2) * lanes]
         columns = slice(pair * lanes, (pair + 1) * lanes)
-        scores[at, columns] = jnp.where(low, first, pltpu.roll(second, lanes // 2, 1))
-        slopes[at, columns] = jnp.where(low, pltpu.roll(first, lanes // 2, 1), second)
-
-    @pl.when(step == pl.num_programs(0) - 1)
-    def _():
-        top = jnp.max(scores[...], axis=0, keepdims=True)
-        raised = jnp.exp(scores[...] - top)
-        scores[...] = raised
-        total = jnp.sum(raised, axis=0, keepdims=True)
-        dotted = jnp.sum(raised * slopes[...], axis=0, keepdims=True)
-        own_stats = jnp.concatenate((top, total, dotted, dotted), 0)
-        stats[...] = jnp.broadcast_to(own_stats[None], stats.shape)
-        tops[...] = jnp.broadcast_to(top, tops.shape)
+        raised[:, columns] = jnp.where(low, first, pltpu.roll(second, lanes // 2, 1))
+        slopes[:, columns] = jnp.where(low, pltpu.roll(first, lanes // 2, 1), second)
+
+    top = jnp.max(raised[...], axis=0, keepdims=True)
+    value = jnp.exp(raised[...] - top)
+    raised[...] = value
+    total = jnp.sum(value, axis=0, keepdims=True)
+    dotted = jnp.sum(value * slopes[...], axis=0, keepdims=True)
+    own_stats = jnp.concatenate((top, total, dotted, dotted), 0)
+    stats[...] = jnp.broadcast_to(own_stats[None], stats.shape)
+    tops[...] = jnp.broadcast_to(top, tops.shape)
 
 
 def merged(parts):
@@ -194,45 +183,36 @@
             compiler_params=pltpu.CompilerParams(vmem_limit_bytes=MIB),
         )(pltpu.with_memory_space_constraint(out_weight, pltpu.HBM), block)
     with jax.named_scope("gather_xy"):
-        behind, ahead = send(block, along_xy(1)), send(block, along_xy(3))
-        held, weight = lax.optimization_barrier((block, weight))
-        own = [held, behind, ahead, send(behind[:2], along_xy(1)), send(ahead[2:], along_xy(3))]
-        theirs = [send(piece, other_core) for piece in own]
-
-    steps = 4
-    at_once = lambda *n: pl.BlockSpec(n, lambda i: (0,) * len(n))
+        pieces = {0: block}
+        for k in HOPS:
+            pieces[k] = send(block, along_xy(k))
+        pieces[0], weight = lax.optimization_barrier((pieces[0], weight))
+        theirs = {k: send(pieces[k], other_core) for k in (0,) + HOPS}
+
     with jax.named_scope("scores"):
         raised, slopes, stats, top = pl.pallas_call(
             scores_kernel,
-            grid=(steps,),
             out_shape=(
                 shape((vocab, tokens), F32),
                 shape((vocab, tokens), F32),
-                shape((2 * NQ, 4, tokens), F32),
+                shape((NQ * NQ, 4, tokens), F32),
                 shape((4, tokens), F32),
             ),
-            in_specs=[VMEM] * 11,
-            out_specs=(
-                at_once(vocab, tokens),
-                at_once(vocab, tokens),
-                at_once(2 * NQ, 4, tokens),
-                at_once(4, tokens),
-            ),
-            scratch_shapes=[
-                pltpu.VMEM((features, 2 * tokens), BF),
-            ],
+            in_specs=[VMEM] * (2 * NQ + 1),
+            out_specs=(VMEM,) * 4,
+            scratch_shapes=[pltpu.VMEM((features, 2 * tokens), BF)],
             compiler_params=pltpu.CompilerParams(vmem_limit_bytes=20 * MIB),
-        )(*own, *theirs, weight)
+        )(*(pieces[k] for k in PLACE), *(theirs[k] for k in PLACE), weight)
 
     with jax.named_scope("statistics"):
         stats = pl.pallas_call(
             merge_kernel,
-            out_shape=shape((NZ * NQ, 4, tokens), F32),
+            out_shape=shape((2 * NZ, 4, tokens), F32),
             in_specs=[VMEM],
             out_specs=VMEM,
             compiler_params=pltpu.CompilerParams(vmem_limit_bytes=4 * MIB),
-        )(all_of(stats, ("x", "c")))
-        parts = all_of(stats, ("z", "y"))
+        )(all_of(stats, ("y", "x")))
+        parts = all_of(stats, ("z", "c"))
 
     with jax.named_scope("product"):
         give, mixture = pl.pallas_call(

time: 128 us -> 127 us (level)
  waiting for transfers between devices: 35.5 us -> 39.5 us
  starting transfers between devices: 20 us -> 16.8 us
  blocking collectives: 53.2 us -> 51.7 us
    ppermute x19 -> x17, waiting for transfers between devices: 35.5 us -> 39.5 us  [send(): return lax.ppermute(value, AXES, perm(move))]
    ppermute x19 -> x17, starting transfers between devices: 20 us -> 16.8 us  [send(): return lax.ppermute(value, AXES, perm(move))]
    all_to_all x4, blocking collectives: 53.2 us -> 51.7 us  [all_of(): return lax.all_to_all(value, axes, 0, 0)]
  transfers between devices with their start and end apart: 19 -> 17, of which waited for: 12 -> 12; matrix products, arithmetic and copies ran while one was open for 0% -> 0% of each run, Pallas kernels for 5% -> 5%
where the time goes in v5:
time: 127 us; the launch traced here: 126 us
  blocking collectives  51.7 us (41%)
  waiting for transfers between devices  39.5 us (31%)
  starting transfers between devices  16.8 us (13%)
  Pallas kernels  16.2 us (13%)
  other arithmetic  2.05 us (2%)
    all_to_all x4, blocking collectives, all_of(): return lax.all_to_all(value, axes, 0, 0)  51.7 us
    ppermute x17, waiting for transfers between devices, send(): return lax.ppermute(value, AXES, perm(move))  39.5 us
    ppermute x17, starting transfers between devices, send(): return lax.ppermute(value, AXES, perm(move))  16.8 us
    pallas_call x1, Pallas kernels, per_device(): pl.pallas_call(scores_kernel, out_shape=(shape((vocab, tokens), F32), sha...  7.53 us
    pallas_call x1, Pallas kernels, per_device(): pl.pallas_call(load_kernel, out_shape=pltpu.VMEM((vocab, features), BF),...  4.14 us
  transfers between devices with their start and end apart: 17, of which 12 were waited for; matrix products, arithmetic and copies ran while one was open for 0% of the time, Pallas kernels for 5%

profile of v5, /device:TPU:6, one launch (start us, length us, event | category | flops | bytes accessed | tf_op | source)
XLA Modules:
  0.0 126.4 jit_solution(11158330027531274423)
XLA Ops:
  0.0 0.7 pad_maximum_fusion.1
  0.8 18.7 %all_to_all.20.block = bf16[8,2,8,672]{3,2,1,0:T(8,128)(2,1)S(1)} all-to-all(bf16[8,2,8,672]{3,2,1,0:T(8,128)(2,1)S(1)} %broadcast_in_dim.2), channel_id=1, replica_groups=mesh['z'=8,'y'=4,'x'=4,'c'=2] {'z'}, dimensions={0} | all-to-all | bytes 344064 | tf_op jit(solution)/shard_map/gather_z/all_to_all | solution.py:53
  19.5 0.1 gather_z.1
  19.6 3.1 %collective-permute-start.2 = (bf16[672,128]{1,0:T(8,128)(2,1)S(1)}, bf16[672,128]{1,0:T(8,128)(2,1)S(1)}, u32[]{:S(2)}, u32[]{:S(2)}) collective-permute-start(bf16[672,128]{1,0:T(8,128)(2,1)S(1)} %gather_z.1), channel_id=1, source_target_pairs={{0,24},{1,7},{2,26},{3,1},{4,28},{5,3},{6,30},{7,5},{8,0},{9,15},{... | collective-permute-start | bytes 516104 | tf_op jit(solution)/shard_map/gather_yx/ppermute | solution.py:33
  22.7 0.6 collective-permute-start.1
  23.3 1.0 collective-permute-start
  24.3 3.2 %collective-permute-done.2 = bf16[672,128]{1,0:T(8,128)(2,1)S(1)} collective-permute-done((bf16[672,128]{1,0:T(8,128)(2,1)S(1)}, bf16[672,128]{1,0:T(8,128)(2,1)S(1)}, u32[]{:S(2)}, u32[]{:S(2)}) %collective-permute-start.2) | collective-permute-done | bytes 172064 | tf_op jit(solution)/shard_map/gather_yx/ppermute | solution.py:33
  27.5 2.2 %collective-permute-done.1 = bf16[672,128]{1,0:T(8,128)(2,1)S(1)} collective-permute-done((bf16[672,128]{1,0:T(8,128)(2,1)S(1)}, bf16[672,128]{1,0:T(8,128)(2,1)S(1)}, u32[]{:S(2)}, u32[]{:S(2)}) %collective-permute-start.1) | collective-permute-done | bytes 172064 | tf_op jit(solution)/shard_map/gather_yx/ppermute | solution.py:33
  29.7 1.7 %collective-permute-done = bf16[672,128]{1,0:T(8,128)(2,1)S(1)} collective-permute-done((bf16[672,128]{1,0:T(8,128)(2,1)S(1)}, bf16[672,128]{1,0:T(8,128)(2,1)S(1)}, u32[]{:S(2)}, u32[]{:S(2)}) %collective-permute-start) | collective-permute-done | bytes 172064 | tf_op jit(solution)/shard_map/gather_yx/ppermute | solution.py:33
  31.5 0.1 pad_maximum_fusion._.refs_0_
  31.6 0.9 collective-permute-start.5
  32.5 2.4 %collective-permute-start.4 = (bf16[4,672,128]{2,1,0:T(8,128)(2,1)S(1)}, bf16[4,672,128]{2,1,0:T(8,128)(2,1)S(1)}, u32[]{:S(2)}, u32[]{:S(2)}) collective-permute-start(bf16[4,672,128]{2,1,0:T(8,128)(2,1)S(1)} %pad_maximum_fusion._.refs_0_), channel_id=1, source_target_pairs={{0,2},{1,9},{2,4},{3,11},{4,6},{5,13},{6,0},{7,15},{8,10},{9,17},{... | collective-permute-start | bytes 2064392 | tf_op jit(solution)/shard_map/gather_xy/ppermute | solution.py:33
  34.9 0.2 collective-permute-start.3
  35.1 4.1 %gather_yx.1.refs_8_.w = bf16[1024,5376]{1,0:T(8,128)(2,1)S(1)} custom-call(bf16[1024,5376]{1,0:T(8,128)(2,1)} %w.1, bf16[4,672,128]{2,1,0:T(8,128)(2,1)S(1)} %pad_maximum_fusion._.refs_0_), custom_call_target="tpu_custom_call" | custom-call | bytes 22020096 | tf_op jit(solution)/shard_map/gather_yx/pallas_call | solution.py:174
  39.2 0.1 collective-permute-start.6
  39.3 11.8 %collective-permute-done.5.refs_3_ = bf16[4,672,128]{2,1,0:T(8,128)(2,1)S(1)} collective-permute-done((bf16[4,672,128]{2,1,0:T(8,128)(2,1)S(1)}, bf16[4,672,128]{2,1,0:T(8,128)(2,1)S(1)}, u32[]{:S(2)}, u32[]{:S(2)}) %collective-permute-start.5) | collective-permute-done | bytes 688160 | tf_op jit(solution)/shard_map/gather_xy/ppermute | solution.py:33
  51.2 0.0 collective-permute-start.9
  51.2 0.0 collective-permute-done.4.refs_2_
  51.2 0.5 collective-permute-start.8
  51.7 0.0 collective-permute-done.3.refs_1_
  51.7 0.1 collective-permute-start.7
  51.8 0.0 collective-permute-done.6.refs_4_
  51.8 1.5 %collective-permute-done.9.refs_7_ = bf16[4,672,128]{2,1,0:T(8,128)(2,1)S(1)} collective-permute-done((bf16[4,672,128]{2,1,0:T(8,128)(2,1)S(1)}, bf16[4,672,128]{2,1,0:T(8,128)(2,1)S(1)}, u32[]{:S(2)}, u32[]{:S(2)}) %collective-permute-start.9) | collective-permute-done | bytes 688160 | tf_op jit(solution)/shard_map/gather_xy/ppermute | solution.py:33
  53.3 1.0 collective-permute-done.8.refs_6_
  54.3 1.0 collective-permute-done.7.refs_5_
  55.3 7.5 %scores.1 = (f32[1024,256]{1,0:T(8,128)S(1)}, f32[1024,256]{1,0:T(8,128)S(1)}, f32[16,4,256]{2,1,0:T(4,128)S(1)}, f32[4,256]{1,0:T(4,128)S(1)}) custom-call(bf16[4,672,128]{2,1,0:T(8,128)(2,1)S(1)} %pad_maximum_fusion._.refs_0_, bf16[4,672,128]{2,1,0:T(8,128)(2,1)S(1)} %collective-permute-done.3.refs_1_, ...), custom_call_target="tpu_custom_call" | custom-call | tf_op jit(solution)/shard_map/scores/pallas_call | solution.py:193
  62.8 10.4 %all_to_all.21.parts = f32[16,4,256]{2,1,0:T(4,128)S(1)} all-to-all(f32[16,4,256]{2,1,0:T(4,128)S(1)} %get-tuple-element.15), channel_id=1, replica_groups=mesh['z'=8,'y'=4,'x'=4,'c'=2] {'y','x'}, dimensions={0} | all-to-all | bytes 131072 | tf_op jit(solution)/shard_map/statistics/all_to_all | solution.py:53
  73.3 10.4 %all_to_all.22.parts = f32[16,4,256]{2,1,0:T(4,128)S(1)} all-to-all(f32[16,4,256]{2,1,0:T(4,128)S(1)} %statistics.1), channel_id=1, replica_groups=mesh['z'=8,'y'=4,'x'=4,'c'=2] {'z','c'}, dimensions={0} | all-to-all | bytes 131072 | tf_op jit(solution)/shard_map/statistics/all_to_all | solution.py:53
  83.6 2.3 %product.2 = (bf16[4,4,64,672]{3,2,1,0:T(8,128)(2,1)S(1)}, bf16[256,1024]{1,0:T(8,128)(2,1)S(1)}) custom-call(f32[16,4,256]{2,1,0:T(4,128)S(1)} %all_to_all.22.parts, f32[4,256]{1,0:T(4,128)S(1)} %get-tuple-element.16.own_top, f32[1024,256]{1,0:T(8,128)S(1)} %get-tuple-element.17.raised, f32[1024,256]{1,0:T(8,128)S(1)} %get-tuple-element.18.slopes, ...), custom_call_target="tpu_custom_call" | custom-call | tf_op jit(solution)/shard_map/product/pallas_call | solution.py:218
  86.0 0.5 collective-permute-start.10
  86.5 2.0 %product.3 = f32[4,4,64,672]{3,2,1,0:T(8,128)S(1)} custom-call(bf16[256,1024]{1,0:T(8,128)(2,1)S(1)} %get-tuple-element.19.mixture, bf16[1024,5376]{1,0:T(8,128)(2,1)S(1)} %gather_yx.1.refs_8_.w), custom_call_target="tpu_custom_call" | custom-call | flops 1409286144 | bytes 11010048 | tf_op jit(solution)/shard_map/product/pallas_call | solution.py:229
  88.5 1.0 collective-permute-done.10
  89.5 0.3 fusion.7
  89.8 2.1 %collective-permute-start.11 = (bf16[4,64,672]{2,1,0:T(8,128)(2,1)S(1)}, bf16[4,64,672]{2,1,0:T(8,128)(2,1)S(1)}, u32[]{:S(2)}, u32[]{:S(2)}) collective-permute-start(bf16[4,64,672]{2,1,0:T(8,128)(2,1)S(1)} %get-tuple-element.23), channel_id=1, source_target_pairs={{0,2},{1,9},{2,4},{3,11},{4,6},{5,13},{6,0},{7,15},{8,10},{9,17},{... | collective-permute-start | bytes 1032200 | tf_op jit(solution)/shard_map/scatter_xy/ppermute | solution.py:33
  92.0 0.7 collective-permute-start.13
  92.7 0.7 collective-permute-start.12
  93.4 8.1 %collective-permute-done.11 = bf16[4,64,672]{2,1,0:T(8,128)(2,1)S(1)} collective-permute-done((bf16[4,64,672]{2,1,0:T(8,128)(2,1)S(1)}, bf16[4,64,672]{2,1,0:T(8,128)(2,1)S(1)}, u32[]{:S(2)}, u32[]{:S(2)}) %collective-permute-start.11) | collective-permute-done | bytes 344096 | tf_op jit(solution)/shard_map/scatter_xy/ppermute | solution.py:33
  101.5 0.0 collective-permute-done.13
  101.5 3.9 %collective-permute-done.12 = bf16[4,64,672]{2,1,0:T(8,128)(2,1)S(1)} collective-permute-done((bf16[4,64,672]{2,1,0:T(8,128)(2,1)S(1)}, bf16[4,64,672]{2,1,0:T(8,128)(2,1)S(1)}, u32[]{:S(2)}, u32[]{:S(2)}) %collective-permute-start.12) | collective-permute-done | bytes 344096 | tf_op jit(solution)/shard_map/scatter_xy/ppermute | solution.py:33
  105.5 0.2 fusion.14
  105.7 0.6 collective-permute-start.14
  106.4 2.0 %collective-permute-start.16 = (bf16[64,672]{1,0:T(8,128)(2,1)S(1)}, bf16[64,672]{1,0:T(8,128)(2,1)S(1)}, u32[]{:S(2)}, u32[]{:S(2)}) collective-permute-start(bf16[64,672]{1,0:T(8,128)(2,1)S(1)} %get-tuple-element.27), channel_id=1, source_target_pairs={{0,16},{1,5},{2,18},{3,7},{4,20},{5,1},{6,22},{7,3},{8,24},{9,13},... | collective-permute-start | bytes 258056 | tf_op jit(solution)/shard_map/scatter_yx/ppermute | solution.py:33
  108.4 1.3 %collective-permute-start.15 = (bf16[64,672]{1,0:T(8,128)(2,1)S(1)}, bf16[64,672]{1,0:T(8,128)(2,1)S(1)}, u32[]{:S(2)}, u32[]{:S(2)}) collective-permute-start(bf16[64,672]{1,0:T(8,128)(2,1)S(1)} %get-tuple-element.28), channel_id=1, source_target_pairs={{0,24},{1,7},{2,26},{3,1},{4,28},{5,3},{6,30},{7,5},{8,0},{9,15},{... | collective-permute-start | bytes 258056 | tf_op jit(solution)/shard_map/scatter_yx/ppermute | solution.py:33
  109.6 3.1 %collective-permute-done.14 = bf16[64,672]{1,0:T(8,128)(2,1)S(1)} collective-permute-done((bf16[64,672]{1,0:T(8,128)(2,1)S(1)}, bf16[64,672]{1,0:T(8,128)(2,1)S(1)}, u32[]{:S(2)}, u32[]{:S(2)}) %collective-permute-start.14) | collective-permute-done | bytes 86048 | tf_op jit(solution)/shard_map/scatter_yx/ppermute | solution.py:33
  112.7 0.0 collective-permute-done.16
  112.7 0.9 collective-permute-done.15
  113.6 12.2 %all_to_all.23 = f32[8,8,672]{2,1,0:T(8,128)S(1)} all-to-all(f32[8,8,672]{2,1,0:T(8,128)S(1)} %fusion.13), channel_id=1, replica_groups=mesh['z'=8,'y'=4,'x'=4,'c'=2] {'z'}, dimensions={0} | all-to-all | bytes 344064 | tf_op jit(solution)/shard_map/scatter_z/all_to_all | solution.py:53
  125.8 0.6 reduce_sum.9
  (4 shorter events, 0.1 us)
Async XLA Ops:
  19.6 7.9 %collective-permute-start.2 = (bf16[672,128]{1,0:T(8,128)(2,1)S(1)}, bf16[672,128]{1,0:T(8,128)(2,1)S(1)}, u32[]{:S(2)}, u32[]{:S(2)}) collective-permute-start(bf16[672,128]{1,0:T(8,128)(2,1)S(1)} %gather_z.1), channel_id=1, source_target_pairs={{0,24},{1,7},{2,26},{3,1},{4,28},{5,3},{6,30},{7,5},{8,0},{9,15},{... | collective-permute-start | bytes 516104 | tf_op jit(solution)/shard_map/gather_yx/ppermute | solution.py:33
  22.7 7.0 %collective-permute-start.1 = (bf16[672,128]{1,0:T(8,128)(2,1)S(1)}, bf16[672,128]{1,0:T(8,128)(2,1)S(1)}, u32[]{:S(2)}, u32[]{:S(2)}) collective-permute-start(bf16[672,128]{1,0:T(8,128)(2,1)S(1)} %gather_z.1), channel_id=1, source_target_pairs={{0,16},{1,5},{2,18},{3,7},{4,20},{5,1},{6,22},{7,3},{8,24},{9,13},... | collective-permute-start | bytes 516104 | tf_op jit(solution)/shard_map/gather_yx/ppermute | solution.py:33
  23.3 8.1 %collective-permute-start = (bf16[672,128]{1,0:T(8,128)(2,1)S(1)}, bf16[672,128]{1,0:T(8,128)(2,1)S(1)}, u32[]{:S(2)}, u32[]{:S(2)}) collective-permute-start(bf16[672,128]{1,0:T(8,128)(2,1)S(1)} %gather_z.1), channel_id=1, source_target_pairs={{0,8},{1,3},{2,10},{3,5},{4,12},{5,7},{6,14},{7,1},{8,16},{9,11},{... | collective-permute-start | bytes 516104 | tf_op jit(solution)/shard_map/gather_yx/ppermute | solution.py:33
  31.6 19.6 %collective-permute-start.5 = (bf16[4,672,128]{2,1,0:T(8,128)(2,1)S(1)}, bf16[4,672,128]{2,1,0:T(8,128)(2,1)S(1)}, u32[]{:S(2)}, u32[]{:S(2)}) collective-permute-start(bf16[4,672,128]{2,1,0:T(8,128)(2,1)S(1)} %pad_maximum_fusion._.refs_0_), channel_id=1, source_target_pairs={{0,6},{1,25},{2,0},{3,27},{4,2},{5,29},{6,4},{7,31},{8,14},{9,1},{... | collective-permute-start | bytes 2064392 | tf_op jit(solution)/shard_map/gather_xy/ppermute | solution.py:33
  32.5 18.7 %collective-permute-start.4 = (bf16[4,672,128]{2,1,0:T(8,128)(2,1)S(1)}, bf16[4,672,128]{2,1,0:T(8,128)(2,1)S(1)}, u32[]{:S(2)}, u32[]{:S(2)}) collective-permute-start(bf16[4,672,128]{2,1,0:T(8,128)(2,1)S(1)} %pad_maximum_fusion._.refs_0_), channel_id=1, source_target_pairs={{0,2},{1,9},{2,4},{3,11},{4,6},{5,13},{6,0},{7,15},{8,10},{9,17},{... | collective-permute-start | bytes 2064392 | tf_op jit(solution)/shard_map/gather_xy/ppermute | solution.py:33
  34.9 16.8 %collective-permute-start.3 = (bf16[4,672,128]{2,1,0:T(8,128)(2,1)S(1)}, bf16[4,672,128]{2,1,0:T(8,128)(2,1)S(1)}, u32[]{:S(2)}, u32[]{:S(2)}) collective-permute-start(bf16[4,672,128]{2,1,0:T(8,128)(2,1)S(1)} %pad_maximum_fusion._.refs_0_), channel_id=1, source_target_pairs={{0,4},{1,17},{2,6},{3,19},{4,0},{5,21},{6,2},{7,23},{8,12},{9,25},... | collective-permute-start | bytes 2064392 | tf_op jit(solution)/shard_map/gather_xy/ppermute | solution.py:33
  39.2 12.6 %collective-permute-start.6 = (bf16[4,672,128]{2,1,0:T(8,128)(2,1)S(1)}, bf16[4,672,128]{2,1,0:T(8,128)(2,1)S(1)}, u32[]{:S(2)}, u32[]{:S(2)}) collective-permute-start(bf16[4,672,128]{2,1,0:T(8,128)(2,1)S(1)} %pad_maximum_fusion._.refs_0_), channel_id=1, source_target_pairs={{0,1},{1,0},{2,3},{3,2},{4,5},{5,4},{6,7},{7,6},{8,9},{9,8},{10,11... | collective-permute-start | bytes 2064392 | tf_op jit(solution)/shard_map/gather_xy/ppermute | solution.py:33
  51.2 2.1 %collective-permute-start.9 = (bf16[4,672,128]{2,1,0:T(8,128)(2,1)S(1)}, bf16[4,672,128]{2,1,0:T(8,128)(2,1)S(1)}, u32[]{:S(2)}, u32[]{:S(2)}) collective-permute-start(bf16[4,672,128]{2,1,0:T(8,128)(2,1)S(1)} %collective-permute-done.5.refs_3_), channel_id=1, source_target_pairs={{0,1},{1,0},{2,3},{3,2},{4,5},{5,4},{6,7},{7,6},{8,9},{9,8},{10,11... | collective-permute-start | bytes 2064392 | tf_op jit(solution)/shard_map/gather_xy/ppermute | solution.py:33
  51.2 3.1 %collective-permute-start.8 = (bf16[4,672,128]{2,1,0:T(8,128)(2,1)S(1)}, bf16[4,672,128]{2,1,0:T(8,128)(2,1)S(1)}, u32[]{:S(2)}, u32[]{:S(2)}) collective-permute-start(bf16[4,672,128]{2,1,0:T(8,128)(2,1)S(1)} %collective-permute-done.4.refs_2_), channel_id=1, source_target_pairs={{0,1},{1,0},{2,3},{3,2},{4,5},{5,4},{6,7},{7,6},{8,9},{9,8},{10,11... | collective-permute-start | bytes 2064392 | tf_op jit(solution)/shard_map/gather_xy/ppermute | solution.py:33
  51.7 3.6 %collective-permute-start.7 = (bf16[4,672,128]{2,1,0:T(8,128)(2,1)S(1)}, bf16[4,672,128]{2,1,0:T(8,128)(2,1)S(1)}, u32[]{:S(2)}, u32[]{:S(2)}) collective-permute-start(bf16[4,672,128]{2,1,0:T(8,128)(2,1)S(1)} %collective-permute-done.3.refs_1_), channel_id=1, source_target_pairs={{0,1},{1,0},{2,3},{3,2},{4,5},{5,4},{6,7},{7,6},{8,9},{9,8},{10,11... | collective-permute-start | bytes 2064392 | tf_op jit(solution)/shard_map/gather_xy/ppermute | solution.py:33
  86.0 3.5 %collective-permute-start.10 = (bf16[4,4,64,672]{3,2,1,0:T(8,128)(2,1)S(1)}, bf16[4,4,64,672]{3,2,1,0:T(8,128)(2,1)S(1)}, u32[]{:S(2)}, u32[]{:S(2)}) collective-permute-start(bf16[4,4,64,672]{3,2,1,0:T(8,128)(2,1)S(1)} %get-tuple-element.20), channel_id=1, source_target_pairs={{0,1},{1,0},{2,3},{3,2},{4,5},{5,4},{6,7},{7,6},{8,9},{9,8},{10,11... | collective-permute-start | bytes 4128776 | tf_op jit(solution)/shard_map/product/ppermute | solution.py:33
  89.8 11.7 %collective-permute-start.11 = (bf16[4,64,672]{2,1,0:T(8,128)(2,1)S(1)}, bf16[4,64,672]{2,1,0:T(8,128)(2,1)S(1)}, u32[]{:S(2)}, u32[]{:S(2)}) collective-permute-start(bf16[4,64,672]{2,1,0:T(8,128)(2,1)S(1)} %get-tuple-element.23), channel_id=1, source_target_pairs={{0,2},{1,9},{2,4},{3,11},{4,6},{5,13},{6,0},{7,15},{8,10},{9,17},{... | collective-permute-start | bytes 1032200 | tf_op jit(solution)/shard_map/scatter_xy/ppermute | solution.py:33
  92.0 9.5 %collective-permute-start.13 = (bf16[4,64,672]{2,1,0:T(8,128)(2,1)S(1)}, bf16[4,64,672]{2,1,0:T(8,128)(2,1)S(1)}, u32[]{:S(2)}, u32[]{:S(2)}) collective-permute-start(bf16[4,64,672]{2,1,0:T(8,128)(2,1)S(1)} %get-tuple-element.24), channel_id=1, source_target_pairs={{0,4},{1,17},{2,6},{3,19},{4,0},{5,21},{6,2},{7,23},{8,12},{9,25},... | collective-permute-start | bytes 1032200 | tf_op jit(solution)/shard_map/scatter_xy/ppermute | solution.py:33
  92.7 12.8 %collective-permute-start.12 = (bf16[4,64,672]{2,1,0:T(8,128)(2,1)S(1)}, bf16[4,64,672]{2,1,0:T(8,128)(2,1)S(1)}, u32[]{:S(2)}, u32[]{:S(2)}) collective-permute-start(bf16[4,64,672]{2,1,0:T(8,128)(2,1)S(1)} %get-tuple-element.25), channel_id=1, source_target_pairs={{0,6},{1,25},{2,0},{3,27},{4,2},{5,29},{6,4},{7,31},{8,14},{9,1},{... | collective-permute-start | bytes 1032200 | tf_op jit(solution)/shard_map/scatter_xy/ppermute | solution.py:33
  105.7 7.0 %collective-permute-start.14 = (bf16[64,672]{1,0:T(8,128)(2,1)S(1)}, bf16[64,672]{1,0:T(8,128)(2,1)S(1)}, u32[]{:S(2)}, u32[]{:S(2)}) collective-permute-start(bf16[64,672]{1,0:T(8,128)(2,1)S(1)} %get-tuple-element.26), channel_id=1, source_target_pairs={{0,8},{1,3},{2,10},{3,5},{4,12},{5,7},{6,14},{7,1},{8,16},{9,11},{... | collective-permute-start | bytes 258056 | tf_op jit(solution)/shard_map/scatter_yx/ppermute | solution.py:33
  106.4 6.3 %collective-permute-start.16 = (bf16[64,672]{1,0:T(8,128)(2,1)S(1)}, bf16[64,672]{1,0:T(8,128)(2,1)S(1)}, u32[]{:S(2)}, u32[]{:S(2)}) collective-permute-start(bf16[64,672]{1,0:T(8,128)(2,1)S(1)} %get-tuple-element.27), channel_id=1, source_target_pairs={{0,16},{1,5},{2,18},{3,7},{4,20},{5,1},{6,22},{7,3},{8,24},{9,13},... | collective-permute-start | bytes 258056 | tf_op jit(solution)/shard_map/scatter_yx/ppermute | solution.py:33
  108.4 5.2 %collective-permute-start.15 = (bf16[64,672]{1,0:T(8,128)(2,1)S(1)}, bf16[64,672]{1,0:T(8,128)(2,1)S(1)}, u32[]{:S(2)}, u32[]{:S(2)}) collective-permute-start(bf16[64,672]{1,0:T(8,128)(2,1)S(1)} %get-tuple-element.28), channel_id=1, source_target_pairs={{0,24},{1,7},{2,26},{3,1},{4,28},{5,3},{6,30},{7,5},{8,0},{9,15},{... | collective-permute-start | bytes 258056 | tf_op jit(solution)/shard_map/scatter_yx/ppermute | solution.py:33

commit v6 on v5

--- a/solution.py
+++ b/solution.py
@@ -33,6 +33,10 @@
     return lax.ppermute(value, AXES, perm(move))
 
 
+def along_x(k):
+    return lambda z, y, x, c: (z, y, x + k, c)
+
+
 def along_yx(k):
     return lambda z, y, x, c: (z, y + k, x, c) if c == 0 else (z, y, x + k, c)
 
@@ -46,7 +50,6 @@
 
 
 HOPS = (1, 3, 2)
-PLACE = (0, 2, 1, 3)
 
 
 def all_of(value, axes):
@@ -66,8 +69,8 @@
 
 
 def scores_kernel(*refs):
-    own, theirs = refs[:NQ], refs[NQ : 2 * NQ]
-    w, raised, slopes, stats, tops, whole = refs[2 * NQ :]
+    own, theirs = refs[:5], refs[5:10]
+    w, raised, slopes, stats, whole = refs[10:]
     width, lanes = own[0].shape[1:]
     y, x, c = lax.axis_index("y"), lax.axis_index("x"), lax.axis_index("c")
     for pieces, parity in ((own, c), (theirs, 1 - c)):
@@ -79,7 +82,16 @@
                 y_at = lax.rem(y + NQ - y_back, NQ)
                 first = pl.multiple_of((2 * x_at + parity) * width, width)
                 column = pl.multiple_of(y_at * lanes, lanes)
-                whole[pl.ds(first, width), pl.ds(column, lanes)] = pieces[PLACE[k]][r]
+                same, near, far, behind, ahead = pieces
+                if k == 0:
+                    piece = same[r]
+                elif k == 2:
+                    piece = (near, far)[r // 2][r % 2]
+                elif r == 0:
+                    piece = same[NQ + k // 2]
+                else:
+                    piece = (behind, ahead)[k // 2][r - 1]
+                whole[pl.ds(first, width), pl.ds(column, lanes)] = piece
 
     both = jnp.dot(w[...], whole[...], preferred_element_type=F32)
     low = lax.broadcasted_iota(jnp.int32, (both.shape[0], lanes), 1) < lanes // 2
@@ -95,9 +107,7 @@
     raised[...] = value
     total = jnp.sum(value, axis=0, keepdims=True)
     dotted = jnp.sum(value * slopes[...], axis=0, keepdims=True)
-    own_stats = jnp.concatenate((top, total, dotted, dotted), 0)
-    stats[...] = jnp.broadcast_to(own_stats[None], stats.shape)
-    tops[...] = jnp.broadcast_to(top, tops.shape)
+    stats[...] = jnp.concatenate((top, total, dotted, dotted), 0)
 
 
 def merged(parts):
@@ -109,10 +119,11 @@
     return top, total, dotted
 
 
-def merge_kernel(parts, out):
-    top, total, dotted = merged(parts[...])
+def merge_kernel(*refs):
+    *parts, out = refs
+    top, total, dotted = merged(jnp.stack([part[...] for part in parts]))
     own = jnp.concatenate((top, total, dotted, dotted), 0)
-    out[...] = jnp.broadcast_to(own[None], out.shape)
+    out[...] = jnp.broadcast_to(own, out.shape)
 
 
 def part_product(mixture, w, parity, out):
@@ -167,10 +178,10 @@
             compiler_params=pltpu.CompilerParams(vmem_limit_bytes=4 * MIB),
         )(block)
     with jax.named_scope("gather_yx"):
-        pieces = {0: block}
-        for k in HOPS:
-            pieces[k] = send(block, along_yx(k))
-        block = jnp.stack([pieces[k] for k in range(NQ)])
+        pieces = {k: send(block, along_yx(k)) for k in HOPS}
+        early = [send(block, along_xy(k)) for k in (1, 3)]
+        pieces[1], *early = lax.optimization_barrier((pieces[1], *early))
+        late = jnp.stack([pieces[k] for k in range(1, NQ)])
         weight = pl.pallas_call(
             load_kernel,
             out_shape=pltpu.VMEM((vocab, features), BF),
@@ -181,38 +192,44 @@
                 flops=0, transcendentals=0, bytes_accessed=4 * vocab * features
             ),
             compiler_params=pltpu.CompilerParams(vmem_limit_bytes=MIB),
-        )(pltpu.with_memory_space_constraint(out_weight, pltpu.HBM), block)
+        )(pltpu.with_memory_space_constraint(out_weight, pltpu.HBM), late)
     with jax.named_scope("gather_xy"):
-        pieces = {0: block}
-        for k in HOPS:
-            pieces[k] = send(block, along_xy(k))
-        pieces[0], weight = lax.optimization_barrier((pieces[0], weight))
-        theirs = {k: send(pieces[k], other_core) for k in (0,) + HOPS}
+        behind, ahead = send(late, along_xy(1)), send(late, along_xy(3))
+        pieces[0] = block
+        across = [send(jnp.stack((pieces[k], pieces[k + 1])), along_xy(2)) for k in (0, 2)]
+        same = jnp.stack((*(pieces[k] for k in range(NQ)), *early))
+        same, weight = lax.optimization_barrier((same, weight))
+        own = [same, *across, behind, ahead]
+        theirs = [send(piece, other_core) for piece in own]
 
     with jax.named_scope("scores"):
-        raised, slopes, stats, top = pl.pallas_call(
+        raised, slopes, mine = pl.pallas_call(
             scores_kernel,
             out_shape=(
                 shape((vocab, tokens), F32),
                 shape((vocab, tokens), F32),
-                shape((NQ * NQ, 4, tokens), F32),
                 shape((4, tokens), F32),
             ),
-            in_specs=[VMEM] * (2 * NQ + 1),
-            out_specs=(VMEM,) * 4,
+            in_specs=[VMEM] * 11,
+            out_specs=(VMEM,) * 3,
             scratch_shapes=[pltpu.VMEM((features, 2 * tokens), BF)],
             compiler_params=pltpu.CompilerParams(vmem_limit_bytes=20 * MIB),
-        )(*(pieces[k] for k in PLACE), *(theirs[k] for k in PLACE), weight)
+        )(*own, *theirs, weight)
 
     with jax.named_scope("statistics"):
-        stats = pl.pallas_call(
-            merge_kernel,
-            out_shape=shape((2 * NZ, 4, tokens), F32),
-            in_specs=[VMEM],
-            out_specs=VMEM,
-            compiler_params=pltpu.CompilerParams(vmem_limit_bytes=4 * MIB),
-        )(all_of(stats, ("y", "x")))
-        parts = all_of(stats, ("z", "c"))
+
+        def merge(parts, *copies):
+            return pl.pallas_call(
+                merge_kernel,
+                out_shape=shape((*copies, 4, tokens), F32),
+                in_specs=[VMEM] * len(parts),
+                out_specs=VMEM,
+                compiler_params=pltpu.CompilerParams(vmem_limit_bytes=4 * MIB),
+            )(*parts)
+
+        chip = merge([mine, send(mine, other_core)])
+        row = merge([chip, *(send(chip, along_x(k)) for k in HOPS)], NZ * NQ)
+        parts = all_of(row, ("z", "y"))
 
     with jax.named_scope("product"):
         give, mixture = pl.pallas_call(
@@ -224,7 +241,7 @@
             in_specs=[VMEM] * 5,
             out_specs=(VMEM, VMEM),
             compiler_params=pltpu.CompilerParams(vmem_limit_bytes=8 * MIB),
-        )(parts, top, raised, slopes, weight)
+        )(parts, mine, raised, slopes, weight)
         got = send(give, other_core)
         keep = pl.pallas_call(
             keep_kernel,

time: 127 us -> 129 us (1.016)
  starting transfers between devices: 16.8 us -> 26.2 us
  blocking collectives: 51.7 us -> 46.6 us
  waiting for transfers between devices: 39.5 us -> 37 us
    ppermute x17 -> x25, starting transfers between devices: 16.8 us -> 26.2 us  [send(): return lax.ppermute(value, AXES, perm(move))]
    all_to_all x4 -> x3, blocking collectives: 51.7 us -> 46.6 us  [all_of(): return lax.all_to_all(value, axes, 0, 0)]
    ppermute x17 -> x25, waiting for transfers between devices: 39.5 us -> 37 us  [send(): return lax.ppermute(value, AXES, perm(move))]
  transfers between devices with their start and end apart: 17 -> 25, of which waited for: 12 -> 14; matrix products, arithmetic and copies ran while one was open for 0% -> 0% of each run, Pallas kernels for 5% -> 5%
where the time goes in v6:
time: 129 us
  blocking collectives  46.6 us (36%)
  waiting for transfers between devices  37 us (29%)
  starting transfers between devices  26.2 us (20%)
  Pallas kernels  16.3 us (13%)
  other arithmetic  2.09 us (2%)
    all_to_all x3, blocking collectives, all_of(): return lax.all_to_all(value, axes, 0, 0)  46.6 us
    ppermute x25, waiting for transfers between devices, send(): return lax.ppermute(value, AXES, perm(move))  37 us
    ppermute x25, starting transfers between devices, send(): return lax.ppermute(value, AXES, perm(move))  26.2 us
    pallas_call x1, Pallas kernels, per_device(): pl.pallas_call(scores_kernel, out_shape=(shape((vocab, tokens), F32), sha...  7.54 us
    pallas_call x1, Pallas kernels, per_device(): pl.pallas_call(load_kernel, out_shape=pltpu.VMEM((vocab, features), BF),...  4.14 us
  transfers between devices with their start and end apart: 25, of which 14 were waited for; matrix products, arithmetic and copies ran while one was open for 0% of the time, Pallas kernels for 5%

profile of v6, /device:TPU:6, one launch (start us, length us, event | category | flops | bytes accessed | tf_op | source)
XLA Modules:
  0.0 128.5 jit_solution(1422431050148831830)
XLA Ops:
  0.0 0.7 pad_maximum_fusion.3
  0.8 18.7 %all_to_all.15.block = bf16[8,2,8,672]{3,2,1,0:T(8,128)(2,1)S(1)} all-to-all(bf16[8,2,8,672]{3,2,1,0:T(8,128)(2,1)S(1)} %broadcast_in_dim.2), channel_id=1, replica_groups=mesh['z'=8,'y'=4,'x'=4,'c'=2] {'z'}, dimensions={0} | all-to-all | bytes 344064 | tf_op jit(solution)/shard_map/gather_z/all_to_all | solution.py:56
  19.5 0.1 gather_z.1
  19.6 3.1 %collective-permute-start.4 = (bf16[672,128]{1,0:T(8,128)(2,1)S(1)}, bf16[672,128]{1,0:T(8,128)(2,1)S(1)}, u32[]{:S(2)}, u32[]{:S(2)}) collective-permute-start(bf16[672,128]{1,0:T(8,128)(2,1)S(1)} %gather_z.1), channel_id=1, source_target_pairs={{0,24},{1,7},{2,26},{3,1},{4,28},{5,3},{6,30},{7,5},{8,0},{9,15},{... | collective-permute-start | bytes 516104 | tf_op jit(solution)/shard_map/gather_yx/ppermute | solution.py:33
  22.7 0.6 collective-permute-start.3
  23.3 0.8 collective-permute-start.2
  24.2 2.4 %collective-permute-start.1 = (bf16[672,128]{1,0:T(8,128)(2,1)S(1)}, bf16[672,128]{1,0:T(8,128)(2,1)S(1)}, u32[]{:S(2)}, u32[]{:S(2)}) collective-permute-start(bf16[672,128]{1,0:T(8,128)(2,1)S(1)} %gather_z.1), channel_id=1, source_target_pairs={{0,2},{1,9},{2,4},{3,11},{4,6},{5,13},{6,0},{7,15},{8,10},{9,17},{... | collective-permute-start | bytes 516104 | tf_op jit(solution)/shard_map/gather_yx/ppermute | solution.py:33
  26.6 1.0 collective-permute-start
  27.6 2.4 %collective-permute-done.2 = bf16[672,128]{1,0:T(8,128)(2,1)S(1)} collective-permute-done((bf16[672,128]{1,0:T(8,128)(2,1)S(1)}, bf16[672,128]{1,0:T(8,128)(2,1)S(1)}, u32[]{:S(2)}, u32[]{:S(2)}) %collective-permute-start.2) | collective-permute-done | bytes 172064 | tf_op jit(solution)/shard_map/gather_yx/ppermute | solution.py:33
  30.0 0.0 collective-permute-done.1
  30.0 3.2 %collective-permute-done = bf16[672,128]{1,0:T(8,128)(2,1)S(1)} collective-permute-done((bf16[672,128]{1,0:T(8,128)(2,1)S(1)}, bf16[672,128]{1,0:T(8,128)(2,1)S(1)}, u32[]{:S(2)}, u32[]{:S(2)}) %collective-permute-start) | collective-permute-done | bytes 172064 | tf_op jit(solution)/shard_map/gather_yx/ppermute | solution.py:33
  33.2 0.0 collective-permute-done.4
  33.2 0.0 collective-permute-done.3
  33.2 0.1 pad_maximum_fusion._
  33.3 0.1 collective-permute-start.8
  33.4 3.2 %collective-permute-start.7 = (bf16[3,672,128]{2,1,0:T(8,128)(2,1)S(1)}, bf16[3,672,128]{2,1,0:T(8,128)(2,1)S(1)}, u32[]{:S(2)}, u32[]{:S(2)}) collective-permute-start(bf16[3,672,128]{2,1,0:T(8,128)(2,1)S(1)} %pad_maximum_fusion._), channel_id=1, source_target_pairs={{0,2},{1,9},{2,4},{3,11},{4,6},{5,13},{6,0},{7,15},{8,10},{9,17},{... | collective-permute-start | bytes 1548296 | tf_op jit(solution)/shard_map/gather_xy/ppermute | solution.py:33
  36.7 4.1 %gather_yx.1.refs_10_.w = bf16[1024,5376]{1,0:T(8,128)(2,1)S(1)} custom-call(bf16[1024,5376]{1,0:T(8,128)(2,1)} %w.1, bf16[3,672,128]{2,1,0:T(8,128)(2,1)S(1)} %pad_maximum_fusion._), custom_call_target="tpu_custom_call" | custom-call | bytes 22020096 | tf_op jit(solution)/shard_map/gather_yx/pallas_call | solution.py:185
  40.9 0.1 collective-permute-start.9
  41.0 0.1 collective-permute-start.6
  41.2 3.6 %collective-permute-start.5 = (bf16[2,672,128]{2,1,0:T(8,128)(2,1)S(1)}, bf16[2,672,128]{2,1,0:T(8,128)(2,1)S(1)}, u32[]{:S(2)}, u32[]{:S(2)}) collective-permute-start(bf16[2,672,128]{2,1,0:T(8,128)(2,1)S(1)} %pad_maximum_fusion.1), channel_id=1, source_target_pairs={{0,4},{1,17},{2,6},{3,19},{4,0},{5,21},{6,2},{7,23},{8,12},{9,25},... | collective-permute-start | bytes 1032200 | tf_op jit(solution)/shard_map/gather_xy/ppermute | solution.py:33
  44.8 0.0 collective-permute-done.8.refs_4_
  44.8 0.3 collective-permute-start.13
  45.1 5.5 %collective-permute-done.7.refs_3_ = bf16[3,672,128]{2,1,0:T(8,128)(2,1)S(1)} collective-permute-done((bf16[3,672,128]{2,1,0:T(8,128)(2,1)S(1)}, bf16[3,672,128]{2,1,0:T(8,128)(2,1)S(1)}, u32[]{:S(2)}, u32[]{:S(2)}) %collective-permute-start.7) | collective-permute-done | bytes 516128 | tf_op jit(solution)/shard_map/gather_xy/ppermute | solution.py:33
  50.6 0.0 collective-permute-start.12
  50.6 0.0 collective-permute-done.6.refs_2_
  50.6 0.5 collective-permute-start.11
  51.1 2.4 %collective-permute-done.5.refs_1_ = bf16[2,672,128]{2,1,0:T(8,128)(2,1)S(1)} collective-permute-done((bf16[2,672,128]{2,1,0:T(8,128)(2,1)S(1)}, bf16[2,672,128]{2,1,0:T(8,128)(2,1)S(1)}, u32[]{:S(2)}, u32[]{:S(2)}) %collective-permute-start.5) | collective-permute-done | bytes 344096 | tf_op jit(solution)/shard_map/gather_xy/ppermute | solution.py:33
  53.6 0.0 collective-permute-start.10
  53.6 0.0 collective-permute-done.11.refs_7_
  53.6 1.6 %collective-permute-done.10.refs_6_ = bf16[2,672,128]{2,1,0:T(8,128)(2,1)S(1)} collective-permute-done((bf16[2,672,128]{2,1,0:T(8,128)(2,1)S(1)}, bf16[2,672,128]{2,1,0:T(8,128)(2,1)S(1)}, u32[]{:S(2)}, u32[]{:S(2)}) %collective-permute-start.10) | collective-permute-done | bytes 344096 | tf_op jit(solution)/shard_map/gather_xy/ppermute | solution.py:33
  55.2 0.0 collective-permute-done.13.refs_9_
  55.2 0.0 collective-permute-done.12.refs_8_
  55.2 0.0 collective-permute-done.9.refs_5_
  55.2 7.5 %scores.1 = (f32[1024,256]{1,0:T(8,128)S(1)}, f32[1024,256]{1,0:T(8,128)S(1)}, f32[4,256]{1,0:T(4,128)S(1)}) custom-call(bf16[6,672,128]{2,1,0:T(8,128)(2,1)S(1)} %bitcast_dynamic-update-slice_fusion.refs_0_, bf16[2,672,128]{2,1,0:T(8,128)(2,1)S(1)} %collective-permute-done.5.refs_1_, bf16[2,672,128]{2,1,0:T(8,128)(2,1)S(1)} %collective-permute-done.6.refs_2_, ...), custom_call_target="tpu_custom_call" | custom-call | tf_op jit(solution)/shard_map/scores/pallas_call | solution.py:206
  62.8 0.2 collective-permute-start.14
  63.0 1.0 collective-permute-done.14.refs_1_
  64.0 0.1 collective-permute-start.17
  64.2 2.8 %collective-permute-start.16 = (f32[4,256]{1,0:T(4,128)S(1)}, f32[4,256]{1,0:T(4,128)S(1)}, u32[]{:S(2)}, u32[]{:S(2)}) collective-permute-start(f32[4,256]{1,0:T(4,128)S(1)} %statistics.2.refs_0_), channel_id=1, source_target_pairs={{0,6},{1,7},{2,0},{3,1},{4,2},{5,3},{6,4},{7,5},{8,14},{9,15},{10,... | collective-permute-start | bytes 12296 | tf_op jit(solution)/shard_map/statistics/ppermute | solution.py:33
  66.9 0.5 collective-permute-start.15
  67.5 1.8 %collective-permute-done.17.refs_3_ = f32[4,256]{1,0:T(4,128)S(1)} collective-permute-done((f32[4,256]{1,0:T(4,128)S(1)}, f32[4,256]{1,0:T(4,128)S(1)}, u32[]{:S(2)}, u32[]{:S(2)}) %collective-permute-start.17) | collective-permute-done | bytes 4128 | tf_op jit(solution)/shard_map/statistics/ppermute | solution.py:33
  69.2 0.0 collective-permute-done.16.refs_2_
  69.3 1.3 collective-permute-done.15.refs_1_
  70.6 15.7 %all_to_all.16.parts = f32[32,4,256]{2,1,0:T(4,128)S(1)} all-to-all(f32[32,4,256]{2,1,0:T(4,128)S(1)} %statistics.3), channel_id=1, replica_groups=mesh['z'=8,'y'=4,'x'=4,'c'=2] {'z','y'}, dimensions={0} | all-to-all | bytes 262144 | tf_op jit(solution)/shard_map/statistics/all_to_all | solution.py:56
  86.2 2.2 %product.2 = (bf16[4,4,64,672]{3,2,1,0:T(8,128)(2,1)S(1)}, bf16[256,1024]{1,0:T(8,128)(2,1)S(1)}) custom-call(f32[32,4,256]{2,1,0:T(4,128)S(1)} %all_to_all.16.parts, f32[4,256]{1,0:T(4,128)S(1)} %get-tuple-element.20.refs_0_.own_top, f32[1024,256]{1,0:T(8,128)S(1)} %get-tuple-element.21.raised, f32[1024,256]{1,0:T(8,128)S(1)} %get-tuple-element.22.slopes, ...), custom_call_target="tpu_custom_call" | custom-call | tf_op jit(solution)/shard_map/product/pallas_call | solution.py:235
  88.4 0.1 collective-permute-start.18
  88.5 2.2 %product.3 = f32[4,4,64,672]{3,2,1,0:T(8,128)S(1)} custom-call(bf16[256,1024]{1,0:T(8,128)(2,1)S(1)} %get-tuple-element.23.mixture, bf16[1024,5376]{1,0:T(8,128)(2,1)S(1)} %gather_yx.1.refs_10_.w), custom_call_target="tpu_custom_call" | custom-call | flops 1409286144 | bytes 11010048 | tf_op jit(solution)/shard_map/product/pallas_call | solution.py:246
  90.8 1.2 collective-permute-done.18
  91.9 0.3 fusion.7
  92.3 1.8 %collective-permute-start.19 = (bf16[4,64,672]{2,1,0:T(8,128)(2,1)S(1)}, bf16[4,64,672]{2,1,0:T(8,128)(2,1)S(1)}, u32[]{:S(2)}, u32[]{:S(2)}) collective-permute-start(bf16[4,64,672]{2,1,0:T(8,128)(2,1)S(1)} %get-tuple-element.27), channel_id=1, source_target_pairs={{0,2},{1,9},{2,4},{3,11},{4,6},{5,13},{6,0},{7,15},{8,10},{9,17},{... | collective-permute-start | bytes 1032200 | tf_op jit(solution)/shard_map/scatter_xy/ppermute | solution.py:33
  94.1 0.9 collective-permute-start.21
  95.0 0.0 collective-permute-start.20
  95.0 5.1 %collective-permute-done.19 = bf16[4,64,672]{2,1,0:T(8,128)(2,1)S(1)} collective-permute-done((bf16[4,64,672]{2,1,0:T(8,128)(2,1)S(1)}, bf16[4,64,672]{2,1,0:T(8,128)(2,1)S(1)}, u32[]{:S(2)}, u32[]{:S(2)}) %collective-permute-start.19) | collective-permute-done | bytes 344096 | tf_op jit(solution)/shard_map/scatter_xy/ppermute | solution.py:33
  100.1 3.3 %collective-permute-done.21 = bf16[4,64,672]{2,1,0:T(8,128)(2,1)S(1)} collective-permute-done((bf16[4,64,672]{2,1,0:T(8,128)(2,1)S(1)}, bf16[4,64,672]{2,1,0:T(8,128)(2,1)S(1)}, u32[]{:S(2)}, u32[]{:S(2)}) %collective-permute-start.21) | collective-permute-done | bytes 344096 | tf_op jit(solution)/shard_map/scatter_xy/ppermute | solution.py:33
  103.5 4.1 %collective-permute-done.20 = bf16[4,64,672]{2,1,0:T(8,128)(2,1)S(1)} collective-permute-done((bf16[4,64,672]{2,1,0:T(8,128)(2,1)S(1)}, bf16[4,64,672]{2,1,0:T(8,128)(2,1)S(1)}, u32[]{:S(2)}, u32[]{:S(2)}) %collective-permute-start.20) | collective-permute-done | bytes 344096 | tf_op jit(solution)/shard_map/scatter_xy/ppermute | solution.py:33
  107.6 0.2 fusion.14
  107.8 0.2 collective-permute-start.22
  108.0 2.7 %collective-permute-start.24 = (bf16[64,672]{1,0:T(8,128)(2,1)S(1)}, bf16[64,672]{1,0:T(8,128)(2,1)S(1)}, u32[]{:S(2)}, u32[]{:S(2)}) collective-permute-start(bf16[64,672]{1,0:T(8,128)(2,1)S(1)} %get-tuple-element.31), channel_id=1, source_target_pairs={{0,16},{1,5},{2,18},{3,7},{4,20},{5,1},{6,22},{7,3},{8,24},{9,13},... | collective-permute-start | bytes 258056 | tf_op jit(solution)/shard_map/scatter_yx/ppermute | solution.py:33
  110.7 1.0 collective-permute-start.23
  111.7 3.1 %collective-permute-done.22 = bf16[64,672]{1,0:T(8,128)(2,1)S(1)} collective-permute-done((bf16[64,672]{1,0:T(8,128)(2,1)S(1)}, bf16[64,672]{1,0:T(8,128)(2,1)S(1)}, u32[]{:S(2)}, u32[]{:S(2)}) %collective-permute-start.22) | collective-permute-done | bytes 86048 | tf_op jit(solution)/shard_map/scatter_yx/ppermute | solution.py:33
  114.8 0.0 collective-permute-done.24
  114.8 0.9 collective-permute-done.23
  115.7 12.2 %all_to_all.17 = f32[8,8,672]{2,1,0:T(8,128)S(1)} all-to-all(f32[8,8,672]{2,1,0:T(8,128)S(1)} %fusion.13), channel_id=1, replica_groups=mesh['z'=8,'y'=4,'x'=4,'c'=2] {'z'}, dimensions={0} | all-to-all | bytes 344064 | tf_op jit(solution)/shard_map/scatter_z/all_to_all | solution.py:56
  127.9 0.6 reduce_sum.9
  (13 shorter events, 0.3 us)
Async XLA Ops:
  19.6 13.6 %collective-permute-start.4 = (bf16[672,128]{1,0:T(8,128)(2,1)S(1)}, bf16[672,128]{1,0:T(8,128)(2,1)S(1)}, u32[]{:S(2)}, u32[]{:S(2)}) collective-permute-start(bf16[672,128]{1,0:T(8,128)(2,1)S(1)} %gather_z.1), channel_id=1, source_target_pairs={{0,24},{1,7},{2,26},{3,1},{4,28},{5,3},{6,30},{7,5},{8,0},{9,15},{... | collective-permute-start | bytes 516104 | tf_op jit(solution)/shard_map/gather_yx/ppermute | solution.py:33
  22.7 10.5 %collective-permute-start.3 = (bf16[672,128]{1,0:T(8,128)(2,1)S(1)}, bf16[672,128]{1,0:T(8,128)(2,1)S(1)}, u32[]{:S(2)}, u32[]{:S(2)}) collective-permute-start(bf16[672,128]{1,0:T(8,128)(2,1)S(1)} %gather_z.1), channel_id=1, source_target_pairs={{0,16},{1,5},{2,18},{3,7},{4,20},{5,1},{6,22},{7,3},{8,24},{9,13},... | collective-permute-start | bytes 516104 | tf_op jit(solution)/shard_map/gather_yx/ppermute | solution.py:33
  23.3 6.6 %collective-permute-start.2 = (bf16[672,128]{1,0:T(8,128)(2,1)S(1)}, bf16[672,128]{1,0:T(8,128)(2,1)S(1)}, u32[]{:S(2)}, u32[]{:S(2)}) collective-permute-start(bf16[672,128]{1,0:T(8,128)(2,1)S(1)} %gather_z.1), channel_id=1, source_target_pairs={{0,6},{1,25},{2,0},{3,27},{4,2},{5,29},{6,4},{7,31},{8,14},{9,1},{... | collective-permute-start | bytes 516104 | tf_op jit(solution)/shard_map/gather_yx/ppermute | solution.py:33
  24.2 5.8 %collective-permute-start.1 = (bf16[672,128]{1,0:T(8,128)(2,1)S(1)}, bf16[672,128]{1,0:T(8,128)(2,1)S(1)}, u32[]{:S(2)}, u32[]{:S(2)}) collective-permute-start(bf16[672,128]{1,0:T(8,128)(2,1)S(1)} %gather_z.1), channel_id=1, source_target_pairs={{0,2},{1,9},{2,4},{3,11},{4,6},{5,13},{6,0},{7,15},{8,10},{9,17},{... | collective-permute-start | bytes 516104 | tf_op jit(solution)/shard_map/gather_yx/ppermute | solution.py:33
  26.6 6.6 %collective-permute-start = (bf16[672,128]{1,0:T(8,128)(2,1)S(1)}, bf16[672,128]{1,0:T(8,128)(2,1)S(1)}, u32[]{:S(2)}, u32[]{:S(2)}) collective-permute-start(bf16[672,128]{1,0:T(8,128)(2,1)S(1)} %gather_z.1), channel_id=1, source_target_pairs={{0,8},{1,3},{2,10},{3,5},{4,12},{5,7},{6,14},{7,1},{8,16},{9,11},{... | collective-permute-start | bytes 516104 | tf_op jit(solution)/shard_map/gather_yx/ppermute | solution.py:33
  33.3 11.5 %collective-permute-start.8 = (bf16[3,672,128]{2,1,0:T(8,128)(2,1)S(1)}, bf16[3,672,128]{2,1,0:T(8,128)(2,1)S(1)}, u32[]{:S(2)}, u32[]{:S(2)}) collective-permute-start(bf16[3,672,128]{2,1,0:T(8,128)(2,1)S(1)} %pad_maximum_fusion._), channel_id=1, source_target_pairs={{0,6},{1,25},{2,0},{3,27},{4,2},{5,29},{6,4},{7,31},{8,14},{9,1},{... | collective-permute-start | bytes 1548296 | tf_op jit(solution)/shard_map/gather_xy/ppermute | solution.py:33
  33.4 17.2 %collective-permute-start.7 = (bf16[3,672,128]{2,1,0:T(8,128)(2,1)S(1)}, bf16[3,672,128]{2,1,0:T(8,128)(2,1)S(1)}, u32[]{:S(2)}, u32[]{:S(2)}) collective-permute-start(bf16[3,672,128]{2,1,0:T(8,128)(2,1)S(1)} %pad_maximum_fusion._), channel_id=1, source_target_pairs={{0,2},{1,9},{2,4},{3,11},{4,6},{5,13},{6,0},{7,15},{8,10},{9,17},{... | collective-permute-start | bytes 1548296 | tf_op jit(solution)/shard_map/gather_xy/ppermute | solution.py:33
  40.9 14.3 %collective-permute-start.9 = (bf16[6,672,128]{2,1,0:T(8,128)(2,1)S(1)}, bf16[6,672,128]{2,1,0:T(8,128)(2,1)S(1)}, u32[]{:S(2)}, u32[]{:S(2)}) collective-permute-start(bf16[6,672,128]{2,1,0:T(8,128)(2,1)S(1)} %bitcast_dynamic-update-slice_fusion.refs_0_), channel_id=1, source_target_pairs={{0,1},{1,0},{2,3},{3,2},{4,5},{5,4},{6,7},{7,6},{8,9},{9,8},{10,11... | collective-permute-start | bytes 3096584 | tf_op jit(solution)/shard_map/gather_xy/ppermute | solution.py:33
  41.0 9.6 %collective-permute-start.6 = (bf16[2,672,128]{2,1,0:T(8,128)(2,1)S(1)}, bf16[2,672,128]{2,1,0:T(8,128)(2,1)S(1)}, u32[]{:S(2)}, u32[]{:S(2)}) collective-permute-start(bf16[2,672,128]{2,1,0:T(8,128)(2,1)S(1)} %pad_maximum_fusion.2), channel_id=1, source_target_pairs={{0,4},{1,17},{2,6},{3,19},{4,0},{5,21},{6,2},{7,23},{8,12},{9,25},... | collective-permute-start | bytes 1032200 | tf_op jit(solution)/shard_map/gather_xy/ppermute | solution.py:33
  41.2 12.4 %collective-permute-start.5 = (bf16[2,672,128]{2,1,0:T(8,128)(2,1)S(1)}, bf16[2,672,128]{2,1,0:T(8,128)(2,1)S(1)}, u32[]{:S(2)}, u32[]{:S(2)}) collective-permute-start(bf16[2,672,128]{2,1,0:T(8,128)(2,1)S(1)} %pad_maximum_fusion.1), channel_id=1, source_target_pairs={{0,4},{1,17},{2,6},{3,19},{4,0},{5,21},{6,2},{7,23},{8,12},{9,25},... | collective-permute-start | bytes 1032200 | tf_op jit(solution)/shard_map/gather_xy/ppermute | solution.py:33
  44.8 10.4 %collective-permute-start.13 = (bf16[3,672,128]{2,1,0:T(8,128)(2,1)S(1)}, bf16[3,672,128]{2,1,0:T(8,128)(2,1)S(1)}, u32[]{:S(2)}, u32[]{:S(2)}) collective-permute-start(bf16[3,672,128]{2,1,0:T(8,128)(2,1)S(1)} %collective-permute-done.8.refs_4_), channel_id=1, source_target_pairs={{0,1},{1,0},{2,3},{3,2},{4,5},{5,4},{6,7},{7,6},{8,9},{9,8},{10,11... | collective-permute-start | bytes 1548296 | tf_op jit(solution)/shard_map/gather_xy/ppermute | solution.py:33
  50.6 4.6 %collective-permute-start.12 = (bf16[3,672,128]{2,1,0:T(8,128)(2,1)S(1)}, bf16[3,672,128]{2,1,0:T(8,128)(2,1)S(1)}, u32[]{:S(2)}, u32[]{:S(2)}) collective-permute-start(bf16[3,672,128]{2,1,0:T(8,128)(2,1)S(1)} %collective-permute-done.7.refs_3_), channel_id=1, source_target_pairs={{0,1},{1,0},{2,3},{3,2},{4,5},{5,4},{6,7},{7,6},{8,9},{9,8},{10,11... | collective-permute-start | bytes 1548296 | tf_op jit(solution)/shard_map/gather_xy/ppermute | solution.py:33
  50.6 3.0 %collective-permute-start.11 = (bf16[2,672,128]{2,1,0:T(8,128)(2,1)S(1)}, bf16[2,672,128]{2,1,0:T(8,128)(2,1)S(1)}, u32[]{:S(2)}, u32[]{:S(2)}) collective-permute-start(bf16[2,672,128]{2,1,0:T(8,128)(2,1)S(1)} %collective-permute-done.6.refs_2_), channel_id=1, source_target_pairs={{0,1},{1,0},{2,3},{3,2},{4,5},{5,4},{6,7},{7,6},{8,9},{9,8},{10,11... | collective-permute-start | bytes 1032200 | tf_op jit(solution)/shard_map/gather_xy/ppermute | solution.py:33
  53.6 1.7 %collective-permute-start.10 = (bf16[2,672,128]{2,1,0:T(8,128)(2,1)S(1)}, bf16[2,672,128]{2,1,0:T(8,128)(2,1)S(1)}, u32[]{:S(2)}, u32[]{:S(2)}) collective-permute-start(bf16[2,672,128]{2,1,0:T(8,128)(2,1)S(1)} %collective-permute-done.5.refs_1_), channel_id=1, source_target_pairs={{0,1},{1,0},{2,3},{3,2},{4,5},{5,4},{6,7},{7,6},{8,9},{9,8},{10,11... | collective-permute-start | bytes 1032200 | tf_op jit(solution)/shard_map/gather_xy/ppermute | solution.py:33
  62.8 1.3 collective-permute-start.14
  64.0 5.2 %collective-permute-start.17 = (f32[4,256]{1,0:T(4,128)S(1)}, f32[4,256]{1,0:T(4,128)S(1)}, u32[]{:S(2)}, u32[]{:S(2)}) collective-permute-start(f32[4,256]{1,0:T(4,128)S(1)} %statistics.2.refs_0_), channel_id=1, source_target_pairs={{0,4},{1,5},{2,6},{3,7},{4,0},{5,1},{6,2},{7,3},{8,12},{9,13},{10,... | collective-permute-start | bytes 12296 | tf_op jit(solution)/shard_map/statistics/ppermute | solution.py:33
  64.2 5.1 %collective-permute-start.16 = (f32[4,256]{1,0:T(4,128)S(1)}, f32[4,256]{1,0:T(4,128)S(1)}, u32[]{:S(2)}, u32[]{:S(2)}) collective-permute-start(f32[4,256]{1,0:T(4,128)S(1)} %statistics.2.refs_0_), channel_id=1, source_target_pairs={{0,6},{1,7},{2,0},{3,1},{4,2},{5,3},{6,4},{7,5},{8,14},{9,15},{10,... | collective-permute-start | bytes 12296 | tf_op jit(solution)/shard_map/statistics/ppermute | solution.py:33
  66.9 3.6 %collective-permute-start.15 = (f32[4,256]{1,0:T(4,128)S(1)}, f32[4,256]{1,0:T(4,128)S(1)}, u32[]{:S(2)}, u32[]{:S(2)}) collective-permute-start(f32[4,256]{1,0:T(4,128)S(1)} %statistics.2.refs_0_), channel_id=1, source_target_pairs={{0,2},{1,3},{2,4},{3,5},{4,6},{5,7},{6,0},{7,1},{8,10},{9,11},{10,... | collective-permute-start | bytes 12296 | tf_op jit(solution)/shard_map/statistics/ppermute | solution.py:33
  88.4 3.5 %collective-permute-start.18 = (bf16[4,4,64,672]{3,2,1,0:T(8,128)(2,1)S(1)}, bf16[4,4,64,672]{3,2,1,0:T(8,128)(2,1)S(1)}, u32[]{:S(2)}, u32[]{:S(2)}) collective-permute-start(bf16[4,4,64,672]{3,2,1,0:T(8,128)(2,1)S(1)} %get-tuple-element.24), channel_id=1, source_target_pairs={{0,1},{1,0},{2,3},{3,2},{4,5},{5,4},{6,7},{7,6},{8,9},{9,8},{10,11... | collective-permute-start | bytes 4128776 | tf_op jit(solution)/shard_map/product/ppermute | solution.py:33
  92.3 7.9 %collective-permute-start.19 = (bf16[4,64,672]{2,1,0:T(8,128)(2,1)S(1)}, bf16[4,64,672]{2,1,0:T(8,128)(2,1)S(1)}, u32[]{:S(2)}, u32[]{:S(2)}) collective-permute-start(bf16[4,64,672]{2,1,0:T(8,128)(2,1)S(1)} %get-tuple-element.27), channel_id=1, source_target_pairs={{0,2},{1,9},{2,4},{3,11},{4,6},{5,13},{6,0},{7,15},{8,10},{9,17},{... | collective-permute-start | bytes 1032200 | tf_op jit(solution)/shard_map/scatter_xy/ppermute | solution.py:33
  94.1 9.4 %collective-permute-start.21 = (bf16[4,64,672]{2,1,0:T(8,128)(2,1)S(1)}, bf16[4,64,672]{2,1,0:T(8,128)(2,1)S(1)}, u32[]{:S(2)}, u32[]{:S(2)}) collective-permute-start(bf16[4,64,672]{2,1,0:T(8,128)(2,1)S(1)} %get-tuple-element.28), channel_id=1, source_target_pairs={{0,4},{1,17},{2,6},{3,19},{4,0},{5,21},{6,2},{7,23},{8,12},{9,25},... | collective-permute-start | bytes 1032200 | tf_op jit(solution)/shard_map/scatter_xy/ppermute | solution.py:33
  95.0 12.6 %collective-permute-start.20 = (bf16[4,64,672]{2,1,0:T(8,128)(2,1)S(1)}, bf16[4,64,672]{2,1,0:T(8,128)(2,1)S(1)}, u32[]{:S(2)}, u32[]{:S(2)}) collective-permute-start(bf16[4,64,672]{2,1,0:T(8,128)(2,1)S(1)} %get-tuple-element.29), channel_id=1, source_target_pairs={{0,6},{1,25},{2,0},{3,27},{4,2},{5,29},{6,4},{7,31},{8,14},{9,1},{... | collective-permute-start | bytes 1032200 | tf_op jit(solution)/shard_map/scatter_xy/ppermute | solution.py:33
  107.8 7.0 %collective-permute-start.22 = (bf16[64,672]{1,0:T(8,128)(2,1)S(1)}, bf16[64,672]{1,0:T(8,128)(2,1)S(1)}, u32[]{:S(2)}, u32[]{:S(2)}) collective-permute-start(bf16[64,672]{1,0:T(8,128)(2,1)S(1)} %get-tuple-element.30), channel_id=1, source_target_pairs={{0,8},{1,3},{2,10},{3,5},{4,12},{5,7},{6,14},{7,1},{8,16},{9,11},{... | collective-permute-start | bytes 258056 | tf_op jit(solution)/shard_map/scatter_yx/ppermute | solution.py:33
  108.0 6.8 %collective-permute-start.24 = (bf16[64,672]{1,0:T(8,128)(2,1)S(1)}, bf16[64,672]{1,0:T(8,128)(2,1)S(1)}, u32[]{:S(2)}, u32[]{:S(2)}) collective-permute-start(bf16[64,672]{1,0:T(8,128)(2,1)S(1)} %get-tuple-element.31), channel_id=1, source_target_pairs={{0,16},{1,5},{2,18},{3,7},{4,20},{5,1},{6,22},{7,3},{8,24},{9,13},... | collective-permute-start | bytes 258056 | tf_op jit(solution)/shard_map/scatter_yx/ppermute | solution.py:33
  110.7 5.0 %collective-permute-start.23 = (bf16[64,672]{1,0:T(8,128)(2,1)S(1)}, bf16[64,672]{1,0:T(8,128)(2,1)S(1)}, u32[]{:S(2)}, u32[]{:S(2)}) collective-permute-start(bf16[64,672]{1,0:T(8,128)(2,1)S(1)} %get-tuple-element.32), channel_id=1, source_target_pairs={{0,24},{1,7},{2,26},{3,1},{4,28},{5,3},{6,30},{7,5},{8,0},{9,15},{... | collective-permute-start | bytes 258056 | tf_op jit(solution)/shard_map/scatter_yx/ppermute | solution.py:33

commit v7 on v5

--- a/solution.py
+++ b/solution.py
@@ -46,7 +46,6 @@
 
 
 HOPS = (1, 3, 2)
-PLACE = (0, 2, 1, 3)
 
 
 def all_of(value, axes):
@@ -66,8 +65,8 @@
 
 
 def scores_kernel(*refs):
-    own, theirs = refs[:NQ], refs[NQ : 2 * NQ]
-    w, raised, slopes, stats, tops, whole = refs[2 * NQ :]
+    own, theirs = refs[:5], refs[5:10]
+    w, raised, slopes, stats, tops, whole = refs[10:]
     width, lanes = own[0].shape[1:]
     y, x, c = lax.axis_index("y"), lax.axis_index("x"), lax.axis_index("c")
     for pieces, parity in ((own, c), (theirs, 1 - c)):
@@ -79,7 +78,12 @@
                 y_at = lax.rem(y + NQ - y_back, NQ)
                 first = pl.multiple_of((2 * x_at + parity) * width, width)
                 column = pl.multiple_of(y_at * lanes, lanes)
-                whole[pl.ds(first, width), pl.ds(column, lanes)] = pieces[PLACE[k]][r]
+                far, near, behind, ahead, same = pieces
+                if k == 2:
+                    piece = (near, far)[r // 2][r % 2]
+                else:
+                    piece = (same, behind, None, ahead)[k][r]
+                whole[pl.ds(first, width), pl.ds(column, lanes)] = piece
 
     both = jnp.dot(w[...], whole[...], preferred_element_type=F32)
     low = lax.broadcasted_iota(jnp.int32, (both.shape[0], lanes), 1) < lanes // 2
@@ -183,11 +187,13 @@
             compiler_params=pltpu.CompilerParams(vmem_limit_bytes=MIB),
         )(pltpu.with_memory_space_constraint(out_weight, pltpu.HBM), block)
     with jax.named_scope("gather_xy"):
-        pieces = {0: block}
-        for k in HOPS:
-            pieces[k] = send(block, along_xy(k))
-        pieces[0], weight = lax.optimization_barrier((pieces[0], weight))
-        theirs = {k: send(pieces[k], other_core) for k in (0,) + HOPS}
+        ahead = send(block, along_xy(3))
+        near = send(block[: NQ // 2], along_xy(2))
+        behind = send(block, along_xy(1))
+        far = send(ahead[NQ // 2 :], along_xy(3))
+        same, weight = lax.optimization_barrier((block, weight))
+        own = [far, near, behind, ahead, same]
+        theirs = [send(piece, other_core) for piece in own]
 
     with jax.named_scope("scores"):
         raised, slopes, stats, top = pl.pallas_call(
@@ -198,11 +204,11 @@
                 shape((NQ * NQ, 4, tokens), F32),
                 shape((4, tokens), F32),
             ),
-            in_specs=[VMEM] * (2 * NQ + 1),
+            in_specs=[VMEM] * 11,
             out_specs=(VMEM,) * 4,
             scratch_shapes=[pltpu.VMEM((features, 2 * tokens), BF)],
             compiler_params=pltpu.CompilerParams(vmem_limit_bytes=20 * MIB),
-        )(*(pieces[k] for k in PLACE), *(theirs[k] for k in PLACE), weight)
+        )(*own, *theirs, weight)
 
     with jax.named_scope("statistics"):
         stats = pl.pallas_call(

time: 127 us -> 129 us (1.016)
  waiting for transfers between devices: 39.5 us -> 41.6 us
    ppermute x17 -> x19, waiting for transfers between devices: 39.5 us -> 41.6 us  [send(): return lax.ppermute(value, AXES, perm(move))]
    ppermute x17 -> x19, starting transfers between devices: 16.8 us -> 17.3 us  [send(): return lax.ppermute(value, AXES, perm(move))]
  transfers between devices with their start and end apart: 17 -> 19, of which waited for: 12 -> 11; matrix products, arithmetic and copies ran while one was open for 0% -> 0% of each run, Pallas kernels for 5% -> 5%
where the time goes in v7:
time: 129 us
  blocking collectives  51.6 us (40%)
  waiting for transfers between devices  41.6 us (32%)
  starting transfers between devices  17.3 us (13%)
  Pallas kernels  16 us (12%)
  other arithmetic  2.08 us (2%)
    all_to_all x4, blocking collectives, all_of(): return lax.all_to_all(value, axes, 0, 0)  51.6 us
    ppermute x19, waiting for transfers between devices, send(): return lax.ppermute(value, AXES, perm(move))  41.6 us
    ppermute x19, starting transfers between devices, send(): return lax.ppermute(value, AXES, perm(move))  17.3 us
    pallas_call x1, Pallas kernels, per_device(): pl.pallas_call(scores_kernel, out_shape=(shape((vocab, tokens), F32), sha...  7.54 us
    pallas_call x1, Pallas kernels, per_device(): pl.pallas_call(load_kernel, out_shape=pltpu.VMEM((vocab, features), BF),...  4.14 us
  transfers between devices with their start and end apart: 19, of which 11 were waited for; matrix products, arithmetic and copies ran while one was open for 0% of the time, Pallas kernels for 5%

profile of v7, /device:TPU:6, one launch (start us, length us, event | category | flops | bytes accessed | tf_op | source)
XLA Modules:
  0.0 128.7 jit_solution(14800830391436470537)
XLA Ops:
  0.0 0.7 pad_maximum_fusion.2
  0.8 18.7 %all_to_all.20.block = bf16[8,2,8,672]{3,2,1,0:T(8,128)(2,1)S(1)} all-to-all(bf16[8,2,8,672]{3,2,1,0:T(8,128)(2,1)S(1)} %broadcast_in_dim.2), channel_id=1, replica_groups=mesh['z'=8,'y'=4,'x'=4,'c'=2] {'z'}, dimensions={0} | all-to-all | bytes 344064 | tf_op jit(solution)/shard_map/gather_z/all_to_all | solution.py:52
  19.5 0.1 gather_z.1
  19.6 3.1 %collective-permute-start.2 = (bf16[672,128]{1,0:T(8,128)(2,1)S(1)}, bf16[672,128]{1,0:T(8,128)(2,1)S(1)}, u32[]{:S(2)}, u32[]{:S(2)}) collective-permute-start(bf16[672,128]{1,0:T(8,128)(2,1)S(1)} %gather_z.1), channel_id=1, source_target_pairs={{0,24},{1,7},{2,26},{3,1},{4,28},{5,3},{6,30},{7,5},{8,0},{9,15},{... | collective-permute-start | bytes 516104 | tf_op jit(solution)/shard_map/gather_yx/ppermute | solution.py:33
  22.7 0.6 collective-permute-start.1
  23.3 1.0 collective-permute-start
  24.3 3.2 %collective-permute-done.2 = bf16[672,128]{1,0:T(8,128)(2,1)S(1)} collective-permute-done((bf16[672,128]{1,0:T(8,128)(2,1)S(1)}, bf16[672,128]{1,0:T(8,128)(2,1)S(1)}, u32[]{:S(2)}, u32[]{:S(2)}) %collective-permute-start.2) | collective-permute-done | bytes 172064 | tf_op jit(solution)/shard_map/gather_yx/ppermute | solution.py:33
  27.5 2.2 %collective-permute-done.1 = bf16[672,128]{1,0:T(8,128)(2,1)S(1)} collective-permute-done((bf16[672,128]{1,0:T(8,128)(2,1)S(1)}, bf16[672,128]{1,0:T(8,128)(2,1)S(1)}, u32[]{:S(2)}, u32[]{:S(2)}) %collective-permute-start.1) | collective-permute-done | bytes 172064 | tf_op jit(solution)/shard_map/gather_yx/ppermute | solution.py:33
  29.7 1.7 %collective-permute-done = bf16[672,128]{1,0:T(8,128)(2,1)S(1)} collective-permute-done((bf16[672,128]{1,0:T(8,128)(2,1)S(1)}, bf16[672,128]{1,0:T(8,128)(2,1)S(1)}, u32[]{:S(2)}, u32[]{:S(2)}) %collective-permute-start) | collective-permute-done | bytes 172064 | tf_op jit(solution)/shard_map/gather_yx/ppermute | solution.py:33
  31.5 0.1 pad_maximum_fusion._.refs_4_
  31.6 0.9 collective-permute-start.3
  32.5 2.4 %collective-permute-start.6 = (bf16[4,672,128]{2,1,0:T(8,128)(2,1)S(1)}, bf16[4,672,128]{2,1,0:T(8,128)(2,1)S(1)}, u32[]{:S(2)}, u32[]{:S(2)}) collective-permute-start(bf16[4,672,128]{2,1,0:T(8,128)(2,1)S(1)} %pad_maximum_fusion._.refs_4_), channel_id=1, source_target_pairs={{0,2},{1,9},{2,4},{3,11},{4,6},{5,13},{6,0},{7,15},{8,10},{9,17},{... | collective-permute-start | bytes 2064392 | tf_op jit(solution)/shard_map/gather_xy/ppermute | solution.py:33
  34.9 0.3 collective-permute-start.5
  35.2 4.1 %gather_yx.1.refs_10_.w = bf16[1024,5376]{1,0:T(8,128)(2,1)S(1)} custom-call(bf16[1024,5376]{1,0:T(8,128)(2,1)} %w.1, bf16[4,672,128]{2,1,0:T(8,128)(2,1)S(1)} %pad_maximum_fusion._.refs_4_), custom_call_target="tpu_custom_call" | custom-call | bytes 22020096 | tf_op jit(solution)/shard_map/gather_yx/pallas_call | solution.py:178
  39.3 0.1 collective-permute-start.11
  39.4 8.0 %collective-permute-done.3.refs_3_ = bf16[4,672,128]{2,1,0:T(8,128)(2,1)S(1)} collective-permute-done((bf16[4,672,128]{2,1,0:T(8,128)(2,1)S(1)}, bf16[4,672,128]{2,1,0:T(8,128)(2,1)S(1)}, u32[]{:S(2)}, u32[]{:S(2)}) %collective-permute-start.3) | collective-permute-done | bytes 688160 | tf_op jit(solution)/shard_map/gather_xy/ppermute | solution.py:33
  47.5 0.1 collective-permute-start.4
  47.6 0.0 collective-permute-done.6.refs_2_
  47.6 0.1 collective-permute-start.9
  47.7 0.5 collective-permute-start.10
  48.2 0.0 collective-permute-done.5.refs_1_
  48.2 0.1 collective-permute-start.8
  48.3 7.7 %collective-permute-done.4.refs_0_ = bf16[2,672,128]{2,1,0:T(8,128)(2,1)S(1)} collective-permute-done((bf16[2,672,128]{2,1,0:T(8,128)(2,1)S(1)}, bf16[2,672,128]{2,1,0:T(8,128)(2,1)S(1)}, u32[]{:S(2)}, u32[]{:S(2)}) %collective-permute-start.4) | collective-permute-done | bytes 344096 | tf_op jit(solution)/shard_map/gather_xy/ppermute | solution.py:33
  56.0 0.0 collective-permute-start.7
  56.0 0.0 collective-permute-done.8.refs_6_
  56.0 0.0 collective-permute-done.11.refs_9_
  56.0 0.0 collective-permute-done.9.refs_7_
  56.1 1.6 %collective-permute-done.7.refs_5_ = bf16[2,672,128]{2,1,0:T(8,128)(2,1)S(1)} collective-permute-done((bf16[2,672,128]{2,1,0:T(8,128)(2,1)S(1)}, bf16[2,672,128]{2,1,0:T(8,128)(2,1)S(1)}, u32[]{:S(2)}, u32[]{:S(2)}) %collective-permute-start.7) | collective-permute-done | bytes 344096 | tf_op jit(solution)/shard_map/gather_xy/ppermute | solution.py:33
  57.7 0.0 collective-permute-done.10.refs_8_
  57.7 7.5 %scores.1 = (f32[1024,256]{1,0:T(8,128)S(1)}, f32[1024,256]{1,0:T(8,128)S(1)}, f32[16,4,256]{2,1,0:T(4,128)S(1)}, f32[4,256]{1,0:T(4,128)S(1)}) custom-call(bf16[2,672,128]{2,1,0:T(8,128)(2,1)S(1)} %collective-permute-done.4.refs_0_, bf16[2,672,128]{2,1,0:T(8,128)(2,1)S(1)} %collective-permute-done.5.refs_1_, ...), custom_call_target="tpu_custom_call" | custom-call | tf_op jit(solution)/shard_map/scores/pallas_call | solution.py:199
  65.2 10.3 %all_to_all.21.parts = f32[16,4,256]{2,1,0:T(4,128)S(1)} all-to-all(f32[16,4,256]{2,1,0:T(4,128)S(1)} %get-tuple-element.15), channel_id=1, replica_groups=mesh['z'=8,'y'=4,'x'=4,'c'=2] {'y','x'}, dimensions={0} | all-to-all | bytes 131072 | tf_op jit(solution)/shard_map/statistics/all_to_all | solution.py:52
  75.5 10.4 %all_to_all.22.parts = f32[16,4,256]{2,1,0:T(4,128)S(1)} all-to-all(f32[16,4,256]{2,1,0:T(4,128)S(1)} %statistics.1), channel_id=1, replica_groups=mesh['z'=8,'y'=4,'x'=4,'c'=2] {'z','c'}, dimensions={0} | all-to-all | bytes 131072 | tf_op jit(solution)/shard_map/statistics/all_to_all | solution.py:52
  85.9 2.2 %product.2 = (bf16[4,4,64,672]{3,2,1,0:T(8,128)(2,1)S(1)}, bf16[256,1024]{1,0:T(8,128)(2,1)S(1)}) custom-call(f32[16,4,256]{2,1,0:T(4,128)S(1)} %all_to_all.22.parts, f32[4,256]{1,0:T(4,128)S(1)} %get-tuple-element.16.own_top, f32[1024,256]{1,0:T(8,128)S(1)} %get-tuple-element.17.raised, f32[1024,256]{1,0:T(8,128)S(1)} %get-tuple-element.18.slopes, ...), custom_call_target="tpu_custom_call" | custom-call | tf_op jit(solution)/shard_map/product/pallas_call | solution.py:224
  88.1 0.5 collective-permute-start.12
  88.6 2.0 %product.3 = f32[4,4,64,672]{3,2,1,0:T(8,128)S(1)} custom-call(bf16[256,1024]{1,0:T(8,128)(2,1)S(1)} %get-tuple-element.19.mixture, bf16[1024,5376]{1,0:T(8,128)(2,1)S(1)} %gather_yx.1.refs_10_.w), custom_call_target="tpu_custom_call" | custom-call | flops 1409286144 | bytes 11010048 | tf_op jit(solution)/shard_map/product/pallas_call | solution.py:235
  90.6 1.0 collective-permute-done.12
  91.6 0.3 fusion.7
  91.9 2.4 %collective-permute-start.13 = (bf16[4,64,672]{2,1,0:T(8,128)(2,1)S(1)}, bf16[4,64,672]{2,1,0:T(8,128)(2,1)S(1)}, u32[]{:S(2)}, u32[]{:S(2)}) collective-permute-start(bf16[4,64,672]{2,1,0:T(8,128)(2,1)S(1)} %get-tuple-element.23), channel_id=1, source_target_pairs={{0,2},{1,9},{2,4},{3,11},{4,6},{5,13},{6,0},{7,15},{8,10},{9,17},{... | collective-permute-start | bytes 1032200 | tf_op jit(solution)/shard_map/scatter_xy/ppermute | solution.py:33
  94.3 0.7 collective-permute-start.15
  95.0 0.7 collective-permute-start.14
  95.7 8.1 %collective-permute-done.13 = bf16[4,64,672]{2,1,0:T(8,128)(2,1)S(1)} collective-permute-done((bf16[4,64,672]{2,1,0:T(8,128)(2,1)S(1)}, bf16[4,64,672]{2,1,0:T(8,128)(2,1)S(1)}, u32[]{:S(2)}, u32[]{:S(2)}) %collective-permute-start.13) | collective-permute-done | bytes 344096 | tf_op jit(solution)/shard_map/scatter_xy/ppermute | solution.py:33
  103.8 0.0 collective-permute-done.15
  103.8 3.9 %collective-permute-done.14 = bf16[4,64,672]{2,1,0:T(8,128)(2,1)S(1)} collective-permute-done((bf16[4,64,672]{2,1,0:T(8,128)(2,1)S(1)}, bf16[4,64,672]{2,1,0:T(8,128)(2,1)S(1)}, u32[]{:S(2)}, u32[]{:S(2)}) %collective-permute-start.14) | collective-permute-done | bytes 344096 | tf_op jit(solution)/shard_map/scatter_xy/ppermute | solution.py:33
  107.8 0.2 fusion.14
  108.1 0.6 collective-permute-start.16
  108.7 2.1 %collective-permute-start.18 = (bf16[64,672]{1,0:T(8,128)(2,1)S(1)}, bf16[64,672]{1,0:T(8,128)(2,1)S(1)}, u32[]{:S(2)}, u32[]{:S(2)}) collective-permute-start(bf16[64,672]{1,0:T(8,128)(2,1)S(1)} %get-tuple-element.27), channel_id=1, source_target_pairs={{0,16},{1,5},{2,18},{3,7},{4,20},{5,1},{6,22},{7,3},{8,24},{9,13},... | collective-permute-start | bytes 258056 | tf_op jit(solution)/shard_map/scatter_yx/ppermute | solution.py:33
  110.7 1.2 collective-permute-start.17
  112.0 3.1 %collective-permute-done.16 = bf16[64,672]{1,0:T(8,128)(2,1)S(1)} collective-permute-done((bf16[64,672]{1,0:T(8,128)(2,1)S(1)}, bf16[64,672]{1,0:T(8,128)(2,1)S(1)}, u32[]{:S(2)}, u32[]{:S(2)}) %collective-permute-start.16) | collective-permute-done | bytes 86048 | tf_op jit(solution)/shard_map/scatter_yx/ppermute | solution.py:33
  115.0 0.0 collective-permute-done.18
  115.0 0.9 collective-permute-done.17
  115.9 12.2 %all_to_all.23 = f32[8,8,672]{2,1,0:T(8,128)S(1)} all-to-all(f32[8,8,672]{2,1,0:T(8,128)S(1)} %fusion.13), channel_id=1, replica_groups=mesh['z'=8,'y'=4,'x'=4,'c'=2] {'z'}, dimensions={0} | all-to-all | bytes 344064 | tf_op jit(solution)/shard_map/scatter_z/all_to_all | solution.py:52
  128.1 0.6 reduce_sum.9
  (6 shorter events, 0.2 us)
Async XLA Ops:
  19.6 7.9 %collective-permute-start.2 = (bf16[672,128]{1,0:T(8,128)(2,1)S(1)}, bf16[672,128]{1,0:T(8,128)(2,1)S(1)}, u32[]{:S(2)}, u32[]{:S(2)}) collective-permute-start(bf16[672,128]{1,0:T(8,128)(2,1)S(1)} %gather_z.1), channel_id=1, source_target_pairs={{0,24},{1,7},{2,26},{3,1},{4,28},{5,3},{6,30},{7,5},{8,0},{9,15},{... | collective-permute-start | bytes 516104 | tf_op jit(solution)/shard_map/gather_yx/ppermute | solution.py:33
  22.7 7.0 %collective-permute-start.1 = (bf16[672,128]{1,0:T(8,128)(2,1)S(1)}, bf16[672,128]{1,0:T(8,128)(2,1)S(1)}, u32[]{:S(2)}, u32[]{:S(2)}) collective-permute-start(bf16[672,128]{1,0:T(8,128)(2,1)S(1)} %gather_z.1), channel_id=1, source_target_pairs={{0,16},{1,5},{2,18},{3,7},{4,20},{5,1},{6,22},{7,3},{8,24},{9,13},... | collective-permute-start | bytes 516104 | tf_op jit(solution)/shard_map/gather_yx/ppermute | solution.py:33
  23.3 8.1 %collective-permute-start = (bf16[672,128]{1,0:T(8,128)(2,1)S(1)}, bf16[672,128]{1,0:T(8,128)(2,1)S(1)}, u32[]{:S(2)}, u32[]{:S(2)}) collective-permute-start(bf16[672,128]{1,0:T(8,128)(2,1)S(1)} %gather_z.1), channel_id=1, source_target_pairs={{0,8},{1,3},{2,10},{3,5},{4,12},{5,7},{6,14},{7,1},{8,16},{9,11},{... | collective-permute-start | bytes 516104 | tf_op jit(solution)/shard_map/gather_yx/ppermute | solution.py:33
  31.6 15.9 %collective-permute-start.3 = (bf16[4,672,128]{2,1,0:T(8,128)(2,1)S(1)}, bf16[4,672,128]{2,1,0:T(8,128)(2,1)S(1)}, u32[]{:S(2)}, u32[]{:S(2)}) collective-permute-start(bf16[4,672,128]{2,1,0:T(8,128)(2,1)S(1)} %pad_maximum_fusion._.refs_4_), channel_id=1, source_target_pairs={{0,6},{1,25},{2,0},{3,27},{4,2},{5,29},{6,4},{7,31},{8,14},{9,1},{... | collective-permute-start | bytes 2064392 | tf_op jit(solution)/shard_map/gather_xy/ppermute | solution.py:33
  32.5 15.1 %collective-permute-start.6 = (bf16[4,672,128]{2,1,0:T(8,128)(2,1)S(1)}, bf16[4,672,128]{2,1,0:T(8,128)(2,1)S(1)}, u32[]{:S(2)}, u32[]{:S(2)}) collective-permute-start(bf16[4,672,128]{2,1,0:T(8,128)(2,1)S(1)} %pad_maximum_fusion._.refs_4_), channel_id=1, source_target_pairs={{0,2},{1,9},{2,4},{3,11},{4,6},{5,13},{6,0},{7,15},{8,10},{9,17},{... | collective-permute-start | bytes 2064392 | tf_op jit(solution)/shard_map/gather_xy/ppermute | solution.py:33
  34.9 13.3 %collective-permute-start.5 = (bf16[2,672,128]{2,1,0:T(8,128)(2,1)S(1)}, bf16[2,672,128]{2,1,0:T(8,128)(2,1)S(1)}, u32[]{:S(2)}, u32[]{:S(2)}) collective-permute-start(bf16[2,672,128]{2,1,0:T(8,128)(2,1)S(1)} %pad_maximum_fusion.1), channel_id=1, source_target_pairs={{0,4},{1,17},{2,6},{3,19},{4,0},{5,21},{6,2},{7,23},{8,12},{9,25},... | collective-permute-start | bytes 1032200 | tf_op jit(solution)/shard_map/gather_xy/ppermute | solution.py:33
  39.3 16.7 %collective-permute-start.11 = (bf16[4,672,128]{2,1,0:T(8,128)(2,1)S(1)}, bf16[4,672,128]{2,1,0:T(8,128)(2,1)S(1)}, u32[]{:S(2)}, u32[]{:S(2)}) collective-permute-start(bf16[4,672,128]{2,1,0:T(8,128)(2,1)S(1)} %pad_maximum_fusion._.refs_4_), channel_id=1, source_target_pairs={{0,1},{1,0},{2,3},{3,2},{4,5},{5,4},{6,7},{7,6},{8,9},{9,8},{10,11... | collective-permute-start | bytes 2064392 | tf_op jit(solution)/shard_map/gather_xy/ppermute | solution.py:33
  47.5 8.5 %collective-permute-start.4 = (bf16[2,672,128]{2,1,0:T(8,128)(2,1)S(1)}, bf16[2,672,128]{2,1,0:T(8,128)(2,1)S(1)}, u32[]{:S(2)}, u32[]{:S(2)}) collective-permute-start(bf16[2,672,128]{2,1,0:T(8,128)(2,1)S(1)} %slice.57), channel_id=1, source_target_pairs={{0,6},{1,25},{2,0},{3,27},{4,2},{5,29},{6,4},{7,31},{8,14},{9,1},{... | collective-permute-start | bytes 1032200 | tf_op jit(solution)/shard_map/gather_xy/ppermute | solution.py:33
  47.6 8.5 %collective-permute-start.9 = (bf16[4,672,128]{2,1,0:T(8,128)(2,1)S(1)}, bf16[4,672,128]{2,1,0:T(8,128)(2,1)S(1)}, u32[]{:S(2)}, u32[]{:S(2)}) collective-permute-start(bf16[4,672,128]{2,1,0:T(8,128)(2,1)S(1)} %collective-permute-done.6.refs_2_), channel_id=1, source_target_pairs={{0,1},{1,0},{2,3},{3,2},{4,5},{5,4},{6,7},{7,6},{8,9},{9,8},{10,11... | collective-permute-start | bytes 2064392 | tf_op jit(solution)/shard_map/gather_xy/ppermute | solution.py:33
  47.7 10.0 %collective-permute-start.10 = (bf16[4,672,128]{2,1,0:T(8,128)(2,1)S(1)}, bf16[4,672,128]{2,1,0:T(8,128)(2,1)S(1)}, u32[]{:S(2)}, u32[]{:S(2)}) collective-permute-start(bf16[4,672,128]{2,1,0:T(8,128)(2,1)S(1)} %collective-permute-done.3.refs_3_), channel_id=1, source_target_pairs={{0,1},{1,0},{2,3},{3,2},{4,5},{5,4},{6,7},{7,6},{8,9},{9,8},{10,11... | collective-permute-start | bytes 2064392 | tf_op jit(solution)/shard_map/gather_xy/ppermute | solution.py:33
  48.2 7.8 %collective-permute-start.8 = (bf16[2,672,128]{2,1,0:T(8,128)(2,1)S(1)}, bf16[2,672,128]{2,1,0:T(8,128)(2,1)S(1)}, u32[]{:S(2)}, u32[]{:S(2)}) collective-permute-start(bf16[2,672,128]{2,1,0:T(8,128)(2,1)S(1)} %collective-permute-done.5.refs_1_), channel_id=1, source_target_pairs={{0,1},{1,0},{2,3},{3,2},{4,5},{5,4},{6,7},{7,6},{8,9},{9,8},{10,11... | collective-permute-start | bytes 1032200 | tf_op jit(solution)/shard_map/gather_xy/ppermute | solution.py:33
  56.0 1.7 %collective-permute-start.7 = (bf16[2,672,128]{2,1,0:T(8,128)(2,1)S(1)}, bf16[2,672,128]{2,1,0:T(8,128)(2,1)S(1)}, u32[]{:S(2)}, u32[]{:S(2)}) collective-permute-start(bf16[2,672,128]{2,1,0:T(8,128)(2,1)S(1)} %collective-permute-done.4.refs_0_), channel_id=1, source_target_pairs={{0,1},{1,0},{2,3},{3,2},{4,5},{5,4},{6,7},{7,6},{8,9},{9,8},{10,11... | collective-permute-start | bytes 1032200 | tf_op jit(solution)/shard_map/gather_xy/ppermute | solution.py:33
  88.1 3.5 %collective-permute-start.12 = (bf16[4,4,64,672]{3,2,1,0:T(8,128)(2,1)S(1)}, bf16[4,4,64,672]{3,2,1,0:T(8,128)(2,1)S(1)}, u32[]{:S(2)}, u32[]{:S(2)}) collective-permute-start(bf16[4,4,64,672]{3,2,1,0:T(8,128)(2,1)S(1)} %get-tuple-element.20), channel_id=1, source_target_pairs={{0,1},{1,0},{2,3},{3,2},{4,5},{5,4},{6,7},{7,6},{8,9},{9,8},{10,11... | collective-permute-start | bytes 4128776 | tf_op jit(solution)/shard_map/product/ppermute | solution.py:33
  91.9 11.9 %collective-permute-start.13 = (bf16[4,64,672]{2,1,0:T(8,128)(2,1)S(1)}, bf16[4,64,672]{2,1,0:T(8,128)(2,1)S(1)}, u32[]{:S(2)}, u32[]{:S(2)}) collective-permute-start(bf16[4,64,672]{2,1,0:T(8,128)(2,1)S(1)} %get-tuple-element.23), channel_id=1, source_target_pairs={{0,2},{1,9},{2,4},{3,11},{4,6},{5,13},{6,0},{7,15},{8,10},{9,17},{... | collective-permute-start | bytes 1032200 | tf_op jit(solution)/shard_map/scatter_xy/ppermute | solution.py:33
  94.3 9.5 %collective-permute-start.15 = (bf16[4,64,672]{2,1,0:T(8,128)(2,1)S(1)}, bf16[4,64,672]{2,1,0:T(8,128)(2,1)S(1)}, u32[]{:S(2)}, u32[]{:S(2)}) collective-permute-start(bf16[4,64,672]{2,1,0:T(8,128)(2,1)S(1)} %get-tuple-element.24), channel_id=1, source_target_pairs={{0,4},{1,17},{2,6},{3,19},{4,0},{5,21},{6,2},{7,23},{8,12},{9,25},... | collective-permute-start | bytes 1032200 | tf_op jit(solution)/shard_map/scatter_xy/ppermute | solution.py:33
  95.0 12.8 %collective-permute-start.14 = (bf16[4,64,672]{2,1,0:T(8,128)(2,1)S(1)}, bf16[4,64,672]{2,1,0:T(8,128)(2,1)S(1)}, u32[]{:S(2)}, u32[]{:S(2)}) collective-permute-start(bf16[4,64,672]{2,1,0:T(8,128)(2,1)S(1)} %get-tuple-element.25), channel_id=1, source_target_pairs={{0,6},{1,25},{2,0},{3,27},{4,2},{5,29},{6,4},{7,31},{8,14},{9,1},{... | collective-permute-start | bytes 1032200 | tf_op jit(solution)/shard_map/scatter_xy/ppermute | solution.py:33
  108.1 7.0 %collective-permute-start.16 = (bf16[64,672]{1,0:T(8,128)(2,1)S(1)}, bf16[64,672]{1,0:T(8,128)(2,1)S(1)}, u32[]{:S(2)}, u32[]{:S(2)}) collective-permute-start(bf16[64,672]{1,0:T(8,128)(2,1)S(1)} %get-tuple-element.26), channel_id=1, source_target_pairs={{0,8},{1,3},{2,10},{3,5},{4,12},{5,7},{6,14},{7,1},{8,16},{9,11},{... | collective-permute-start | bytes 258056 | tf_op jit(solution)/shard_map/scatter_yx/ppermute | solution.py:33
  108.7 6.4 %collective-permute-start.18 = (bf16[64,672]{1,0:T(8,128)(2,1)S(1)}, bf16[64,672]{1,0:T(8,128)(2,1)S(1)}, u32[]{:S(2)}, u32[]{:S(2)}) collective-permute-start(bf16[64,672]{1,0:T(8,128)(2,1)S(1)} %get-tuple-element.27), channel_id=1, source_target_pairs={{0,16},{1,5},{2,18},{3,7},{4,20},{5,1},{6,22},{7,3},{8,24},{9,13},... | collective-permute-start | bytes 258056 | tf_op jit(solution)/shard_map/scatter_yx/ppermute | solution.py:33
  110.7 5.2 %collective-permute-start.17 = (bf16[64,672]{1,0:T(8,128)(2,1)S(1)}, bf16[64,672]{1,0:T(8,128)(2,1)S(1)}, u32[]{:S(2)}, u32[]{:S(2)}) collective-permute-start(bf16[64,672]{1,0:T(8,128)(2,1)S(1)} %get-tuple-element.28), channel_id=1, source_target_pairs={{0,24},{1,7},{2,26},{3,1},{4,28},{5,3},{6,30},{7,5},{8,0},{9,15},{... | collective-permute-start | bytes 258056 | tf_op jit(solution)/shard_map/scatter_yx/ppermute | solution.py:33

commit v8 on v7

--- a/solution.py
+++ b/solution.py
@@ -46,6 +46,7 @@
 
 
 HOPS = (1, 3, 2)
+BACK_HOPS = (2, 3, 1)
 
 
 def all_of(value, axes):
@@ -78,7 +79,7 @@
                 y_at = lax.rem(y + NQ - y_back, NQ)
                 first = pl.multiple_of((2 * x_at + parity) * width, width)
                 column = pl.multiple_of(y_at * lanes, lanes)
-                far, near, behind, ahead, same = pieces
+                near, far, behind, ahead, same = pieces
                 if k == 2:
                     piece = (near, far)[r // 2][r % 2]
                 else:
@@ -187,12 +188,10 @@
             compiler_params=pltpu.CompilerParams(vmem_limit_bytes=MIB),
         )(pltpu.with_memory_space_constraint(out_weight, pltpu.HBM), block)
     with jax.named_scope("gather_xy"):
-        ahead = send(block, along_xy(3))
-        near = send(block[: NQ // 2], along_xy(2))
-        behind = send(block, along_xy(1))
-        far = send(ahead[NQ // 2 :], along_xy(3))
+        ahead, behind = send(block, along_xy(3)), send(block, along_xy(1))
+        near, far = (send(half, along_xy(2)) for half in (block[: NQ // 2], block[NQ // 2 :]))
         same, weight = lax.optimization_barrier((block, weight))
-        own = [far, near, behind, ahead, same]
+        own = [near, far, behind, ahead, same]
         theirs = [send(piece, other_core) for piece in own]
 
     with jax.named_scope("scores"):
@@ -248,14 +247,15 @@
     with jax.named_scope("scatter_xy"):
         sums = [keep[k] + got[k].astype(F32) for k in range(NQ)]
         total = sums[0]
-        for k in HOPS:
+        for k in BACK_HOPS:
             total = total + send(sums[k].astype(BF), along_xy(k)).astype(F32)
     with jax.named_scope("scatter_yx"):
         total, rest = total[0], total
-        for k in HOPS:
+        for k in BACK_HOPS:
             total = total + send(rest[k].astype(BF), along_yx(k)).astype(F32)
     with jax.named_scope("scatter_z"):
-        return jnp.sum(all_of(total.reshape(NZ, rows, width), "z"), axis=0)
+        total = total.astype(BF).reshape(NZ, rows, width)
+        return jnp.sum(all_of(total, "z").astype(F32), axis=0)
 
 
 def solution(mesh):

time: 129 us -> 125 us (0.969); the launches traced: 129 us -> 123 us
  waiting for transfers between devices: 41.6 us -> 31.6 us
  starting transfers between devices: 17.3 us -> 22 us
    ppermute x19, waiting for transfers between devices: 41.6 us -> 31.6 us  [send(): return lax.ppermute(value, AXES, perm(move))]
    ppermute x19, starting transfers between devices: 17.3 us -> 22 us  [send(): return lax.ppermute(value, AXES, perm(move))]
  transfers between devices with their start and end apart: 19 -> 19, of which waited for: 11 -> 12; matrix products, arithmetic and copies ran while one was open for 0% -> 0% of each run, Pallas kernels for 5% -> 5%
where the time goes in v8:
time: 125 us; the launch traced here: 123 us
  blocking collectives  50.9 us (41%)
  waiting for transfers between devices  31.6 us (25%)
  starting transfers between devices  22 us (18%)
  Pallas kernels  16 us (13%)
  other arithmetic  2.12 us (2%)
    all_to_all x4, blocking collectives, all_of(): return lax.all_to_all(value, axes, 0, 0)  50.9 us
    ppermute x19, waiting for transfers between devices, send(): return lax.ppermute(value, AXES, perm(move))  31.6 us
    ppermute x19, starting transfers between devices, send(): return lax.ppermute(value, AXES, perm(move))  22 us
    pallas_call x1, Pallas kernels, per_device(): pl.pallas_call(scores_kernel, out_shape=(shape((vocab, tokens), F32), sha...  7.54 us
    pallas_call x1, Pallas kernels, per_device(): pl.pallas_call(load_kernel, out_shape=pltpu.VMEM((vocab, features), BF),...  4.14 us
  transfers between devices with their start and end apart: 19, of which 12 were waited for; matrix products, arithmetic and copies ran while one was open for 0% of the time, Pallas kernels for 5%

profile of v8, /device:TPU:6, one launch (start us, length us, event | category | flops | bytes accessed | tf_op | source)
XLA Modules:
  0.0 122.8 jit_solution(14419627252883892635)
XLA Ops:
  0.0 0.7 pad_maximum_fusion.3
  0.8 18.7 %all_to_all.20.block = bf16[8,2,8,672]{3,2,1,0:T(8,128)(2,1)S(1)} all-to-all(bf16[8,2,8,672]{3,2,1,0:T(8,128)(2,1)S(1)} %broadcast_in_dim.2), channel_id=1, replica_groups=mesh['z'=8,'y'=4,'x'=4,'c'=2] {'z'}, dimensions={0} | all-to-all | bytes 344064 | tf_op jit(solution)/shard_map/gather_z/all_to_all | solution.py:53
  19.5 0.1 gather_z.1
  19.6 3.1 %collective-permute-start.3 = (bf16[672,128]{1,0:T(8,128)(2,1)S(1)}, bf16[672,128]{1,0:T(8,128)(2,1)S(1)}, u32[]{:S(2)}, u32[]{:S(2)}) collective-permute-start(bf16[672,128]{1,0:T(8,128)(2,1)S(1)} %gather_z.1), channel_id=1, source_target_pairs={{0,24},{1,7},{2,26},{3,1},{4,28},{5,3},{6,30},{7,5},{8,0},{9,15},{... | collective-permute-start | bytes 516104 | tf_op jit(solution)/shard_map/gather_yx/ppermute | solution.py:33
  22.7 0.6 collective-permute-start.2
  23.3 1.0 collective-permute-start
  24.3 3.2 %collective-permute-done.3 = bf16[672,128]{1,0:T(8,128)(2,1)S(1)} collective-permute-done((bf16[672,128]{1,0:T(8,128)(2,1)S(1)}, bf16[672,128]{1,0:T(8,128)(2,1)S(1)}, u32[]{:S(2)}, u32[]{:S(2)}) %collective-permute-start.3) | collective-permute-done | bytes 172064 | tf_op jit(solution)/shard_map/gather_yx/ppermute | solution.py:33
  27.5 2.2 %collective-permute-done.2 = bf16[672,128]{1,0:T(8,128)(2,1)S(1)} collective-permute-done((bf16[672,128]{1,0:T(8,128)(2,1)S(1)}, bf16[672,128]{1,0:T(8,128)(2,1)S(1)}, u32[]{:S(2)}, u32[]{:S(2)}) %collective-permute-start.2) | collective-permute-done | bytes 172064 | tf_op jit(solution)/shard_map/gather_yx/ppermute | solution.py:33
  29.7 1.7 %collective-permute-done = bf16[672,128]{1,0:T(8,128)(2,1)S(1)} collective-permute-done((bf16[672,128]{1,0:T(8,128)(2,1)S(1)}, bf16[672,128]{1,0:T(8,128)(2,1)S(1)}, u32[]{:S(2)}, u32[]{:S(2)}) %collective-permute-start) | collective-permute-done | bytes 172064 | tf_op jit(solution)/shard_map/gather_yx/ppermute | solution.py:33
  31.5 0.1 pad_maximum_fusion._.refs_4_
  31.6 0.9 collective-permute-start.6
  32.5 2.4 %collective-permute-start.5 = (bf16[4,672,128]{2,1,0:T(8,128)(2,1)S(1)}, bf16[4,672,128]{2,1,0:T(8,128)(2,1)S(1)}, u32[]{:S(2)}, u32[]{:S(2)}) collective-permute-start(bf16[4,672,128]{2,1,0:T(8,128)(2,1)S(1)} %pad_maximum_fusion._.refs_4_), channel_id=1, source_target_pairs={{0,2},{1,9},{2,4},{3,11},{4,6},{5,13},{6,0},{7,15},{8,10},{9,17},{... | collective-permute-start | bytes 2064392 | tf_op jit(solution)/shard_map/gather_xy/ppermute | solution.py:33
  34.9 0.3 collective-permute-start.4
  35.2 3.4 %collective-permute-start.1 = (bf16[2,672,128]{2,1,0:T(8,128)(2,1)S(1)}, bf16[2,672,128]{2,1,0:T(8,128)(2,1)S(1)}, u32[]{:S(2)}, u32[]{:S(2)}) collective-permute-start(bf16[2,672,128]{2,1,0:T(8,128)(2,1)S(1)} %pad_maximum_fusion.1), channel_id=1, source_target_pairs={{0,4},{1,17},{2,6},{3,19},{4,0},{5,21},{6,2},{7,23},{8,12},{9,25},... | collective-permute-start | bytes 1032200 | tf_op jit(solution)/shard_map/gather_xy/ppermute | solution.py:33
  38.6 4.1 %gather_yx.1.refs_10_.w = bf16[1024,5376]{1,0:T(8,128)(2,1)S(1)} custom-call(bf16[1024,5376]{1,0:T(8,128)(2,1)} %w.1, bf16[4,672,128]{2,1,0:T(8,128)(2,1)S(1)} %pad_maximum_fusion._.refs_4_), custom_call_target="tpu_custom_call" | custom-call | bytes 22020096 | tf_op jit(solution)/shard_map/gather_yx/pallas_call | solution.py:179
  42.8 0.1 collective-permute-start.11
  42.9 8.3 %collective-permute-done.6.refs_3_ = bf16[4,672,128]{2,1,0:T(8,128)(2,1)S(1)} collective-permute-done((bf16[4,672,128]{2,1,0:T(8,128)(2,1)S(1)}, bf16[4,672,128]{2,1,0:T(8,128)(2,1)S(1)}, u32[]{:S(2)}, u32[]{:S(2)}) %collective-permute-start.6) | collective-permute-done | bytes 688160 | tf_op jit(solution)/shard_map/gather_xy/ppermute | solution.py:33
  51.2 0.0 collective-permute-start.10
  51.2 0.0 collective-permute-done.5.refs_2_
  51.2 0.5 collective-permute-start.9
  51.7 0.0 collective-permute-done.4.refs_1_
  51.7 0.1 collective-permute-start.8
  51.8 0.0 collective-permute-done.1.refs_0_
  51.8 0.4 collective-permute-start.7
  52.2 2.6 %collective-permute-done.8.refs_6_ = bf16[2,672,128]{2,1,0:T(8,128)(2,1)S(1)} collective-permute-done((bf16[2,672,128]{2,1,0:T(8,128)(2,1)S(1)}, bf16[2,672,128]{2,1,0:T(8,128)(2,1)S(1)}, u32[]{:S(2)}, u32[]{:S(2)}) %collective-permute-start.8) | collective-permute-done | bytes 344096 | tf_op jit(solution)/shard_map/gather_xy/ppermute | solution.py:33
  54.8 0.5 collective-permute-done.7.refs_5_
  55.3 0.0 collective-permute-done.11.refs_9_
  55.3 0.0 collective-permute-done.10.refs_8_
  55.3 0.0 collective-permute-done.9.refs_7_
  55.3 7.5 %scores.1 = (f32[1024,256]{1,0:T(8,128)S(1)}, f32[1024,256]{1,0:T(8,128)S(1)}, f32[16,4,256]{2,1,0:T(4,128)S(1)}, f32[4,256]{1,0:T(4,128)S(1)}) custom-call(bf16[2,672,128]{2,1,0:T(8,128)(2,1)S(1)} %collective-permute-done.1.refs_0_, bf16[2,672,128]{2,1,0:T(8,128)(2,1)S(1)} %collective-permute-done.4.refs_1_, ...), custom_call_target="tpu_custom_call" | custom-call | tf_op jit(solution)/shard_map/scores/pallas_call | solution.py:198
  62.8 10.6 %all_to_all.21.parts = f32[16,4,256]{2,1,0:T(4,128)S(1)} all-to-all(f32[16,4,256]{2,1,0:T(4,128)S(1)} %get-tuple-element.15), channel_id=1, replica_groups=mesh['z'=8,'y'=4,'x'=4,'c'=2] {'y','x'}, dimensions={0} | all-to-all | bytes 131072 | tf_op jit(solution)/shard_map/statistics/all_to_all | solution.py:53
  73.5 10.4 %all_to_all.22.parts = f32[16,4,256]{2,1,0:T(4,128)S(1)} all-to-all(f32[16,4,256]{2,1,0:T(4,128)S(1)} %statistics.1), channel_id=1, replica_groups=mesh['z'=8,'y'=4,'x'=4,'c'=2] {'z','c'}, dimensions={0} | all-to-all | bytes 131072 | tf_op jit(solution)/shard_map/statistics/all_to_all | solution.py:53
  83.8 2.2 %product.2 = (bf16[4,4,64,672]{3,2,1,0:T(8,128)(2,1)S(1)}, bf16[256,1024]{1,0:T(8,128)(2,1)S(1)}) custom-call(f32[16,4,256]{2,1,0:T(4,128)S(1)} %all_to_all.22.parts, f32[4,256]{1,0:T(4,128)S(1)} %get-tuple-element.16.own_top, f32[1024,256]{1,0:T(8,128)S(1)} %get-tuple-element.17.raised, f32[1024,256]{1,0:T(8,128)S(1)} %get-tuple-element.18.slopes, ...), custom_call_target="tpu_custom_call" | custom-call | tf_op jit(solution)/shard_map/product/pallas_call | solution.py:223
  86.0 0.5 collective-permute-start.12
  86.5 2.0 %product.3 = f32[4,4,64,672]{3,2,1,0:T(8,128)S(1)} custom-call(bf16[256,1024]{1,0:T(8,128)(2,1)S(1)} %get-tuple-element.19.mixture, bf16[1024,5376]{1,0:T(8,128)(2,1)S(1)} %gather_yx.1.refs_10_.w), custom_call_target="tpu_custom_call" | custom-call | flops 1409286144 | bytes 11010048 | tf_op jit(solution)/shard_map/product/pallas_call | solution.py:234
  88.5 1.0 collective-permute-done.12
  89.5 0.3 fusion.7
  89.8 2.2 %collective-permute-start.13 = (bf16[4,64,672]{2,1,0:T(8,128)(2,1)S(1)}, bf16[4,64,672]{2,1,0:T(8,128)(2,1)S(1)}, u32[]{:S(2)}, u32[]{:S(2)}) collective-permute-start(bf16[4,64,672]{2,1,0:T(8,128)(2,1)S(1)} %get-tuple-element.23), channel_id=1, source_target_pairs={{0,4},{1,17},{2,6},{3,19},{4,0},{5,21},{6,2},{7,23},{8,12},{9,25},... | collective-permute-start | bytes 1032200 | tf_op jit(solution)/shard_map/scatter_xy/ppermute | solution.py:33
  92.0 1.3 %collective-permute-start.15 = (bf16[4,64,672]{2,1,0:T(8,128)(2,1)S(1)}, bf16[4,64,672]{2,1,0:T(8,128)(2,1)S(1)}, u32[]{:S(2)}, u32[]{:S(2)}) collective-permute-start(bf16[4,64,672]{2,1,0:T(8,128)(2,1)S(1)} %get-tuple-element.24), channel_id=1, source_target_pairs={{0,2},{1,9},{2,4},{3,11},{4,6},{5,13},{6,0},{7,15},{8,10},{9,17},{... | collective-permute-start | bytes 1032200 | tf_op jit(solution)/shard_map/scatter_xy/ppermute | solution.py:33
  93.3 0.7 collective-permute-start.14
  94.0 5.3 %collective-permute-done.13 = bf16[4,64,672]{2,1,0:T(8,128)(2,1)S(1)} collective-permute-done((bf16[4,64,672]{2,1,0:T(8,128)(2,1)S(1)}, bf16[4,64,672]{2,1,0:T(8,128)(2,1)S(1)}, u32[]{:S(2)}, u32[]{:S(2)}) %collective-permute-start.13) | collective-permute-done | bytes 344096 | tf_op jit(solution)/shard_map/scatter_xy/ppermute | solution.py:33
  99.3 3.6 %collective-permute-done.15 = bf16[4,64,672]{2,1,0:T(8,128)(2,1)S(1)} collective-permute-done((bf16[4,64,672]{2,1,0:T(8,128)(2,1)S(1)}, bf16[4,64,672]{2,1,0:T(8,128)(2,1)S(1)}, u32[]{:S(2)}, u32[]{:S(2)}) %collective-permute-start.15) | collective-permute-done | bytes 344096 | tf_op jit(solution)/shard_map/scatter_xy/ppermute | solution.py:33
  102.9 0.6 collective-permute-done.14
  103.4 0.2 fusion.15
  103.7 1.3 %collective-permute-start.16 = (bf16[64,672]{1,0:T(8,128)(2,1)S(1)}, bf16[64,672]{1,0:T(8,128)(2,1)S(1)}, u32[]{:S(2)}, u32[]{:S(2)}) collective-permute-start(bf16[64,672]{1,0:T(8,128)(2,1)S(1)} %get-tuple-element.26), channel_id=1, source_target_pairs={{0,16},{1,5},{2,18},{3,7},{4,20},{5,1},{6,22},{7,3},{8,24},{9,13},... | collective-permute-start | bytes 258056 | tf_op jit(solution)/shard_map/scatter_yx/ppermute | solution.py:33
  105.0 0.8 collective-permute-start.18
  105.8 2.5 %collective-permute-start.17 = (bf16[64,672]{1,0:T(8,128)(2,1)S(1)}, bf16[64,672]{1,0:T(8,128)(2,1)S(1)}, u32[]{:S(2)}, u32[]{:S(2)}) collective-permute-start(bf16[64,672]{1,0:T(8,128)(2,1)S(1)} %get-tuple-element.28), channel_id=1, source_target_pairs={{0,24},{1,7},{2,26},{3,1},{4,28},{5,3},{6,30},{7,5},{8,0},{9,15},{... | collective-permute-start | bytes 258056 | tf_op jit(solution)/shard_map/scatter_yx/ppermute | solution.py:33
  108.3 1.7 %collective-permute-done.16 = bf16[64,672]{1,0:T(8,128)(2,1)S(1)} collective-permute-done((bf16[64,672]{1,0:T(8,128)(2,1)S(1)}, bf16[64,672]{1,0:T(8,128)(2,1)S(1)}, u32[]{:S(2)}, u32[]{:S(2)}) %collective-permute-start.16) | collective-permute-done | bytes 86048 | tf_op jit(solution)/shard_map/scatter_yx/ppermute | solution.py:33
  109.9 1.0 collective-permute-done.18
  111.0 0.0 collective-permute-done.17
  111.0 0.1 fusion.14
  111.0 11.2 %all_to_all.23 = bf16[8,8,672]{2,1,0:T(8,128)(2,1)S(1)} all-to-all(bf16[8,8,672]{2,1,0:T(8,128)(2,1)S(1)} %fusion.14), channel_id=1, replica_groups=mesh['z'=8,'y'=4,'x'=4,'c'=2] {'z'}, dimensions={0} | all-to-all | bytes 172032 | tf_op jit(solution)/shard_map/scatter_z/all_to_all | solution.py:53
  122.2 0.6 convert_reduce_fusion
  (5 shorter events, 0.1 us)
Async XLA Ops:
  19.6 7.9 %collective-permute-start.3 = (bf16[672,128]{1,0:T(8,128)(2,1)S(1)}, bf16[672,128]{1,0:T(8,128)(2,1)S(1)}, u32[]{:S(2)}, u32[]{:S(2)}) collective-permute-start(bf16[672,128]{1,0:T(8,128)(2,1)S(1)} %gather_z.1), channel_id=1, source_target_pairs={{0,24},{1,7},{2,26},{3,1},{4,28},{5,3},{6,30},{7,5},{8,0},{9,15},{... | collective-permute-start | bytes 516104 | tf_op jit(solution)/shard_map/gather_yx/ppermute | solution.py:33
  22.7 7.0 %collective-permute-start.2 = (bf16[672,128]{1,0:T(8,128)(2,1)S(1)}, bf16[672,128]{1,0:T(8,128)(2,1)S(1)}, u32[]{:S(2)}, u32[]{:S(2)}) collective-permute-start(bf16[672,128]{1,0:T(8,128)(2,1)S(1)} %gather_z.1), channel_id=1, source_target_pairs={{0,16},{1,5},{2,18},{3,7},{4,20},{5,1},{6,22},{7,3},{8,24},{9,13},... | collective-permute-start | bytes 516104 | tf_op jit(solution)/shard_map/gather_yx/ppermute | solution.py:33
  23.3 8.1 %collective-permute-start = (bf16[672,128]{1,0:T(8,128)(2,1)S(1)}, bf16[672,128]{1,0:T(8,128)(2,1)S(1)}, u32[]{:S(2)}, u32[]{:S(2)}) collective-permute-start(bf16[672,128]{1,0:T(8,128)(2,1)S(1)} %gather_z.1), channel_id=1, source_target_pairs={{0,8},{1,3},{2,10},{3,5},{4,12},{5,7},{6,14},{7,1},{8,16},{9,11},{... | collective-permute-start | bytes 516104 | tf_op jit(solution)/shard_map/gather_yx/ppermute | solution.py:33
  31.6 19.6 %collective-permute-start.6 = (bf16[4,672,128]{2,1,0:T(8,128)(2,1)S(1)}, bf16[4,672,128]{2,1,0:T(8,128)(2,1)S(1)}, u32[]{:S(2)}, u32[]{:S(2)}) collective-permute-start(bf16[4,672,128]{2,1,0:T(8,128)(2,1)S(1)} %pad_maximum_fusion._.refs_4_), channel_id=1, source_target_pairs={{0,6},{1,25},{2,0},{3,27},{4,2},{5,29},{6,4},{7,31},{8,14},{9,1},{... | collective-permute-start | bytes 2064392 | tf_op jit(solution)/shard_map/gather_xy/ppermute | solution.py:33
  32.5 18.7 %collective-permute-start.5 = (bf16[4,672,128]{2,1,0:T(8,128)(2,1)S(1)}, bf16[4,672,128]{2,1,0:T(8,128)(2,1)S(1)}, u32[]{:S(2)}, u32[]{:S(2)}) collective-permute-start(bf16[4,672,128]{2,1,0:T(8,128)(2,1)S(1)} %pad_maximum_fusion._.refs_4_), channel_id=1, source_target_pairs={{0,2},{1,9},{2,4},{3,11},{4,6},{5,13},{6,0},{7,15},{8,10},{9,17},{... | collective-permute-start | bytes 2064392 | tf_op jit(solution)/shard_map/gather_xy/ppermute | solution.py:33
  34.9 16.8 %collective-permute-start.4 = (bf16[2,672,128]{2,1,0:T(8,128)(2,1)S(1)}, bf16[2,672,128]{2,1,0:T(8,128)(2,1)S(1)}, u32[]{:S(2)}, u32[]{:S(2)}) collective-permute-start(bf16[2,672,128]{2,1,0:T(8,128)(2,1)S(1)} %pad_maximum_fusion.2), channel_id=1, source_target_pairs={{0,4},{1,17},{2,6},{3,19},{4,0},{5,21},{6,2},{7,23},{8,12},{9,25},... | collective-permute-start | bytes 1032200 | tf_op jit(solution)/shard_map/gather_xy/ppermute | solution.py:33
  35.2 16.5 %collective-permute-start.1 = (bf16[2,672,128]{2,1,0:T(8,128)(2,1)S(1)}, bf16[2,672,128]{2,1,0:T(8,128)(2,1)S(1)}, u32[]{:S(2)}, u32[]{:S(2)}) collective-permute-start(bf16[2,672,128]{2,1,0:T(8,128)(2,1)S(1)} %pad_maximum_fusion.1), channel_id=1, source_target_pairs={{0,4},{1,17},{2,6},{3,19},{4,0},{5,21},{6,2},{7,23},{8,12},{9,25},... | collective-permute-start | bytes 1032200 | tf_op jit(solution)/shard_map/gather_xy/ppermute | solution.py:33
  42.8 12.5 %collective-permute-start.11 = (bf16[4,672,128]{2,1,0:T(8,128)(2,1)S(1)}, bf16[4,672,128]{2,1,0:T(8,128)(2,1)S(1)}, u32[]{:S(2)}, u32[]{:S(2)}) collective-permute-start(bf16[4,672,128]{2,1,0:T(8,128)(2,1)S(1)} %pad_maximum_fusion._.refs_4_), channel_id=1, source_target_pairs={{0,1},{1,0},{2,3},{3,2},{4,5},{5,4},{6,7},{7,6},{8,9},{9,8},{10,11... | collective-permute-start | bytes 2064392 | tf_op jit(solution)/shard_map/gather_xy/ppermute | solution.py:33
  51.2 4.1 %collective-permute-start.10 = (bf16[4,672,128]{2,1,0:T(8,128)(2,1)S(1)}, bf16[4,672,128]{2,1,0:T(8,128)(2,1)S(1)}, u32[]{:S(2)}, u32[]{:S(2)}) collective-permute-start(bf16[4,672,128]{2,1,0:T(8,128)(2,1)S(1)} %collective-permute-done.6.refs_3_), channel_id=1, source_target_pairs={{0,1},{1,0},{2,3},{3,2},{4,5},{5,4},{6,7},{7,6},{8,9},{9,8},{10,11... | collective-permute-start | bytes 2064392 | tf_op jit(solution)/shard_map/gather_xy/ppermute | solution.py:33
  51.2 4.1 %collective-permute-start.9 = (bf16[4,672,128]{2,1,0:T(8,128)(2,1)S(1)}, bf16[4,672,128]{2,1,0:T(8,128)(2,1)S(1)}, u32[]{:S(2)}, u32[]{:S(2)}) collective-permute-start(bf16[4,672,128]{2,1,0:T(8,128)(2,1)S(1)} %collective-permute-done.5.refs_2_), channel_id=1, source_target_pairs={{0,1},{1,0},{2,3},{3,2},{4,5},{5,4},{6,7},{7,6},{8,9},{9,8},{10,11... | collective-permute-start | bytes 2064392 | tf_op jit(solution)/shard_map/gather_xy/ppermute | solution.py:33
  51.7 3.1 %collective-permute-start.8 = (bf16[2,672,128]{2,1,0:T(8,128)(2,1)S(1)}, bf16[2,672,128]{2,1,0:T(8,128)(2,1)S(1)}, u32[]{:S(2)}, u32[]{:S(2)}) collective-permute-start(bf16[2,672,128]{2,1,0:T(8,128)(2,1)S(1)} %collective-permute-done.4.refs_1_), channel_id=1, source_target_pairs={{0,1},{1,0},{2,3},{3,2},{4,5},{5,4},{6,7},{7,6},{8,9},{9,8},{10,11... | collective-permute-start | bytes 1032200 | tf_op jit(solution)/shard_map/gather_xy/ppermute | solution.py:33
  51.8 3.5 %collective-permute-start.7 = (bf16[2,672,128]{2,1,0:T(8,128)(2,1)S(1)}, bf16[2,672,128]{2,1,0:T(8,128)(2,1)S(1)}, u32[]{:S(2)}, u32[]{:S(2)}) collective-permute-start(bf16[2,672,128]{2,1,0:T(8,128)(2,1)S(1)} %collective-permute-done.1.refs_0_), channel_id=1, source_target_pairs={{0,1},{1,0},{2,3},{3,2},{4,5},{5,4},{6,7},{7,6},{8,9},{9,8},{10,11... | collective-permute-start | bytes 1032200 | tf_op jit(solution)/shard_map/gather_xy/ppermute | solution.py:33
  86.0 3.5 %collective-permute-start.12 = (bf16[4,4,64,672]{3,2,1,0:T(8,128)(2,1)S(1)}, bf16[4,4,64,672]{3,2,1,0:T(8,128)(2,1)S(1)}, u32[]{:S(2)}, u32[]{:S(2)}) collective-permute-start(bf16[4,4,64,672]{3,2,1,0:T(8,128)(2,1)S(1)} %get-tuple-element.20), channel_id=1, source_target_pairs={{0,1},{1,0},{2,3},{3,2},{4,5},{5,4},{6,7},{7,6},{8,9},{9,8},{10,11... | collective-permute-start | bytes 4128776 | tf_op jit(solution)/shard_map/product/ppermute | solution.py:33
  89.8 9.5 %collective-permute-start.13 = (bf16[4,64,672]{2,1,0:T(8,128)(2,1)S(1)}, bf16[4,64,672]{2,1,0:T(8,128)(2,1)S(1)}, u32[]{:S(2)}, u32[]{:S(2)}) collective-permute-start(bf16[4,64,672]{2,1,0:T(8,128)(2,1)S(1)} %get-tuple-element.23), channel_id=1, source_target_pairs={{0,4},{1,17},{2,6},{3,19},{4,0},{5,21},{6,2},{7,23},{8,12},{9,25},... | collective-permute-start | bytes 1032200 | tf_op jit(solution)/shard_map/scatter_xy/ppermute | solution.py:33
  92.0 10.8 %collective-permute-start.15 = (bf16[4,64,672]{2,1,0:T(8,128)(2,1)S(1)}, bf16[4,64,672]{2,1,0:T(8,128)(2,1)S(1)}, u32[]{:S(2)}, u32[]{:S(2)}) collective-permute-start(bf16[4,64,672]{2,1,0:T(8,128)(2,1)S(1)} %get-tuple-element.24), channel_id=1, source_target_pairs={{0,2},{1,9},{2,4},{3,11},{4,6},{5,13},{6,0},{7,15},{8,10},{9,17},{... | collective-permute-start | bytes 1032200 | tf_op jit(solution)/shard_map/scatter_xy/ppermute | solution.py:33
  93.3 10.1 %collective-permute-start.14 = (bf16[4,64,672]{2,1,0:T(8,128)(2,1)S(1)}, bf16[4,64,672]{2,1,0:T(8,128)(2,1)S(1)}, u32[]{:S(2)}, u32[]{:S(2)}) collective-permute-start(bf16[4,64,672]{2,1,0:T(8,128)(2,1)S(1)} %get-tuple-element.25), channel_id=1, source_target_pairs={{0,6},{1,25},{2,0},{3,27},{4,2},{5,29},{6,4},{7,31},{8,14},{9,1},{... | collective-permute-start | bytes 1032200 | tf_op jit(solution)/shard_map/scatter_xy/ppermute | solution.py:33
  103.7 6.2 %collective-permute-start.16 = (bf16[64,672]{1,0:T(8,128)(2,1)S(1)}, bf16[64,672]{1,0:T(8,128)(2,1)S(1)}, u32[]{:S(2)}, u32[]{:S(2)}) collective-permute-start(bf16[64,672]{1,0:T(8,128)(2,1)S(1)} %get-tuple-element.26), channel_id=1, source_target_pairs={{0,16},{1,5},{2,18},{3,7},{4,20},{5,1},{6,22},{7,3},{8,24},{9,13},... | collective-permute-start | bytes 258056 | tf_op jit(solution)/shard_map/scatter_yx/ppermute | solution.py:33
  105.0 5.9 %collective-permute-start.18 = (bf16[64,672]{1,0:T(8,128)(2,1)S(1)}, bf16[64,672]{1,0:T(8,128)(2,1)S(1)}, u32[]{:S(2)}, u32[]{:S(2)}) collective-permute-start(bf16[64,672]{1,0:T(8,128)(2,1)S(1)} %get-tuple-element.27), channel_id=1, source_target_pairs={{0,8},{1,3},{2,10},{3,5},{4,12},{5,7},{6,14},{7,1},{8,16},{9,11},{... | collective-permute-start | bytes 258056 | tf_op jit(solution)/shard_map/scatter_yx/ppermute | solution.py:33
  105.8 5.2 %collective-permute-start.17 = (bf16[64,672]{1,0:T(8,128)(2,1)S(1)}, bf16[64,672]{1,0:T(8,128)(2,1)S(1)}, u32[]{:S(2)}, u32[]{:S(2)}) collective-permute-start(bf16[64,672]{1,0:T(8,128)(2,1)S(1)} %get-tuple-element.28), channel_id=1, source_target_pairs={{0,24},{1,7},{2,26},{3,1},{4,28},{5,3},{6,30},{7,5},{8,0},{9,15},{... | collective-permute-start | bytes 258056 | tf_op jit(solution)/shard_map/scatter_yx/ppermute | solution.py:33

commit v9 on v8

--- a/solution.py
+++ b/solution.py
@@ -79,7 +79,7 @@
                 y_at = lax.rem(y + NQ - y_back, NQ)
                 first = pl.multiple_of((2 * x_at + parity) * width, width)
                 column = pl.multiple_of(y_at * lanes, lanes)
-                near, far, behind, ahead, same = pieces
+                far, near, behind, ahead, same = pieces
                 if k == 2:
                     piece = (near, far)[r // 2][r % 2]
                 else:
@@ -191,7 +191,7 @@
         ahead, behind = send(block, along_xy(3)), send(block, along_xy(1))
         near, far = (send(half, along_xy(2)) for half in (block[: NQ // 2], block[NQ // 2 :]))
         same, weight = lax.optimization_barrier((block, weight))
-        own = [near, far, behind, ahead, same]
+        own = [far, near, behind, ahead, same]
         theirs = [send(piece, other_core) for piece in own]
 
     with jax.named_scope("scores"):

time: 125 us -> 125 us (level)
  waiting for transfers between devices: 31.6 us -> 29.4 us
  blocking collectives: 50.9 us -> 52.5 us
    ppermute x19, waiting for transfers between devices: 31.6 us -> 29.4 us  [send(): return lax.ppermute(value, AXES, perm(move))]
    all_to_all x4, blocking collectives: 50.9 us -> 52.5 us  [all_of(): return lax.all_to_all(value, axes, 0, 0)]
where the time goes in v9:
time: 125 us; the launch traced here: 123 us
  blocking collectives  52.5 us (42%)
  waiting for transfers between devices  29.4 us (24%)
  starting transfers between devices  22.6 us (18%)
  Pallas kernels  16 us (13%)
  other arithmetic  2.12 us (2%)
    all_to_all x4, blocking collectives, all_of(): return lax.all_to_all(value, axes, 0, 0)  52.5 us
    ppermute x19, waiting for transfers between devices, send(): return lax.ppermute(value, AXES, perm(move))  29.4 us
    ppermute x19, starting transfers between devices, send(): return lax.ppermute(value, AXES, perm(move))  22.6 us
    pallas_call x1, Pallas kernels, per_device(): pl.pallas_call(scores_kernel, out_shape=(shape((vocab, tokens), F32), sha...  7.54 us
    pallas_call x1, Pallas kernels, per_device(): pl.pallas_call(load_kernel, out_shape=pltpu.VMEM((vocab, features), BF),...  4.14 us
  transfers between devices with their start and end apart: 19, of which 12 were waited for; matrix products, arithmetic and copies ran while one was open for 0% of the time, Pallas kernels for 5%

profile of v9, /device:TPU:6, one launch (start us, length us, event | category | flops | bytes accessed | tf_op | source)
XLA Modules:
  0.0 122.8 jit_solution(14550835619428815080)
XLA Ops:
  0.0 0.7 pad_maximum_fusion.3
  0.8 18.7 %all_to_all.20.block = bf16[8,2,8,672]{3,2,1,0:T(8,128)(2,1)S(1)} all-to-all(bf16[8,2,8,672]{3,2,1,0:T(8,128)(2,1)S(1)} %broadcast_in_dim.2), channel_id=1, replica_groups=mesh['z'=8,'y'=4,'x'=4,'c'=2] {'z'}, dimensions={0} | all-to-all | bytes 344064 | tf_op jit(solution)/shard_map/gather_z/all_to_all | solution.py:53
  19.5 0.1 gather_z.1
  19.6 1.7 %collective-permute-start.3 = (bf16[672,128]{1,0:T(8,128)(2,1)S(1)}, bf16[672,128]{1,0:T(8,128)(2,1)S(1)}, u32[]{:S(2)}, u32[]{:S(2)}) collective-permute-start(bf16[672,128]{1,0:T(8,128)(2,1)S(1)} %gather_z.1), channel_id=1, source_target_pairs={{0,8},{1,3},{2,10},{3,5},{4,12},{5,7},{6,14},{7,1},{8,16},{9,11},{... | collective-permute-start | bytes 516104 | tf_op jit(solution)/shard_map/gather_yx/ppermute | solution.py:33
  21.3 1.7 %collective-permute-start.1 = (bf16[672,128]{1,0:T(8,128)(2,1)S(1)}, bf16[672,128]{1,0:T(8,128)(2,1)S(1)}, u32[]{:S(2)}, u32[]{:S(2)}) collective-permute-start(bf16[672,128]{1,0:T(8,128)(2,1)S(1)} %gather_z.1), channel_id=1, source_target_pairs={{0,24},{1,7},{2,26},{3,1},{4,28},{5,3},{6,30},{7,5},{8,0},{9,15},{... | collective-permute-start | bytes 516104 | tf_op jit(solution)/shard_map/gather_yx/ppermute | solution.py:33
  22.9 2.0 %collective-permute-start = (bf16[672,128]{1,0:T(8,128)(2,1)S(1)}, bf16[672,128]{1,0:T(8,128)(2,1)S(1)}, u32[]{:S(2)}, u32[]{:S(2)}) collective-permute-start(bf16[672,128]{1,0:T(8,128)(2,1)S(1)} %gather_z.1), channel_id=1, source_target_pairs={{0,16},{1,5},{2,18},{3,7},{4,20},{5,1},{6,22},{7,3},{8,24},{9,13},... | collective-permute-start | bytes 516104 | tf_op jit(solution)/shard_map/gather_yx/ppermute | solution.py:33
  24.9 1.4 %collective-permute-done.3 = bf16[672,128]{1,0:T(8,128)(2,1)S(1)} collective-permute-done((bf16[672,128]{1,0:T(8,128)(2,1)S(1)}, bf16[672,128]{1,0:T(8,128)(2,1)S(1)}, u32[]{:S(2)}, u32[]{:S(2)}) %collective-permute-start.3) | collective-permute-done | bytes 172064 | tf_op jit(solution)/shard_map/gather_yx/ppermute | solution.py:33
  26.3 0.4 collective-permute-done.1
  26.7 3.2 %collective-permute-done = bf16[672,128]{1,0:T(8,128)(2,1)S(1)} collective-permute-done((bf16[672,128]{1,0:T(8,128)(2,1)S(1)}, bf16[672,128]{1,0:T(8,128)(2,1)S(1)}, u32[]{:S(2)}, u32[]{:S(2)}) %collective-permute-start) | collective-permute-done | bytes 172064 | tf_op jit(solution)/shard_map/gather_yx/ppermute | solution.py:33
  29.8 0.1 pad_maximum_fusion._.refs_4_
  29.9 0.9 collective-permute-start.6
  30.8 2.4 %collective-permute-start.5 = (bf16[4,672,128]{2,1,0:T(8,128)(2,1)S(1)}, bf16[4,672,128]{2,1,0:T(8,128)(2,1)S(1)}, u32[]{:S(2)}, u32[]{:S(2)}) collective-permute-start(bf16[4,672,128]{2,1,0:T(8,128)(2,1)S(1)} %pad_maximum_fusion._.refs_4_), channel_id=1, source_target_pairs={{0,2},{1,9},{2,4},{3,11},{4,6},{5,13},{6,0},{7,15},{8,10},{9,17},{... | collective-permute-start | bytes 2064392 | tf_op jit(solution)/shard_map/gather_xy/ppermute | solution.py:33
  33.3 0.3 collective-permute-start.4
  33.6 3.4 %collective-permute-start.2 = (bf16[2,672,128]{2,1,0:T(8,128)(2,1)S(1)}, bf16[2,672,128]{2,1,0:T(8,128)(2,1)S(1)}, u32[]{:S(2)}, u32[]{:S(2)}) collective-permute-start(bf16[2,672,128]{2,1,0:T(8,128)(2,1)S(1)} %pad_maximum_fusion.1), channel_id=1, source_target_pairs={{0,4},{1,17},{2,6},{3,19},{4,0},{5,21},{6,2},{7,23},{8,12},{9,25},... | collective-permute-start | bytes 1032200 | tf_op jit(solution)/shard_map/gather_xy/ppermute | solution.py:33
  37.0 4.1 %gather_yx.1.refs_10_.w = bf16[1024,5376]{1,0:T(8,128)(2,1)S(1)} custom-call(bf16[1024,5376]{1,0:T(8,128)(2,1)} %w.1, bf16[4,672,128]{2,1,0:T(8,128)(2,1)S(1)} %pad_maximum_fusion._.refs_4_), custom_call_target="tpu_custom_call" | custom-call | bytes 22020096 | tf_op jit(solution)/shard_map/gather_yx/pallas_call | solution.py:179
  41.2 0.1 collective-permute-start.11
  41.3 8.3 %collective-permute-done.6.refs_3_ = bf16[4,672,128]{2,1,0:T(8,128)(2,1)S(1)} collective-permute-done((bf16[4,672,128]{2,1,0:T(8,128)(2,1)S(1)}, bf16[4,672,128]{2,1,0:T(8,128)(2,1)S(1)}, u32[]{:S(2)}, u32[]{:S(2)}) %collective-permute-start.6) | collective-permute-done | bytes 688160 | tf_op jit(solution)/shard_map/gather_xy/ppermute | solution.py:33
  49.5 0.0 collective-permute-start.10
  49.5 0.0 collective-permute-done.5.refs_2_
  49.5 0.5 collective-permute-start.9
  50.0 0.0 collective-permute-done.4.refs_1_
  50.1 0.1 collective-permute-start.8
  50.1 0.0 collective-permute-done.2.refs_0_
  50.1 0.4 collective-permute-start.7
  50.6 2.6 %collective-permute-done.8.refs_6_ = bf16[2,672,128]{2,1,0:T(8,128)(2,1)S(1)} collective-permute-done((bf16[2,672,128]{2,1,0:T(8,128)(2,1)S(1)}, bf16[2,672,128]{2,1,0:T(8,128)(2,1)S(1)}, u32[]{:S(2)}, u32[]{:S(2)}) %collective-permute-start.8) | collective-permute-done | bytes 344096 | tf_op jit(solution)/shard_map/gather_xy/ppermute | solution.py:33
  53.2 0.5 collective-permute-done.7.refs_5_
  53.6 0.0 collective-permute-done.11.refs_9_
  53.7 0.0 collective-permute-done.10.refs_8_
  53.7 0.0 collective-permute-done.9.refs_7_
  53.7 7.5 %scores.1 = (f32[1024,256]{1,0:T(8,128)S(1)}, f32[1024,256]{1,0:T(8,128)S(1)}, f32[16,4,256]{2,1,0:T(4,128)S(1)}, f32[4,256]{1,0:T(4,128)S(1)}) custom-call(bf16[2,672,128]{2,1,0:T(8,128)(2,1)S(1)} %collective-permute-done.2.refs_0_, bf16[2,672,128]{2,1,0:T(8,128)(2,1)S(1)} %collective-permute-done.4.refs_1_, ...), custom_call_target="tpu_custom_call" | custom-call | tf_op jit(solution)/shard_map/scores/pallas_call | solution.py:198
  61.2 12.3 %all_to_all.21.parts = f32[16,4,256]{2,1,0:T(4,128)S(1)} all-to-all(f32[16,4,256]{2,1,0:T(4,128)S(1)} %get-tuple-element.15), channel_id=1, replica_groups=mesh['z'=8,'y'=4,'x'=4,'c'=2] {'y','x'}, dimensions={0} | all-to-all | bytes 131072 | tf_op jit(solution)/shard_map/statistics/all_to_all | solution.py:53
  73.5 10.4 %all_to_all.22.parts = f32[16,4,256]{2,1,0:T(4,128)S(1)} all-to-all(f32[16,4,256]{2,1,0:T(4,128)S(1)} %statistics.1), channel_id=1, replica_groups=mesh['z'=8,'y'=4,'x'=4,'c'=2] {'z','c'}, dimensions={0} | all-to-all | bytes 131072 | tf_op jit(solution)/shard_map/statistics/all_to_all | solution.py:53
  83.9 2.2 %product.2 = (bf16[4,4,64,672]{3,2,1,0:T(8,128)(2,1)S(1)}, bf16[256,1024]{1,0:T(8,128)(2,1)S(1)}) custom-call(f32[16,4,256]{2,1,0:T(4,128)S(1)} %all_to_all.22.parts, f32[4,256]{1,0:T(4,128)S(1)} %get-tuple-element.16.own_top, f32[1024,256]{1,0:T(8,128)S(1)} %get-tuple-element.17.raised, f32[1024,256]{1,0:T(8,128)S(1)} %get-tuple-element.18.slopes, ...), custom_call_target="tpu_custom_call" | custom-call | tf_op jit(solution)/shard_map/product/pallas_call | solution.py:223
  86.1 0.5 collective-permute-start.12
  86.5 2.0 %product.3 = f32[4,4,64,672]{3,2,1,0:T(8,128)S(1)} custom-call(bf16[256,1024]{1,0:T(8,128)(2,1)S(1)} %get-tuple-element.19.mixture, bf16[1024,5376]{1,0:T(8,128)(2,1)S(1)} %gather_yx.1.refs_10_.w), custom_call_target="tpu_custom_call" | custom-call | flops 1409286144 | bytes 11010048 | tf_op jit(solution)/shard_map/product/pallas_call | solution.py:234
  88.5 1.0 collective-permute-done.12
  89.6 0.3 fusion.7
  89.9 2.2 %collective-permute-start.13 = (bf16[4,64,672]{2,1,0:T(8,128)(2,1)S(1)}, bf16[4,64,672]{2,1,0:T(8,128)(2,1)S(1)}, u32[]{:S(2)}, u32[]{:S(2)}) collective-permute-start(bf16[4,64,672]{2,1,0:T(8,128)(2,1)S(1)} %get-tuple-element.23), channel_id=1, source_target_pairs={{0,4},{1,17},{2,6},{3,19},{4,0},{5,21},{6,2},{7,23},{8,12},{9,25},... | collective-permute-start | bytes 1032200 | tf_op jit(solution)/shard_map/scatter_xy/ppermute | solution.py:33
  92.0 1.3 %collective-permute-start.15 = (bf16[4,64,672]{2,1,0:T(8,128)(2,1)S(1)}, bf16[4,64,672]{2,1,0:T(8,128)(2,1)S(1)}, u32[]{:S(2)}, u32[]{:S(2)}) collective-permute-start(bf16[4,64,672]{2,1,0:T(8,128)(2,1)S(1)} %get-tuple-element.24), channel_id=1, source_target_pairs={{0,2},{1,9},{2,4},{3,11},{4,6},{5,13},{6,0},{7,15},{8,10},{9,17},{... | collective-permute-start | bytes 1032200 | tf_op jit(solution)/shard_map/scatter_xy/ppermute | solution.py:33
  93.3 0.7 collective-permute-start.14
  94.1 5.3 %collective-permute-done.13 = bf16[4,64,672]{2,1,0:T(8,128)(2,1)S(1)} collective-permute-done((bf16[4,64,672]{2,1,0:T(8,128)(2,1)S(1)}, bf16[4,64,672]{2,1,0:T(8,128)(2,1)S(1)}, u32[]{:S(2)}, u32[]{:S(2)}) %collective-permute-start.13) | collective-permute-done | bytes 344096 | tf_op jit(solution)/shard_map/scatter_xy/ppermute | solution.py:33
  99.4 3.5 %collective-permute-done.15 = bf16[4,64,672]{2,1,0:T(8,128)(2,1)S(1)} collective-permute-done((bf16[4,64,672]{2,1,0:T(8,128)(2,1)S(1)}, bf16[4,64,672]{2,1,0:T(8,128)(2,1)S(1)}, u32[]{:S(2)}, u32[]{:S(2)}) %collective-permute-start.15) | collective-permute-done | bytes 344096 | tf_op jit(solution)/shard_map/scatter_xy/ppermute | solution.py:33
  102.9 0.6 collective-permute-done.14
  103.5 0.2 fusion.15
  103.7 1.3 %collective-permute-start.16 = (bf16[64,672]{1,0:T(8,128)(2,1)S(1)}, bf16[64,672]{1,0:T(8,128)(2,1)S(1)}, u32[]{:S(2)}, u32[]{:S(2)}) collective-permute-start(bf16[64,672]{1,0:T(8,128)(2,1)S(1)} %get-tuple-element.26), channel_id=1, source_target_pairs={{0,16},{1,5},{2,18},{3,7},{4,20},{5,1},{6,22},{7,3},{8,24},{9,13},... | collective-permute-start | bytes 258056 | tf_op jit(solution)/shard_map/scatter_yx/ppermute | solution.py:33
  105.0 0.8 collective-permute-start.18
  105.9 2.4 %collective-permute-start.17 = (bf16[64,672]{1,0:T(8,128)(2,1)S(1)}, bf16[64,672]{1,0:T(8,128)(2,1)S(1)}, u32[]{:S(2)}, u32[]{:S(2)}) collective-permute-start(bf16[64,672]{1,0:T(8,128)(2,1)S(1)} %get-tuple-element.28), channel_id=1, source_target_pairs={{0,24},{1,7},{2,26},{3,1},{4,28},{5,3},{6,30},{7,5},{8,0},{9,15},{... | collective-permute-start | bytes 258056 | tf_op jit(solution)/shard_map/scatter_yx/ppermute | solution.py:33
  108.3 1.7 %collective-permute-done.16 = bf16[64,672]{1,0:T(8,128)(2,1)S(1)} collective-permute-done((bf16[64,672]{1,0:T(8,128)(2,1)S(1)}, bf16[64,672]{1,0:T(8,128)(2,1)S(1)}, u32[]{:S(2)}, u32[]{:S(2)}) %collective-permute-start.16) | collective-permute-done | bytes 86048 | tf_op jit(solution)/shard_map/scatter_yx/ppermute | solution.py:33
  110.0 1.0 collective-permute-done.18
  111.0 0.0 collective-permute-done.17
  111.0 0.1 fusion.14
  111.1 11.2 %all_to_all.23 = bf16[8,8,672]{2,1,0:T(8,128)(2,1)S(1)} all-to-all(bf16[8,8,672]{2,1,0:T(8,128)(2,1)S(1)} %fusion.14), channel_id=1, replica_groups=mesh['z'=8,'y'=4,'x'=4,'c'=2] {'z'}, dimensions={0} | all-to-all | bytes 172032 | tf_op jit(solution)/shard_map/scatter_z/all_to_all | solution.py:53
  122.2 0.6 convert_reduce_fusion
  (5 shorter events, 0.1 us)
Async XLA Ops:
  19.6 6.7 %collective-permute-start.3 = (bf16[672,128]{1,0:T(8,128)(2,1)S(1)}, bf16[672,128]{1,0:T(8,128)(2,1)S(1)}, u32[]{:S(2)}, u32[]{:S(2)}) collective-permute-start(bf16[672,128]{1,0:T(8,128)(2,1)S(1)} %gather_z.1), channel_id=1, source_target_pairs={{0,8},{1,3},{2,10},{3,5},{4,12},{5,7},{6,14},{7,1},{8,16},{9,11},{... | collective-permute-start | bytes 516104 | tf_op jit(solution)/shard_map/gather_yx/ppermute | solution.py:33
  21.3 5.4 %collective-permute-start.1 = (bf16[672,128]{1,0:T(8,128)(2,1)S(1)}, bf16[672,128]{1,0:T(8,128)(2,1)S(1)}, u32[]{:S(2)}, u32[]{:S(2)}) collective-permute-start(bf16[672,128]{1,0:T(8,128)(2,1)S(1)} %gather_z.1), channel_id=1, source_target_pairs={{0,24},{1,7},{2,26},{3,1},{4,28},{5,3},{6,30},{7,5},{8,0},{9,15},{... | collective-permute-start | bytes 516104 | tf_op jit(solution)/shard_map/gather_yx/ppermute | solution.py:33
  22.9 6.9 %collective-permute-start = (bf16[672,128]{1,0:T(8,128)(2,1)S(1)}, bf16[672,128]{1,0:T(8,128)(2,1)S(1)}, u32[]{:S(2)}, u32[]{:S(2)}) collective-permute-start(bf16[672,128]{1,0:T(8,128)(2,1)S(1)} %gather_z.1), channel_id=1, source_target_pairs={{0,16},{1,5},{2,18},{3,7},{4,20},{5,1},{6,22},{7,3},{8,24},{9,13},... | collective-permute-start | bytes 516104 | tf_op jit(solution)/shard_map/gather_yx/ppermute | solution.py:33
  29.9 19.6 %collective-permute-start.6 = (bf16[4,672,128]{2,1,0:T(8,128)(2,1)S(1)}, bf16[4,672,128]{2,1,0:T(8,128)(2,1)S(1)}, u32[]{:S(2)}, u32[]{:S(2)}) collective-permute-start(bf16[4,672,128]{2,1,0:T(8,128)(2,1)S(1)} %pad_maximum_fusion._.refs_4_), channel_id=1, source_target_pairs={{0,6},{1,25},{2,0},{3,27},{4,2},{5,29},{6,4},{7,31},{8,14},{9,1},{... | collective-permute-start | bytes 2064392 | tf_op jit(solution)/shard_map/gather_xy/ppermute | solution.py:33
  30.8 18.7 %collective-permute-start.5 = (bf16[4,672,128]{2,1,0:T(8,128)(2,1)S(1)}, bf16[4,672,128]{2,1,0:T(8,128)(2,1)S(1)}, u32[]{:S(2)}, u32[]{:S(2)}) collective-permute-start(bf16[4,672,128]{2,1,0:T(8,128)(2,1)S(1)} %pad_maximum_fusion._.refs_4_), channel_id=1, source_target_pairs={{0,2},{1,9},{2,4},{3,11},{4,6},{5,13},{6,0},{7,15},{8,10},{9,17},{... | collective-permute-start | bytes 2064392 | tf_op jit(solution)/shard_map/gather_xy/ppermute | solution.py:33
  33.3 16.8 %collective-permute-start.4 = (bf16[2,672,128]{2,1,0:T(8,128)(2,1)S(1)}, bf16[2,672,128]{2,1,0:T(8,128)(2,1)S(1)}, u32[]{:S(2)}, u32[]{:S(2)}) collective-permute-start(bf16[2,672,128]{2,1,0:T(8,128)(2,1)S(1)} %pad_maximum_fusion.2), channel_id=1, source_target_pairs={{0,4},{1,17},{2,6},{3,19},{4,0},{5,21},{6,2},{7,23},{8,12},{9,25},... | collective-permute-start | bytes 1032200 | tf_op jit(solution)/shard_map/gather_xy/ppermute | solution.py:33
  33.6 16.5 %collective-permute-start.2 = (bf16[2,672,128]{2,1,0:T(8,128)(2,1)S(1)}, bf16[2,672,128]{2,1,0:T(8,128)(2,1)S(1)}, u32[]{:S(2)}, u32[]{:S(2)}) collective-permute-start(bf16[2,672,128]{2,1,0:T(8,128)(2,1)S(1)} %pad_maximum_fusion.1), channel_id=1, source_target_pairs={{0,4},{1,17},{2,6},{3,19},{4,0},{5,21},{6,2},{7,23},{8,12},{9,25},... | collective-permute-start | bytes 1032200 | tf_op jit(solution)/shard_map/gather_xy/ppermute | solution.py:33
  41.2 12.5 %collective-permute-start.11 = (bf16[4,672,128]{2,1,0:T(8,128)(2,1)S(1)}, bf16[4,672,128]{2,1,0:T(8,128)(2,1)S(1)}, u32[]{:S(2)}, u32[]{:S(2)}) collective-permute-start(bf16[4,672,128]{2,1,0:T(8,128)(2,1)S(1)} %pad_maximum_fusion._.refs_4_), channel_id=1, source_target_pairs={{0,1},{1,0},{2,3},{3,2},{4,5},{5,4},{6,7},{7,6},{8,9},{9,8},{10,11... | collective-permute-start | bytes 2064392 | tf_op jit(solution)/shard_map/gather_xy/ppermute | solution.py:33
  49.5 4.1 %collective-permute-start.10 = (bf16[4,672,128]{2,1,0:T(8,128)(2,1)S(1)}, bf16[4,672,128]{2,1,0:T(8,128)(2,1)S(1)}, u32[]{:S(2)}, u32[]{:S(2)}) collective-permute-start(bf16[4,672,128]{2,1,0:T(8,128)(2,1)S(1)} %collective-permute-done.6.refs_3_), channel_id=1, source_target_pairs={{0,1},{1,0},{2,3},{3,2},{4,5},{5,4},{6,7},{7,6},{8,9},{9,8},{10,11... | collective-permute-start | bytes 2064392 | tf_op jit(solution)/shard_map/gather_xy/ppermute | solution.py:33
  49.5 4.1 %collective-permute-start.9 = (bf16[4,672,128]{2,1,0:T(8,128)(2,1)S(1)}, bf16[4,672,128]{2,1,0:T(8,128)(2,1)S(1)}, u32[]{:S(2)}, u32[]{:S(2)}) collective-permute-start(bf16[4,672,128]{2,1,0:T(8,128)(2,1)S(1)} %collective-permute-done.5.refs_2_), channel_id=1, source_target_pairs={{0,1},{1,0},{2,3},{3,2},{4,5},{5,4},{6,7},{7,6},{8,9},{9,8},{10,11... | collective-permute-start | bytes 2064392 | tf_op jit(solution)/shard_map/gather_xy/ppermute | solution.py:33
  50.1 3.1 %collective-permute-start.8 = (bf16[2,672,128]{2,1,0:T(8,128)(2,1)S(1)}, bf16[2,672,128]{2,1,0:T(8,128)(2,1)S(1)}, u32[]{:S(2)}, u32[]{:S(2)}) collective-permute-start(bf16[2,672,128]{2,1,0:T(8,128)(2,1)S(1)} %collective-permute-done.4.refs_1_), channel_id=1, source_target_pairs={{0,1},{1,0},{2,3},{3,2},{4,5},{5,4},{6,7},{7,6},{8,9},{9,8},{10,11... | collective-permute-start | bytes 1032200 | tf_op jit(solution)/shard_map/gather_xy/ppermute | solution.py:33
  50.1 3.5 %collective-permute-start.7 = (bf16[2,672,128]{2,1,0:T(8,128)(2,1)S(1)}, bf16[2,672,128]{2,1,0:T(8,128)(2,1)S(1)}, u32[]{:S(2)}, u32[]{:S(2)}) collective-permute-start(bf16[2,672,128]{2,1,0:T(8,128)(2,1)S(1)} %collective-permute-done.2.refs_0_), channel_id=1, source_target_pairs={{0,1},{1,0},{2,3},{3,2},{4,5},{5,4},{6,7},{7,6},{8,9},{9,8},{10,11... | collective-permute-start | bytes 1032200 | tf_op jit(solution)/shard_map/gather_xy/ppermute | solution.py:33
  86.1 3.5 %collective-permute-start.12 = (bf16[4,4,64,672]{3,2,1,0:T(8,128)(2,1)S(1)}, bf16[4,4,64,672]{3,2,1,0:T(8,128)(2,1)S(1)}, u32[]{:S(2)}, u32[]{:S(2)}) collective-permute-start(bf16[4,4,64,672]{3,2,1,0:T(8,128)(2,1)S(1)} %get-tuple-element.20), channel_id=1, source_target_pairs={{0,1},{1,0},{2,3},{3,2},{4,5},{5,4},{6,7},{7,6},{8,9},{9,8},{10,11... | collective-permute-start | bytes 4128776 | tf_op jit(solution)/shard_map/product/ppermute | solution.py:33
  89.9 9.5 %collective-permute-start.13 = (bf16[4,64,672]{2,1,0:T(8,128)(2,1)S(1)}, bf16[4,64,672]{2,1,0:T(8,128)(2,1)S(1)}, u32[]{:S(2)}, u32[]{:S(2)}) collective-permute-start(bf16[4,64,672]{2,1,0:T(8,128)(2,1)S(1)} %get-tuple-element.23), channel_id=1, source_target_pairs={{0,4},{1,17},{2,6},{3,19},{4,0},{5,21},{6,2},{7,23},{8,12},{9,25},... | collective-permute-start | bytes 1032200 | tf_op jit(solution)/shard_map/scatter_xy/ppermute | solution.py:33
  92.0 10.9 %collective-permute-start.15 = (bf16[4,64,672]{2,1,0:T(8,128)(2,1)S(1)}, bf16[4,64,672]{2,1,0:T(8,128)(2,1)S(1)}, u32[]{:S(2)}, u32[]{:S(2)}) collective-permute-start(bf16[4,64,672]{2,1,0:T(8,128)(2,1)S(1)} %get-tuple-element.24), channel_id=1, source_target_pairs={{0,2},{1,9},{2,4},{3,11},{4,6},{5,13},{6,0},{7,15},{8,10},{9,17},{... | collective-permute-start | bytes 1032200 | tf_op jit(solution)/shard_map/scatter_xy/ppermute | solution.py:33
  93.3 10.1 %collective-permute-start.14 = (bf16[4,64,672]{2,1,0:T(8,128)(2,1)S(1)}, bf16[4,64,672]{2,1,0:T(8,128)(2,1)S(1)}, u32[]{:S(2)}, u32[]{:S(2)}) collective-permute-start(bf16[4,64,672]{2,1,0:T(8,128)(2,1)S(1)} %get-tuple-element.25), channel_id=1, source_target_pairs={{0,6},{1,25},{2,0},{3,27},{4,2},{5,29},{6,4},{7,31},{8,14},{9,1},{... | collective-permute-start | bytes 1032200 | tf_op jit(solution)/shard_map/scatter_xy/ppermute | solution.py:33
  103.7 6.2 %collective-permute-start.16 = (bf16[64,672]{1,0:T(8,128)(2,1)S(1)}, bf16[64,672]{1,0:T(8,128)(2,1)S(1)}, u32[]{:S(2)}, u32[]{:S(2)}) collective-permute-start(bf16[64,672]{1,0:T(8,128)(2,1)S(1)} %get-tuple-element.26), channel_id=1, source_target_pairs={{0,16},{1,5},{2,18},{3,7},{4,20},{5,1},{6,22},{7,3},{8,24},{9,13},... | collective-permute-start | bytes 258056 | tf_op jit(solution)/shard_map/scatter_yx/ppermute | solution.py:33
  105.0 6.0 %collective-permute-start.18 = (bf16[64,672]{1,0:T(8,128)(2,1)S(1)}, bf16[64,672]{1,0:T(8,128)(2,1)S(1)}, u32[]{:S(2)}, u32[]{:S(2)}) collective-permute-start(bf16[64,672]{1,0:T(8,128)(2,1)S(1)} %get-tuple-element.27), channel_id=1, source_target_pairs={{0,8},{1,3},{2,10},{3,5},{4,12},{5,7},{6,14},{7,1},{8,16},{9,11},{... | collective-permute-start | bytes 258056 | tf_op jit(solution)/shard_map/scatter_yx/ppermute | solution.py:33
  105.9 5.1 %collective-permute-start.17 = (bf16[64,672]{1,0:T(8,128)(2,1)S(1)}, bf16[64,672]{1,0:T(8,128)(2,1)S(1)}, u32[]{:S(2)}, u32[]{:S(2)}) collective-permute-start(bf16[64,672]{1,0:T(8,128)(2,1)S(1)} %get-tuple-element.28), channel_id=1, source_target_pairs={{0,24},{1,7},{2,26},{3,1},{4,28},{5,3},{6,30},{7,5},{8,0},{9,15},{... | collective-permute-start | bytes 258056 | tf_op jit(solution)/shard_map/scatter_yx/ppermute | solution.py:33
